TPU v7x, 32 devices: a whole 2x2x4 slice. The times are simulated.
32 devices in a mesh: dp: 8 (over z, x), seq: 4 (over y, core).
Axes of the slice: x: 2, y: 2, z: 4, core: 2. Of those that a mesh axis runs over, the one named last changes fastest.
Arguments:
- hidden_in: bfloat16 [64, 512, 768], P('dp', 'seq'), may hold values from -6 to 6
- segment_ids: int32 [64, 512], P('dp'), may hold values from 0 to 512, as said below
- row_lengths: int32 [64], P('dp'), may hold values from 256 to 512
- teacher_scores: bfloat16 [64, 12, 512, 512], P('dp', None, 'seq'), may hold values from -8 to 8
- teacher_hidden: bfloat16 [64, 512, 768], P('dp', 'seq'), may hold values from -6 to 6
- w_query: float32 [768, 768], P(None, 'dp'), may hold values from -0.625 to 0.625
- w_key: float32 [768, 768], P(None, 'dp'), may hold values from -0.625 to 0.625
- w_value: float32 [768, 768], P(None, 'dp'), may hold values from -0.21875 to 0.21875
- w_out: float32 [768, 768], P(None, 'dp'), may hold values from -0.875 to 0.875
- w_up: float32 [768, 3072], P(None, 'dp'), may hold values from -0.21875 to 0.21875
- w_down: float32 [3072, 768], P(None, 'dp'), may hold values from -0.109375 to 0.109375
- b_query: bfloat16 [768], P('dp'), may hold values from -2 to 2
- b_value: bfloat16 [768], P('dp'), may hold values from -2 to 2
- b_out: bfloat16 [768], P('dp'), may hold values from -2 to 2
- b_up: bfloat16 [3072], P('dp'), may hold values from -2 to 2
- b_down: bfloat16 [768], P('dp'), may hold values from -2 to 2
- norm1_gain: bfloat16 [768], P('dp'), may hold values from 0.5 to 1.5
- norm1_bias: bfloat16 [768], P('dp'), may hold values from -2 to 2
- norm2_gain: bfloat16 [768], P('dp'), may hold values from 0.5 to 1.5
- norm2_bias: bfloat16 [768], P('dp'), may hold values from -2 to 2
- clip_in: bfloat16 [768], P('dp'), may hold values from 1 to 3
- clip_ctx: bfloat16 [768], P('dp'), may hold values from 0.5 to 2
- clip_mid: bfloat16 [768], P('dp'), may hold values from 1 to 3
- clip_hid: bfloat16 [3072], P('dp'), may hold values from 0.5 to 2
Outputs:
- output: bfloat16 [64, 512, 768], P('dp', 'seq')
- loss: float32 [], replicated
- grad_input: float32 [64, 512, 768], P('dp', 'seq')
- grad_w_query: float32 [768, 768], P(None, 'dp')
- grad_w_key: float32 [768, 768], P(None, 'dp')
- grad_w_value: float32 [768, 768], P(None, 'dp')
- grad_w_out: float32 [768, 768], P(None, 'dp')
- grad_w_up: float32 [768, 3072], P(None, 'dp')
- grad_w_down: float32 [3072, 768], P(None, 'dp')
- grad_b_query: float32 [768], P('dp')
- grad_b_value: float32 [768], P('dp')
- grad_b_out: float32 [768], P('dp')
- grad_b_up: float32 [3072], P('dp')
- grad_b_down: float32 [768], P('dp')
- grad_norm1_gain: float32 [768], P('dp')
- grad_norm1_bias: float32 [768], P('dp')
- grad_norm2_gain: float32 [768], P('dp')
- grad_norm2_bias: float32 [768], P('dp')
- grad_clip_in: float32 [768], P('dp')
- grad_clip_ctx: float32 [768], P('dp')
- grad_clip_mid: float32 [768], P('dp')
- grad_clip_hid: float32 [3072], P('dp')
Inputs may be any that keep to these rules, and one draw needn't show every extreme that they name: `segment_ids`: within each row, document numbers start at 0 and never fall; positions at or after the row's length hold 512.
All inputs are finite; a program needn't handle non-finite values.
Results may differ from a plain program's by a relative error of at most 0.012.
Values may be sent and summed in bfloat16 or wider, within the bound.
A program may use at most 256 MiB of HBM per device.

v0:
```python
import jax
import jax.numpy as jnp
from jax import lax
from jax.sharding import PartitionSpec as P

MICRO = 2


eps_norm = 1e-05
score_weight = 0.0625
negative = -1e30


def as_sent(value):

    def short(part):
        return part.astype(jnp.bfloat16) if part.dtype == jnp.float32 else part

    return jax.tree.map(short, value)


def soft_clip(value, bound):
    return bound * jnp.tanh(value / bound)


def layer_norm(value, gain, shift):
    centre = value - jnp.mean(value, axis=-1, keepdims=True)
    return (
        centre * lax.rsqrt(jnp.mean(centre * centre, axis=-1, keepdims=True) + eps_norm) * gain
        + shift
    )


def gelu_clip(pre, bound):
    return soft_clip(jax.nn.gelu(pre, approximate=False), bound)


def binarize(latent):
    scale = jnp.mean(jnp.abs(latent), axis=0)
    return (scale * jnp.sign(latent)).astype(jnp.bfloat16)


def latent_grad(latent, grad_binary):
    signs = jnp.sign(latent)
    return signs * (jnp.sum(grad_binary * signs, axis=0) / latent.shape[0])


def product(left, right):
    return jnp.dot(left, right, preferred_element_type=jnp.float32)


def transposed_left(left, right):
    return lax.dot_general(
        left, right, (((0,), (0,)), ((), ())), preferred_element_type=jnp.float32
    )


def transposed_right(left, right):
    return lax.dot_general(
        left, right, (((1,), (1,)), ((), ())), preferred_element_type=jnp.float32
    )


def unpack(full):
    vectors = full[6].astype(jnp.float32)
    hidden_vectors = full[7].astype(jnp.float32)
    return (full[:6], [vectors[i] for i in range(11)], hidden_vectors[0], hidden_vectors[1])


def body(
    hidden_in,
    segment_ids,
    row_lengths,
    teacher_scores,
    teacher_hidden,
    w_query,
    w_key,
    w_value,
    w_out,
    w_up,
    w_down,
    b_query,
    b_value,
    b_out,
    b_up,
    b_down,
    norm1_gain,
    norm1_bias,
    norm2_gain,
    norm2_bias,
    clip_in,
    clip_ctx,
    clip_mid,
    clip_hid,
):
    latents = (w_query, w_key, w_value, w_out, w_up, w_down)
    small_model = jnp.stack(
        [
            b_query,
            b_value,
            b_out,
            b_down,
            norm1_gain,
            norm1_bias,
            norm2_gain,
            norm2_bias,
            clip_in,
            clip_ctx,
            clip_mid,
        ]
    )
    small_hidden = jnp.stack([b_up, clip_hid])
    shards = tuple((binarize(w) for w in latents)) + (small_model, small_hidden)
    rows, block, width = hidden_in.shape
    heads = teacher_scores.shape[1]
    head_dim = width // heads
    seq_len = segment_ids.shape[1]
    rows_micro = rows // MICRO
    scale = head_dim ** (-0.5)
    first = lax.axis_index("seq") * block

    def row_view(start_row):
        segments = segment_ids[start_row : start_row + rows_micro]
        lengths = row_lengths[start_row : start_row + rows_micro]
        query_segments = lax.dynamic_slice_in_dim(segments, first, block, 1)
        query_live = (first + jnp.arange(block, dtype=jnp.int32))[None, :] < lengths[:, None]
        targets = teacher_scores[start_row : start_row + rows_micro]
        return (segments, lengths, query_segments, query_live, targets)

    finals = []
    input_grads = []
    shard_sums = None
    objective_sum = jnp.zeros((), jnp.float32)
    for index in range(MICRO):
        start_row = index * rows_micro
        full = jax.tree.map(
            lambda part, own: part.astype(own.dtype),
            lax.all_gather(as_sent(shards), "dp", axis=1, tiled=True),
            shards,
        )
        matrices, vectors, up_bias, hidden_bound = unpack(full)
        bin_query, bin_key, bin_value, bin_out, bin_up, bin_down = matrices
        (
            bias_query,
            bias_value,
            bias_out,
            bias_down,
            gain_one,
            shift_one,
            gain_two,
            shift_two,
            bound_in,
            bound_ctx,
            bound_mid,
        ) = vectors
        (
            forward_segments,
            forward_lengths,
            forward_query_segments,
            forward_query_live,
            forward_targets,
        ) = row_view(start_row)
        inputs = (
            hidden_in[start_row : start_row + rows_micro].astype(jnp.float32).reshape(-1, width)
        )
        inputs_low = soft_clip(inputs, bound_in).astype(jnp.bfloat16)
        query = (product(inputs_low, bin_query) + bias_query).astype(jnp.bfloat16)
        keys = product(inputs_low, bin_key).astype(jnp.bfloat16).reshape(rows_micro, block, width)
        values = (
            (product(inputs_low, bin_value) + bias_value)
            .astype(jnp.bfloat16)
            .reshape(rows_micro, block, width)
        )
        query_heads = query.reshape(rows_micro, block, heads, head_dim)
        top = jnp.full((rows_micro, heads, block), negative, jnp.float32)
        key_piece = lax.all_gather(keys, "seq", axis=1, tiled=True)
        value_piece = lax.all_gather(values, "seq", axis=1, tiled=True)
        count = key_piece.shape[1]
        key_heads = key_piece.reshape(rows_micro, count, heads, head_dim)
        value_heads = value_piece.reshape(rows_micro, count, heads, head_dim)
        scores = (
            jnp.einsum(
                "rqhd,rkhd->rhqk", query_heads, key_heads, preferred_element_type=jnp.float32
            )
            * scale
        )
        key_live = jnp.arange(count, dtype=jnp.int32)[None, :] < forward_lengths[:, None]
        same = (forward_query_segments[:, :, None] == forward_segments[:, None, :])[:, None]
        counted = same & forward_query_live[:, None, :, None] & key_live[:, None, None, :]
        teacher = forward_targets.astype(jnp.float32)
        distill = jnp.sum(jnp.where(counted, (scores - teacher) ** 2, 0.0))
        new_top = jnp.maximum(top, jnp.max(jnp.where(same, scores, negative), axis=-1))
        expo = jnp.exp(jnp.where(same, scores - new_top[..., None], negative))
        total = jnp.sum(expo, axis=-1)
        accum = jnp.einsum(
            "rhqk,rkhd->rqhd",
            expo.astype(jnp.bfloat16),
            value_heads,
            preferred_element_type=jnp.float32,
        )
        top, total, accum, distill = (new_top, total, accum, distill)
        context = (accum / jnp.transpose(total, (0, 2, 1))[..., None]).reshape(-1, width)
        context_low = soft_clip(context, bound_ctx).astype(jnp.bfloat16)
        first_sum = inputs + product(context_low, bin_out) + bias_out
        normed = layer_norm(first_sum, gain_one, shift_one)
        normed_low = soft_clip(normed, bound_mid).astype(jnp.bfloat16)
        up_pre = product(normed_low, bin_up) + up_bias
        hidden_low = gelu_clip(up_pre, hidden_bound).astype(jnp.bfloat16)
        second_sum = normed + product(hidden_low, bin_down) + bias_down
        final = layer_norm(second_sum, gain_two, shift_two)
        teacher_out = (
            teacher_hidden[start_row : start_row + rows_micro]
            .astype(jnp.float32)
            .reshape(-1, width)
        )
        errors = jnp.where(forward_query_live.reshape(-1)[:, None], final - teacher_out, 0.0)
        objective = 0.5 * jnp.sum(errors * errors) + 0.5 * score_weight * distill
        saved = (
            inputs,
            inputs_low,
            query,
            keys,
            values,
            top,
            total,
            context,
            context_low,
            first_sum,
            normed,
            normed_low,
            up_pre,
            hidden_low,
            second_sum,
            errors,
        )
        final, objective, saved = (final, objective, saved)
        objective_sum = objective_sum + objective
        finals.append(final.reshape(rows_micro, block, width))
        full = jax.tree.map(
            lambda part, own: part.astype(own.dtype),
            lax.all_gather(as_sent(shards), "dp", axis=1, tiled=True),
            shards,
        )
        backward_matrices, backward_vectors, backward_up_bias, backward_hidden_bound = unpack(full)
        (
            backward_bin_query,
            backward_bin_key,
            backward_bin_value,
            backward_bin_out,
            backward_bin_up,
            backward_bin_down,
        ) = backward_matrices
        (
            backward_bias_query,
            backward_bias_value,
            backward_bias_out,
            backward_bias_down,
            backward_gain_one,
            backward_shift_one,
            backward_gain_two,
            backward_shift_two,
            backward_bound_in,
            backward_bound_ctx,
            backward_bound_mid,
        ) = backward_vectors
        (
            backward_inputs,
            backward_inputs_low,
            backward_query,
            backward_keys,
            backward_values,
            backward_top,
            backward_total,
            backward_context,
            backward_context_low,
            backward_first_sum,
            backward_normed,
            backward_normed_low,
            backward_up_pre,
            backward_hidden_low,
            backward_second_sum,
            backward_errors,
        ) = saved
        (
            backward_segments,
            backward_lengths,
            backward_query_segments,
            backward_query_live,
            backward_targets,
        ) = row_view(start_row)
        unused, pull = jax.vjp(
            layer_norm, backward_second_sum, backward_gain_two, backward_shift_two
        )
        grad_second, grad_gain_two, grad_shift_two = pull(backward_errors)
        branch_grad = grad_second.astype(jnp.bfloat16)
        grad_bias_down = jnp.sum(branch_grad.astype(jnp.float32), axis=0)
        grad_bin_down = transposed_left(backward_hidden_low, branch_grad)
        unused, pull = jax.vjp(gelu_clip, backward_up_pre, backward_hidden_bound)
        up_grad, grad_hidden_bound = pull(transposed_right(branch_grad, backward_bin_down))
        up_grad = up_grad.astype(jnp.bfloat16)
        grad_up_bias = jnp.sum(up_grad.astype(jnp.float32), axis=0)
        grad_bin_up = transposed_left(backward_normed_low, up_grad)
        unused, pull = jax.vjp(soft_clip, backward_normed, backward_bound_mid)
        grad_normed_clip, grad_bound_mid = pull(transposed_right(up_grad, backward_bin_up))
        unused, pull = jax.vjp(
            layer_norm, backward_first_sum, backward_gain_one, backward_shift_one
        )
        grad_first, grad_gain_one, grad_shift_one = pull(grad_second + grad_normed_clip)
        out_grad = grad_first.astype(jnp.bfloat16)
        grad_bias_out = jnp.sum(out_grad.astype(jnp.float32), axis=0)
        grad_bin_out = transposed_left(backward_context_low, out_grad)
        unused, pull = jax.vjp(soft_clip, backward_context, backward_bound_ctx)
        grad_context, grad_bound_ctx = pull(transposed_right(out_grad, backward_bin_out))
        context_heads = backward_context.reshape(rows_micro, block, heads, head_dim)
        grad_heads = grad_context.reshape(rows_micro, block, heads, head_dim)
        total_rows = jnp.transpose(backward_total, (0, 2, 1))
        accum_grad = (grad_heads / total_rows[..., None]).astype(jnp.bfloat16)
        delta = jnp.transpose(jnp.sum(grad_heads * context_heads, axis=-1), (0, 2, 1))
        keys_all = lax.all_gather(backward_keys, "seq", axis=1, tiled=True)
        values_all = lax.all_gather(backward_values, "seq", axis=1, tiled=True)
        backward_key_heads = keys_all.reshape(rows_micro, seq_len, heads, head_dim)
        backward_value_heads = values_all.reshape(rows_micro, seq_len, heads, head_dim)
        backward_query_heads = backward_query.reshape(rows_micro, block, heads, head_dim)
        backward_scores = (
            jnp.einsum(
                "rqhd,rkhd->rhqk",
                backward_query_heads,
                backward_key_heads,
                preferred_element_type=jnp.float32,
            )
            * scale
        )
        backward_key_live = (
            jnp.arange(seq_len, dtype=jnp.int32)[None, :] < backward_lengths[:, None]
        )
        backward_same = (backward_query_segments[:, :, None] == backward_segments[:, None, :])[
            :, None
        ]
        backward_counted = (
            backward_same
            & backward_query_live[:, None, :, None]
            & backward_key_live[:, None, None, :]
        )
        backward_expo = jnp.exp(
            jnp.where(backward_same, backward_scores - backward_top[..., None], negative)
        )
        prob_grad = jnp.einsum(
            "rqhd,rkhd->rhqk", accum_grad, backward_value_heads, preferred_element_type=jnp.float32
        )
        score_grad = backward_expo * (
            prob_grad - (delta / backward_total)[..., None]
        ) + score_weight * jnp.where(
            backward_counted, backward_scores - backward_targets.astype(jnp.float32), 0.0
        )
        score_grad = score_grad.astype(jnp.bfloat16)
        query_grad = (
            (
                jnp.einsum(
                    "rhqk,rkhd->rqhd",
                    score_grad,
                    backward_key_heads,
                    preferred_element_type=jnp.float32,
                )
                * scale
            )
            .astype(jnp.bfloat16)
            .reshape(-1, width)
        )
        key_terms = (
            jnp.einsum(
                "rhqk,rqhd->rkhd",
                score_grad,
                backward_query_heads,
                preferred_element_type=jnp.float32,
            )
            * scale
        ).reshape(rows_micro, seq_len, width)
        value_terms = jnp.einsum(
            "rhqk,rqhd->rkhd",
            backward_expo.astype(jnp.bfloat16),
            accum_grad,
            preferred_element_type=jnp.float32,
        ).reshape(rows_micro, seq_len, width)
        key_sum = lax.psum_scatter(
            key_terms.astype(jnp.bfloat16), "seq", scatter_dimension=1, tiled=True
        ).astype(jnp.float32)
        value_sum = lax.psum_scatter(
            value_terms.astype(jnp.bfloat16), "seq", scatter_dimension=1, tiled=True
        ).astype(jnp.float32)
        key_grad = key_sum.reshape(-1, width).astype(jnp.bfloat16)
        value_grad = value_sum.reshape(-1, width).astype(jnp.bfloat16)
        grad_bias_query = jnp.sum(query_grad.astype(jnp.float32), axis=0)
        grad_bias_value = jnp.sum(value_grad.astype(jnp.float32), axis=0)
        grad_bin_query = transposed_left(backward_inputs_low, query_grad)
        grad_bin_key = transposed_left(backward_inputs_low, key_grad)
        grad_bin_value = transposed_left(backward_inputs_low, value_grad)
        grad_inputs_low = (
            transposed_right(query_grad, backward_bin_query)
            + transposed_right(key_grad, backward_bin_key)
            + transposed_right(value_grad, backward_bin_value)
        )
        unused, pull = jax.vjp(soft_clip, backward_inputs, backward_bound_in)
        grad_inputs_clip, grad_bound_in = pull(grad_inputs_low)
        grad_inputs = grad_first + grad_inputs_clip
        small_grads = jnp.stack(
            [
                grad_bias_query,
                grad_bias_value,
                grad_bias_out,
                grad_bias_down,
                grad_gain_one,
                grad_shift_one,
                grad_gain_two,
                grad_shift_two,
                grad_bound_in,
                grad_bound_ctx,
                grad_bound_mid,
            ]
        )
        hidden_grads = jnp.stack([grad_up_bias, grad_hidden_bound])
        weight_grads = (
            grad_bin_query,
            grad_bin_key,
            grad_bin_value,
            grad_bin_out,
            grad_bin_up,
            grad_bin_down,
            small_grads,
            hidden_grads,
        )
        grad_inputs, weight_grads = (grad_inputs, weight_grads)
        input_grads.append(grad_inputs.reshape(rows_micro, block, width))
        reduced = (
            lax.psum_scatter(weight_grads[0], "dp", scatter_dimension=1, tiled=True),
            lax.psum_scatter(weight_grads[1], "dp", scatter_dimension=1, tiled=True),
            lax.psum_scatter(weight_grads[2], "dp", scatter_dimension=1, tiled=True),
            lax.psum_scatter(weight_grads[3], "dp", scatter_dimension=1, tiled=True),
            lax.psum_scatter(weight_grads[4], "dp", scatter_dimension=1, tiled=True),
            lax.psum_scatter(weight_grads[5], "dp", scatter_dimension=1, tiled=True),
            lax.psum_scatter(weight_grads[6], "dp", scatter_dimension=1, tiled=True),
            lax.psum_scatter(weight_grads[7], "dp", scatter_dimension=1, tiled=True),
        )
        shard_sums = reduced if shard_sums is None else jax.tree.map(jnp.add, shard_sums, reduced)
    shard_sums = jax.tree.map(
        lambda part: part.astype(jnp.float32), lax.psum(as_sent(shard_sums), "seq")
    )
    objective_all = lax.psum(objective_sum, ("dp", "seq"))
    loss = objective_all / (lax.axis_size("dp") * rows * seq_len)
    output = jnp.concatenate(finals, axis=0).astype(jnp.bfloat16)
    grad_input = jnp.concatenate(input_grads, axis=0)
    grad_query, grad_key, grad_value, grad_out, grad_up, grad_down, small_sum, hidden_sum = (
        shard_sums
    )
    latent_grads = (
        latent_grad(w_query, grad_query),
        latent_grad(w_key, grad_key),
        latent_grad(w_value, grad_value),
        latent_grad(w_out, grad_out),
        latent_grad(w_up, grad_up),
        latent_grad(w_down, grad_down),
    )
    return (
        (output, loss, grad_input)
        + latent_grads
        + (
            small_sum[0],
            small_sum[1],
            small_sum[2],
            hidden_sum[0],
            small_sum[3],
            small_sum[4],
            small_sum[5],
            small_sum[6],
            small_sum[7],
            small_sum[8],
            small_sum[9],
            small_sum[10],
            hidden_sum[1],
        )
    )


def solution(mesh):
    placed = (
        P("dp", "seq", None),
        P("dp", None),
        P("dp"),
        P("dp", None, "seq", None),
        P("dp", "seq", None),
        P(None, "dp"),
        P(None, "dp"),
        P(None, "dp"),
        P(None, "dp"),
        P(None, "dp"),
        P(None, "dp"),
        P("dp"),
        P("dp"),
        P("dp"),
        P("dp"),
        P("dp"),
        P("dp"),
        P("dp"),
        P("dp"),
        P("dp"),
        P("dp"),
        P("dp"),
        P("dp"),
        P("dp"),
    )
    return jax.shard_map(
        body,
        mesh=mesh,
        in_specs=placed,
        out_specs=(
            P("dp", "seq", None),
            P(),
            P("dp", "seq", None),
            P(None, "dp"),
            P(None, "dp"),
            P(None, "dp"),
            P(None, "dp"),
            P(None, "dp"),
            P(None, "dp"),
            P("dp"),
            P("dp"),
            P("dp"),
            P("dp"),
            P("dp"),
            P("dp"),
            P("dp"),
            P("dp"),
            P("dp"),
            P("dp"),
            P("dp"),
            P("dp"),
            P("dp"),
        ),
        check_vma=False,
    )
```

profile of v0, /device:TPU:0, one launch (start us, length us, event | category | flops | bytes accessed | tf_op | source)
XLA Modules:
  0.0 1533.3 jit_solution(6779331613123017517)
XLA Ops:
  14.4 32.4 %all-gather = bf16[8,96,11]{1,2,0:T(8,128)(2,1)S(1)} all-gather(bf16[1,96,11]{1,2,0:T(8,128)(2,1)S(1)} %bitcast.327), channel_id=1, replica_groups=mesh['dp'=8,'seq'=4] {'dp'}, dimensions={0}, use_global_device_ids=true | all-gather | bytes 19008 | tf_op jit(solution)/shard_map/all_gather | solution.py:138
  48.2 6.6 all-gather.18.cloned.1.call-done
  59.7 37.7 %all-gather.12.cloned.1.call-done = bf16[768,768]{0,1:T(8,128)(2,1)} async-done(((bf16[768,96]{0,1:T(8,128)(2,1)}), bf16[768,768]{0,1:T(8,128)(2,1)}) %all-gather.12.cloned.1.call-update) | async-done | bytes 1179664 | tf_op jit(solution)/shard_map/all_gather | solution.py:138
  107.8 26.1 %all_gather.31 = bf16[2,3072]{1,0:T(2,128)(2,1)S(1)} all-gather(bf16[2,384]{1,0:T(2,128)(2,1)S(1)} %pad_maximum_fusion.2), channel_id=1, replica_groups=mesh['dp'=8,'seq'=4] {'dp'}, dimensions={1}, use_global_device_ids=true | all-gather | bytes 13824 | tf_op jit(solution)/shard_map/all_gather | solution.py:138
  146.4 21.7 %all-gather.20.cloned.1.call-done = bf16[4,512,768]{2,1,0:T(8,128)(2,1)} async-done(((bf16[4,128,768]{2,1,0:T(8,128)(2,1)}), bf16[4,512,768]{2,1,0:T(8,128)(2,1)}) %all-gather.20.cloned.1.call-update) | async-done | bytes 3145744 | tf_op jit(solution)/shard_map/all_gather | solution.py:176
  171.6 9.4 select_reduce_fusion.3
  181.0 17.7 %all-gather.30.cloned.1.call-done = bf16[4,512,768]{2,1,0:T(8,128)(2,1)} async-done(((bf16[4,128,768]{2,1,0:T(8,128)(2,1)}), bf16[4,512,768]{2,1,0:T(8,128)(2,1)}) %all-gather.30.cloned.1.call-update) | async-done | bytes 3145744 | tf_op jit(solution)/shard_map/all_gather | solution.py:176
  202.0 4.5 select_reduce_fusion.2
  206.5 5.0 copy-done
  211.5 16.5 %select_reduce_fusion = (f32[]{:T(128)}, f32[]{:T(128)}, f32[4,12,128]{2,1,0:T(8,128)S(1)}, f32[4,12,128]{2,1,0:T(8,128)S(1)}) fusion(f32[4,12,128,512]{3,2,1,0:T(8,128)S(1)} %get-tuple-element.173, pred[4,128,512]{2,1,0:T(8,128)(4,1)S(1)} %copy-done.71, bf16[8,12,128,512]{3,2,1,0:T(8,128)(2,1)} %param.27, f32[4,12,128,512]{3,2,1,0:T(8,128)} %get-tuple-element.171, ...), kind=kLoop, calls=%fused_computation.2 | loop fusion | flops 56610816 | bytes 38895624 | tf_op jit(solution)/shard_map/reduce_sum | solution.py:191
  232.5 8.2 bitcast_divide_fusion
  242.6 30.0 %all-gather.22.cloned.1.call-done = bf16[768,768]{0,1:T(8,128)(2,1)} async-done(((bf16[768,96]{0,1:T(8,128)(2,1)}), bf16[768,768]{0,1:T(8,128)(2,1)}) %all-gather.22.cloned.1.call-update) | async-done | bytes 1179664 | tf_op jit(solution)/shard_map/all_gather | solution.py:138
  275.3 26.1 %all-gather.14.cloned.1.call-done = bf16[4,512,768]{2,1,0:T(8,128)(2,1)} async-done(((bf16[4,128,768]{2,1,0:T(8,128)(2,1)}), bf16[4,512,768]{2,1,0:T(8,128)(2,1)}) %all-gather.14.cloned.1.call-update) | async-done | bytes 3145744 | tf_op jit(solution)/shard_map/all_gather | solution.py:177
  301.5 4.6 copy.124
  306.1 8.1 bitcast_divide_fusion.2
  320.4 64.2 %all-gather.24.cloned.1.call-done = bf16[768,3072]{1,0:T(8,128)(2,1)} async-done(((bf16[768,384]{1,0:T(8,128)(2,1)}), bf16[768,3072]{1,0:T(8,128)(2,1)}) %all-gather.24.cloned.1.call-update) | async-done | bytes 4718608 | tf_op jit(solution)/shard_map/all_gather | solution.py:138
  384.6 4.9 fusion.55
  392.3 33.7 %fusion.4 = (f32[512,3072]{1,0:T(8,128)}, f32[512,3072]{1,0:T(8,128)}, f32[512,3072]{1,0:T(8,128)}) fusion(f32[3072]{0:T(1024)S(1)} %bitcast.331, f32[512,3072]{1,0:T(8,128)S(1)} %fusion.55, bf16[768,3072]{1,0:T(8,128)(2,1)S(1)} %copy-done.180, f32[768]{0:T(1024)S(1)} %get-tuple-element.68, f32[768]{0:T(1024)S(1)} %get-tuple-element.69, ...), kind=kOutput, calls=%fused_computation.16 | convolution fusion | flops 2616852480 | bytes 31482880 | tf_op jit(solution)/shard_map/dot_general | solution.py:49
  426.0 38.7 %all-gather.26.cloned.1.call-done = bf16[3072,768]{0,1:T(8,128)(2,1)} async-done(((bf16[3072,96]{0,1:T(8,128)(2,1)}), bf16[3072,768]{0,1:T(8,128)(2,1)}) %all-gather.26.cloned.1.call-update) | async-done | bytes 4718608 | tf_op jit(solution)/shard_map/all_gather | solution.py:138
  464.7 9.4 fusion.85
  474.5 5.9 fusion.86
  492.2 18.6 %multiply_reduce_fusion = (f32[3072]{0:T(1024)}, f32[3072]{0:T(1024)}, f32[3072]{0:T(1024)}, f32[3072]{0:T(1024)}, f32[3072]{0:T(1024)}, /*index=5*/bf16[512,307...) fusion(f32[3072]{0:T(1024)S(1)} %bitcast.330, f32[512,3072]{1,0:T(8,128)} %get-tuple-element.143, ...), kind=kOutput, calls=%fused_computation.18 | convolution fusion | flops 2510272512 | bytes 43364352 | tf_op jit(solution)/shard_map/dot_general | solution.py:59
  510.8 6.2 fusion.90
  517.1 7.9 multiply_reduce_fusion.17
  539.6 11.8 add_convert_fusion.1
  563.5 11.7 add_convert_fusion
  582.1 7.9 convolution_convert_fusion.1
  590.0 4.7 copy.142
  596.1 7.7 convolution_convert_fusion
  603.7 4.9 copy.149
  611.5 6.2 convert_reduce_fusion.9
  637.2 36.9 %reduce-scatter.19.cloned.1.call-done = bf16[4,128,768]{2,1,0:T(8,128)(2,1)} async-done(((bf16[4,512,768]{2,1,0:T(8,128)(2,1)}), bf16[4,128,768]{2,1,0:T(8,128)(2,1)}) %reduce-scatter.19.cloned.1.call-update) | async-done | bytes 786448 | tf_op jit(solution)/shard_map/reduce_scatter | solution.py:387
  676.0 38.6 %reduce-scatter.23.cloned.1.call-done = bf16[4,128,768]{2,1,0:T(8,128)(2,1)} async-done(((bf16[4,512,768]{2,1,0:T(8,128)(2,1)}), bf16[4,128,768]{2,1,0:T(8,128)(2,1)}) %reduce-scatter.23.cloned.1.call-update) | async-done | bytes 786448 | tf_op jit(solution)/shard_map/reduce_scatter | solution.py:387
  719.6 5.0 fusion.53
  724.6 5.8 convolution_add_fusion.1
  731.5 6.3 fusion.34
  737.9 11.7 convolution_add_fusion
  765.5 21.6 %reduce-scatter.25.cloned.1.call-done = f32[768,96]{0,1:T(8,128)} async-done(((f32[768,768]{0,1:T(8,128)}), f32[768,96]{0,1:T(8,128)}) %reduce-scatter.25.cloned.1.call-update) | async-done | bytes 294928 | tf_op jit(solution)/shard_map/reduce_scatter | solution.py:434
  788.7 69.8 %reduce-scatter.31.cloned.1.call-done = f32[768,96]{0,1:T(8,128)} async-done(((f32[768,768]{0,1:T(8,128)}), f32[768,96]{0,1:T(8,128)}) %reduce-scatter.31.cloned.1.call-update) | async-done | bytes 294928 | tf_op jit(solution)/shard_map/reduce_scatter | solution.py:437
  860.1 70.4 %reduce-scatter.27.cloned.1.call-done = f32[768,96]{0,1:T(8,128)} async-done(((f32[768,768]{0,1:T(8,128)}), f32[768,96]{0,1:T(8,128)}) %reduce-scatter.27.cloned.1.call-update) | async-done | bytes 294928 | tf_op jit(solution)/shard_map/reduce_scatter | solution.py:435
  932.1 69.7 %reduce-scatter.29.cloned.1.call-done = f32[768,96]{0,1:T(8,128)} async-done(((f32[768,768]{0,1:T(8,128)}), f32[768,96]{0,1:T(8,128)}) %reduce-scatter.29.cloned.1.call-update) | async-done | bytes 294928 | tf_op jit(solution)/shard_map/reduce_scatter | solution.py:436
  1003.5 164.3 %reduce-scatter.33.cloned.1.call-done = f32[768,384]{1,0:T(8,128)} async-done(((f32[768,3072]{1,0:T(8,128)}), f32[768,384]{1,0:T(8,128)}) %reduce-scatter.33.cloned.1.call-update) | async-done | bytes 1179664 | tf_op jit(solution)/shard_map/reduce_scatter | solution.py:438
  1169.9 163.9 %reduce-scatter.35.cloned.1.call-done = f32[3072,96]{0,1:T(8,128)} async-done(((f32[3072,768]{0,1:T(8,128)}), f32[3072,96]{0,1:T(8,128)}) %reduce-scatter.35.cloned.1.call-update) | async-done | bytes 1179664 | tf_op jit(solution)/shard_map/reduce_scatter | solution.py:439
  1338.6 40.1 %psum.63 = f32[]{:T(128)} all-reduce(f32[]{:T(128)S(6)} %add.376), channel_id=1, replica_groups=mesh['dp'=8,'seq'=4] {'dp','seq'}, use_global_device_ids=true, to_apply=%region_22.23 | all-reduce | flops 1 | bytes 8 | tf_op jit(solution)/shard_map/psum | solution.py:447
  1380.7 20.8 %reduce-scatter.39.cloned.1.call-done = f32[384,2]{1,0:T(8,128)} async-done(((f32[3072,2]{1,0:T(8,128)}), f32[384,2]{1,0:T(8,128)}) %reduce-scatter.39.cloned.1.call-update) | async-done | bytes 3088
  1405.9 59.5 %reduce-scatter.37.cloned.1.call-done = f32[96,11]{1,0:T(8,128)} async-done(((f32[768,11]{1,0:T(8,128)}), f32[96,11]{1,0:T(8,128)}) %reduce-scatter.37.cloned.1.call-update) | async-done | bytes 4240
  1466.3 5.8 all-reduce
  1473.2 41.8 %all-reduce.4.cloned.1.call-done = (bf16[768,96]{0,1:T(8,128)(2,1)}, bf16[768,96]{0,1:T(8,128)(2,1)}, bf16[768,96]{0,1:T(8,128)(2,1)}, bf16[768,96]{0,1:T(8,128)...) async-done(((bf16[768,96]{0,1:T(8,128)(2,1)}, bf16[768,96]{0,1:T(8,128)(2,1)}, bf16[768,96]{0,1:T(8,128)(2,1)}, bf16[768,96]{0,1:T(8,128)(2,1)}, ...) | async-done | bytes 1769488 | tf_op jit(solution)/shard_map/psum | solution.py:445
  (630 shorter events, 180.8 us)
Async XLA Ops:
  7.3 40.2 %copy-start.15 = (bf16[8,128,768]{2,1,0:T(8,128)(2,1)S(1)}, bf16[8,128,768]{2,1,0:T(8,128)(2,1)}, u32[]{:S(2)}) copy-start(bf16[8,128,768]{2,1,0:T(8,128)(2,1)} %param.24) | copy-start | bytes 4718596
  7.3 47.5 %all-gather.18.cloned.1.call-start = ((), (), s32[]{:S(2)}) async-start(), calls=%async_computation.15 | async-start | bytes 1327104 | tf_op jit(solution)/shard_map/all_gather | solution.py:138
  10.3 87.1 %all-gather.12.cloned.1.call-start = ((), (), s32[]{:S(2)}) async-start(), calls=%async_computation.12 | async-start | bytes 1327104 | tf_op jit(solution)/shard_map/all_gather | solution.py:138
  13.2 126.2 %all-gather.16.cloned.1.call-start = ((), (), s32[]{:S(2)}) async-start(), calls=%async_computation.14 | async-start | bytes 1327104 | tf_op jit(solution)/shard_map/all_gather | solution.py:138
  14.2 154.0 %all-gather.20.cloned.1.call-start = ((), (), s32[]{:S(2)}) async-start(), calls=%async_computation.16 | async-start | bytes 3932160 | tf_op jit(solution)/shard_map/all_gather | solution.py:176
  47.6 49.8 %copy-start.160 = (f32[768]{0:T(1024)}, f32[768]{0:T(1024)S(1)}, u32[]{:S(2)}) copy-start(f32[768]{0:T(1024)S(1)} %get-tuple-element.73) | copy-start | bytes 9220
  47.6 225.0 %copy-start.143 = (f32[768]{0:T(1024)}, f32[768]{0:T(1024)S(1)}, u32[]{:S(2)}) copy-start(f32[768]{0:T(1024)S(1)} %get-tuple-element.75) | copy-start | bytes 9220
  48.2 49.3 %copy-start.81 = (bf16[512,768]{1,0:T(8,128)(2,1)}, bf16[512,768]{1,0:T(8,128)(2,1)S(1)}, u32[]{:S(2)}) copy-start(bf16[512,768]{1,0:T(8,128)(2,1)S(1)} %get-tuple-element.129) | copy-start | bytes 2359300
  57.9 140.8 %all-gather.30.cloned.1.call-start = ((), (), s32[]{:S(2)}) async-start(), calls=%async_computation.21 | async-start | bytes 3932160 | tf_op jit(solution)/shard_map/all_gather | solution.py:176
  59.7 169.6 %all-gather.28.cloned.1.call-start = ((), (), s32[]{:S(2)}) async-start(), calls=%async_computation.20 | async-start | bytes 3932160 | tf_op jit(solution)/shard_map/all_gather | solution.py:177
  100.5 172.1 %all-gather.22.cloned.1.call-start = ((), (), s32[]{:S(2)}) async-start(), calls=%async_computation.17 | async-start | bytes 1327104 | tf_op jit(solution)/shard_map/all_gather | solution.py:138
  101.5 200.0 %all-gather.14.cloned.1.call-start = ((), (), s32[]{:S(2)}) async-start(), calls=%async_computation.13 | async-start | bytes 3932160 | tf_op jit(solution)/shard_map/all_gather | solution.py:177
  103.5 281.0 %all-gather.24.cloned.1.call-start = ((), (), s32[]{:S(2)}) async-start(), calls=%async_computation.18 | async-start | bytes 5308416 | tf_op jit(solution)/shard_map/all_gather | solution.py:138
  105.0 359.7 %all-gather.26.cloned.1.call-start = ((), (), s32[]{:S(2)}) async-start(), calls=%async_computation.19 | async-start | bytes 5308416 | tf_op jit(solution)/shard_map/all_gather | solution.py:138
  106.4 524.2 %reduce-scatter.17.cloned.1.call-start = ((), (), s32[]{:S(2)}) async-start(), calls=%async_computation.22 | async-start | bytes 3932160 | tf_op jit(solution)/shard_map/reduce_scatter | solution.py:384
  137.9 94.6 %copy-start.56 = (pred[4,128,512]{2,1,0:T(8,128)(4,1)}, pred[4,128,512]{2,1,0:T(8,128)(4,1)S(1)}, u32[]{:S(2)}) copy-start(pred[4,128,512]{2,1,0:T(8,128)(4,1)S(1)} %get-tuple-element.146) | copy-start | bytes 786436
  181.0 125.1 %copy-start.97 = (f32[4,12,128]{2,1,0:T(8,128)}, f32[4,12,128]{2,1,0:T(8,128)S(1)}, u32[]{:S(2)}) copy-start(f32[4,12,128]{2,1,0:T(8,128)S(1)} %broadcast_maximum_fusion.1) | copy-start | bytes 73732
  228.0 78.1 %copy-start.93 = (f32[4,12,128]{2,1,0:T(8,128)}, f32[4,12,128]{2,1,0:T(8,128)S(1)}, u32[]{:S(2)}) copy-start(f32[4,12,128]{2,1,0:T(8,128)S(1)} %get-tuple-element.28) | copy-start | bytes 73732
  242.1 30.5 %copy-start.154 = (f32[768]{0:T(1024)S(1)}, f32[768]{0:T(1024)}, u32[]{:S(2)}) copy-start(f32[768]{0:T(1024)} %get-tuple-element.71) | copy-start | bytes 9220
  242.5 32.4 %copy-start.63 = (f32[512,768]{1,0:T(8,128)}, f32[512,768]{1,0:T(8,128)S(1)}, u32[]{:S(2)}) copy-start(f32[512,768]{1,0:T(8,128)S(1)} %copy.135) | copy-start | bytes 4718596
  275.0 250.1 %copy-start.13 = (f32[512,768]{1,0:T(8,128)}, f32[512,768]{1,0:T(8,128)S(1)}, u32[]{:S(2)}) copy-start(f32[512,768]{1,0:T(8,128)S(1)} %get-tuple-element.175) | copy-start | bytes 4718596
  275.3 30.8 %copy-start.108 = (f32[512]{0:T(512)}, f32[512]{0:T(512)S(1)}, u32[]{:S(2)}) copy-start(f32[512]{0:T(512)S(1)} %multiply_reduce_fusion.27) | copy-start | bytes 6148
  275.3 249.7 %copy-start.104 = (f32[512]{0:T(512)}, f32[512]{0:T(512)S(1)}, u32[]{:S(2)}) copy-start(f32[512]{0:T(512)S(1)} %fusion.62) | copy-start | bytes 6148
  275.3 30.8 %copy-start.59 = (pred[4,128,512]{2,1,0:T(8,128)(4,1)S(1)}, pred[4,128,512]{2,1,0:T(8,128)(4,1)}, u32[]{:S(2)}) copy-start(pred[4,128,512]{2,1,0:T(8,128)(4,1)} %get-tuple-element.148) | copy-start | bytes 786436
  320.0 205.0 %copy-start.32 = (f32[512,768]{1,0:T(8,128)}, f32[512,768]{1,0:T(8,128)S(1)}, u32[]{:S(2)}) copy-start(f32[512,768]{1,0:T(8,128)S(1)} %get-tuple-element.177) | copy-start | bytes 4718596
  320.1 205.0 %copy-start.106 = (f32[512]{0:T(512)}, f32[512]{0:T(512)S(1)}, u32[]{:S(2)}) copy-start(f32[512]{0:T(512)S(1)} %broadcast_multiply_fusion.5) | copy-start | bytes 6148
  320.4 69.2 %copy-start.110 = (f32[512]{0:T(512)}, f32[512]{0:T(512)S(1)}, u32[]{:S(2)}) copy-start(f32[512]{0:T(512)S(1)} %multiply_reduce_fusion.29) | copy-start | bytes 6148
  320.4 204.7 %copy-start.136 = (f32[512]{0:T(512)}, f32[512]{0:T(512)S(1)}, u32[]{:S(2)}) copy-start(f32[512]{0:T(512)S(1)} %fusion.60) | copy-start | bytes 6148
  392.2 72.5 %copy-start.126 = (f32[1,3072]{1,0:T(1,128)S(1)}, f32[1,3072]{1,0:T(1,128)}, u32[]{:S(2)}) copy-start(f32[1,3072]{1,0:T(1,128)} %get-tuple-element.145) | copy-start | bytes 36868
  392.3 72.5 %copy-start.151 = (f32[768]{0:T(1024)S(1)}, f32[768]{0:T(1024)}, u32[]{:S(2)}) copy-start(f32[768]{0:T(1024)} %get-tuple-element.67) | copy-start | bytes 9220
  556.7 76.8 %reduce-scatter.21.cloned.1.call-start = ((), (), s32[]{:S(2)}) async-start(), calls=%async_computation.24 | async-start | bytes 3932160 | tf_op jit(solution)/shard_map/reduce_scatter | solution.py:384
  580.7 93.4 %reduce-scatter.19.cloned.1.call-start = ((), (), s32[]{:S(2)}) async-start(), calls=%async_computation.23 | async-start | bytes 3932160 | tf_op jit(solution)/shard_map/reduce_scatter | solution.py:387
  594.7 119.9 %reduce-scatter.23.cloned.1.call-start = ((), (), s32[]{:S(2)}) async-start(), calls=%async_computation.25 | async-start | bytes 3932160 | tf_op jit(solution)/shard_map/reduce_scatter | solution.py:387
  608.6 178.4 %reduce-scatter.25.cloned.1.call-start = ((), (), s32[]{:S(2)}) async-start(), calls=%async_computation.26 | async-start | bytes 2654208 | tf_op jit(solution)/shard_map/reduce_scatter | solution.py:434
  624.5 234.0 %reduce-scatter.31.cloned.1.call-start = ((), (), s32[]{:S(2)}) async-start(), calls=%async_computation.29 | async-start | bytes 2654208 | tf_op jit(solution)/shard_map/reduce_scatter | solution.py:437
  630.3 300.1 %reduce-scatter.27.cloned.1.call-start = ((), (), s32[]{:S(2)}) async-start(), calls=%async_computation.27 | async-start | bytes 2654208 | tf_op jit(solution)/shard_map/reduce_scatter | solution.py:435
  637.2 364.7 %reduce-scatter.29.cloned.1.call-start = ((), (), s32[]{:S(2)}) async-start(), calls=%async_computation.28 | async-start | bytes 2654208 | tf_op jit(solution)/shard_map/reduce_scatter | solution.py:436
  718.3 449.5 %reduce-scatter.33.cloned.1.call-start = ((), (), s32[]{:S(2)}) async-start(), calls=%async_computation.30 | async-start | bytes 10616832 | tf_op jit(solution)/shard_map/reduce_scatter | solution.py:438
  730.4 603.4 %reduce-scatter.35.cloned.1.call-start = ((), (), s32[]{:S(2)}) async-start(), calls=%async_computation.31 | async-start | bytes 10616832 | tf_op jit(solution)/shard_map/reduce_scatter | solution.py:439
  749.9 651.6 %reduce-scatter.39.cloned.1.call-start = ((), (), s32[]{:S(2)}) async-start(), calls=%async_computation.33 | async-start | bytes 1769472
  752.6 712.8 %reduce-scatter.37.cloned.1.call-start = ((), (), s32[]{:S(2)}) async-start(), calls=%async_computation.32 | async-start | bytes 442368
  765.4 749.6 %all-reduce.4.cloned.1.call-start = ((), (), s32[]{:S(2)}) async-start(), calls=%async_computation.34 | async-start | bytes 3538944 | tf_op jit(solution)/shard_map/psum | solution.py:445
  1169.9 209.4 %copy-start.50 = (bf16[512,768]{1,0:T(8,128)(2,1)S(1)}, bf16[512,768]{1,0:T(8,128)(2,1)}, u32[]{:S(2)}) copy-start(bf16[512,768]{1,0:T(8,128)(2,1)} %get-tuple-element.124) | copy-start | bytes 2359300
  1169.9 209.4 %copy-start.51 = (bf16[512,768]{1,0:T(8,128)(2,1)S(1)}, bf16[512,768]{1,0:T(8,128)(2,1)}, u32[]{:S(2)}) copy-start(bf16[512,768]{1,0:T(8,128)(2,1)} %get-tuple-element.161) | copy-start | bytes 2359300
  1402.5 112.6 %copy-start.39 = (f32[768,96]{0,1:T(8,128)S(1)}, f32[768,96]{0,1:T(8,128)}, u32[]{:S(2)}) copy-start(f32[768,96]{0,1:T(8,128)} %param.29) | copy-start | bytes 884740
  1402.5 114.5 %copy-start.40 = (f32[768,96]{0,1:T(8,128)S(1)}, f32[768,96]{0,1:T(8,128)}, u32[]{:S(2)}) copy-start(f32[768,96]{0,1:T(8,128)} %param.30) | copy-start | bytes 884740
  1405.9 113.2 %copy-start.41 = (f32[768,96]{0,1:T(8,128)S(1)}, f32[768,96]{0,1:T(8,128)}, u32[]{:S(2)}) copy-start(f32[768,96]{0,1:T(8,128)} %param.31) | copy-start | bytes 884740
  1472.0 48.1 %copy-start.43 = (f32[768,96]{0,1:T(8,128)S(1)}, f32[768,96]{0,1:T(8,128)}, u32[]{:S(2)}) copy-start(f32[768,96]{0,1:T(8,128)} %param.32) | copy-start | bytes 884740
  (168 other events, 601.5 us)
Sparse Core Ops, SparseCore 0:
  10.9 43.8 all-gather.17
  57.5 39.8 all-gather.11
  99.6 39.7 all-gather.15
  140.8 27.2 all-gather.19
  170.2 28.5 all-gather.29
  200.7 28.5 all-gather.27
  231.5 41.0 all-gather.21
  274.1 27.2 all-gather.13
  303.5 80.9 all-gather.23
  386.6 78.0 all-gather.25
  556.8 36.0 reduce-scatter.16
  595.5 37.9 reduce-scatter.20
  636.1 37.9 reduce-scatter.18
  676.6 37.9 reduce-scatter.22
  718.0 69.0 reduce-scatter.24
  790.4 68.0 reduce-scatter.30
  862.4 68.0 reduce-scatter.26
  933.8 67.9 reduce-scatter.28
  1005.4 162.3 reduce-scatter.32
  1171.2 162.5 reduce-scatter.34
  1337.2 64.2 reduce-scatter.38
  1405.1 60.2 reduce-scatter.36
  1469.0 45.9 all-reduce.3
where the time goes:
time: 1540 us; the launch traced here: 1530 us
  waiting for transfers between devices  1000 us (65%)
  matrix products  247 us (16%)
  blocking collectives  104 us (7%)
  local copies, waits for them, and re-layouts  85.5 us (6%)
  other arithmetic  71.3 us (5%)
  between operations  21.5 us (1%)
    all_gather x6, waiting for transfers between devices, body(): lax.all_gather(as_sent(shards), 'dp', axis=1, tiled=True)  178 us
    reduce_scatter x1, waiting for transfers between devices, body(): lax.psum_scatter(weight_grads[4], 'dp', scatter_dimension=1, tiled=True)  164 us
    reduce_scatter x1, waiting for transfers between devices, body(): lax.psum_scatter(weight_grads[5], 'dp', scatter_dimension=1, tiled=True)  164 us
    unnamed x25, waiting for transfers between devices  80.7 us
    reduce_scatter x2, waiting for transfers between devices, body(): lax.psum_scatter(value_terms.astype(jnp.bfloat16), 'seq', scatter_dimensi...  75.4 us
    dot_general x12, matrix products, product(): return jnp.dot(left, right, preferred_element_type=jnp.float32)  72.9 us
    reduce_scatter x1, waiting for transfers between devices, body(): lax.psum_scatter(weight_grads[1], 'dp', scatter_dimension=1, tiled=True)  70.4 us
    reduce_scatter x1, waiting for transfers between devices, body(): lax.psum_scatter(weight_grads[3], 'dp', scatter_dimension=1, tiled=True)  69.8 us
  transfers between devices with their start and end apart: 23, of which 22 were waited for; matrix products, arithmetic and copies ran while one was open for 18% of the time, Pallas kernels for 0%

commit v1 on v0

v1 whole, which is shorter than its diff:
```python
import jax
import jax.numpy as jnp
from jax import lax
from jax.sharding import PartitionSpec as P

EPS = 1e-05
SCORE_WEIGHT = 0.0625
NEGATIVE = -1e30
F32 = jnp.float32
BF16 = jnp.bfloat16


def dot_nt(left, right):
    return lax.dot_general(left, right, (((1,), (1,)), ((), ())), preferred_element_type=F32)


def dot_nn(left, right):
    return lax.dot_general(left, right, (((1,), (0,)), ((), ())), preferred_element_type=F32)


def columns(value):
    return jnp.sum(value, axis=0, keepdims=True)


def clip_parts(value, bound):
    ratio = value / bound
    bent = jnp.tanh(ratio)
    slope = 1.0 - bent * bent
    return bound * bent, slope, bent - ratio * slope


def norm_parts(value, gain, shift):
    centre = value - jnp.mean(value, axis=-1, keepdims=True)
    inverse = lax.rsqrt(jnp.mean(centre * centre, axis=-1, keepdims=True) + EPS)
    unit = centre * inverse
    return unit * gain + shift, unit, inverse


def norm_back(grad, unit, inverse, gain):
    scaled = grad * gain
    return inverse * (
        scaled
        - jnp.mean(scaled, axis=-1, keepdims=True)
        - unit * jnp.mean(scaled * unit, axis=-1, keepdims=True)
    )


def signs_and_scale(latent):
    scale = jnp.mean(jnp.abs(latent), axis=0).astype(BF16)
    return jnp.sign(latent).astype(BF16).T, scale


def body(
    hidden_in,
    segment_ids,
    row_lengths,
    teacher_scores,
    teacher_hidden,
    w_query,
    w_key,
    w_value,
    w_out,
    w_up,
    w_down,
    b_query,
    b_value,
    b_out,
    b_up,
    b_down,
    norm1_gain,
    norm1_bias,
    norm2_gain,
    norm2_bias,
    clip_in,
    clip_ctx,
    clip_mid,
    clip_hid,
):
    rows, block, width = hidden_in.shape
    heads = teacher_scores.shape[1]
    head_dim = width // heads
    seq_len = segment_ids.shape[1]
    tokens = rows * block
    scale = head_dim ** (-0.5)
    place = lax.axis_index("seq")
    first = place * block

    shards = [signs_and_scale(w) for w in (w_query, w_key, w_value, w_out, w_up, w_down)]
    small = jnp.stack(
        [shards[0][1], shards[1][1], shards[2][1], shards[3][1], shards[5][1], b_query, b_value,
         b_out, b_down, norm1_gain, norm1_bias, norm2_gain, norm2_bias, clip_in, clip_ctx, clip_mid]
    )
    wide = jnp.stack([shards[4][1], b_up, clip_hid])
    small = lax.all_gather(small, "dp", axis=1, tiled=True).astype(F32)
    wide = lax.all_gather(wide, "dp", axis=1, tiled=True).astype(F32)
    (a_q, a_k, a_v, a_o, a_d, bias_q, bias_v, bias_o, bias_d, g1, s1, g2, s2, c_in, c_ctx, c_mid) = [
        small[i : i + 1] for i in range(16)
    ]
    a_u, bias_u, c_hid = [wide[i : i + 1] for i in range(3)]
    sq, sk, sv, so, su, sd = [
        lax.all_gather(s[0], "dp", axis=0, tiled=True) for s in shards
    ]

    core_swap = [(0, 1), (1, 0), (2, 3), (3, 2)]
    chip_swap = [(0, 2), (2, 0), (1, 3), (3, 1)]
    across = lax.ppermute(hidden_in, "seq", chip_swap)
    beside = lax.ppermute(jnp.stack([hidden_in, across]), "seq", core_swap)
    full = jnp.stack([hidden_in, beside[0], across, beside[1]], axis=1)
    order = jnp.stack([place, place ^ 1, place ^ 2, place ^ 3])
    segments = segment_ids.reshape(rows, 4, block)[:, order].reshape(rows, seq_len)
    positions = (order[:, None] * block + jnp.arange(block)[None, :]).reshape(-1)

    inputs = hidden_in.astype(F32).reshape(tokens, width)
    low_all = clip_parts(full.astype(F32).reshape(-1, width), c_in)[0].astype(BF16)
    low_own = low_all.reshape(rows, 4, block, width)[:, 0].reshape(tokens, width)
    s_query = dot_nt(low_own, sq)
    query = a_q * s_query + bias_q
    query_low = (query * (a_k * scale)).astype(BF16).reshape(rows, block, heads, head_dim)
    s_key = dot_nt(low_all, sk).astype(BF16).reshape(rows, seq_len, heads, head_dim)
    s_value = dot_nt(low_all, sv).astype(BF16).reshape(rows, seq_len, heads, head_dim)

    scores = jnp.einsum("rqhd,rkhd->rhqk", query_low, s_key, preferred_element_type=F32)
    live = positions[None, :] < row_lengths[:, None]
    query_live = live[:, :block]
    same = (segments[:, :block, None] == segments[:, None, :])[:, None]
    counted = same & query_live[:, None, :, None] & live[:, None, None, :]
    targets = teacher_scores.reshape(rows, heads, block, 4, block)[:, :, :, order].reshape(
        rows, heads, block, seq_len
    )
    gap = jnp.where(counted, scores - targets.astype(F32), 0.0)
    distill = jnp.sum(gap * gap)
    top = jnp.max(jnp.where(same, scores, NEGATIVE), axis=-1, keepdims=True)
    expo = jnp.exp(jnp.where(same, scores - top, NEGATIVE))
    total = jnp.sum(expo, axis=-1)
    accum = jnp.einsum("rhqk,rkhd->rqhd", expo.astype(BF16), s_value, preferred_element_type=F32)
    total_rows = jnp.transpose(total, (0, 2, 1))[..., None]
    s_context = (accum / total_rows).reshape(tokens, width)

    context = a_v * s_context + bias_v
    context_low, ctx_slope, ctx_bound = clip_parts(context, c_ctx)
    s_out = dot_nt(context_low.astype(BF16), so)
    normed, unit1, inverse1 = norm_parts(inputs + a_o * s_out + bias_o, g1, s1)
    normed_low, mid_slope, mid_bound = clip_parts(normed, c_mid)
    s_up = dot_nt(normed_low.astype(BF16), su)
    pre = a_u * s_up + bias_u
    phi = 0.5 * (1.0 + lax.erf(pre * (0.5**0.5)))
    act = pre * phi
    act_slope = phi + pre * jnp.exp(-0.5 * pre * pre) * 0.3989422804014327
    hidden_low, hid_slope, hid_bound = clip_parts(act, c_hid)
    s_down = dot_nt(hidden_low.astype(BF16), sd)
    final, unit2, inverse2 = norm_parts(normed + a_d * s_down + bias_d, g2, s2)
    errors = jnp.where(
        query_live.reshape(tokens, 1),
        final - teacher_hidden.astype(F32).reshape(tokens, width),
        0.0,
    )
    objective = 0.5 * jnp.sum(errors * errors) + 0.5 * SCORE_WEIGHT * distill

    grad_second = norm_back(errors, unit2, inverse2, g2)
    grad_hid = dot_nn((grad_second * a_d).astype(BF16), sd)
    up_grad = grad_hid * hid_slope * act_slope
    grad_mid = dot_nn((up_grad * a_u).astype(BF16), su)
    grad_normed = grad_second + grad_mid * mid_slope
    grad_first = norm_back(grad_normed, unit1, inverse1, g1)
    grad_ctx_low = dot_nn((grad_first * a_o).astype(BF16), so)
    grad_ctx = grad_ctx_low * ctx_slope

    pulled = (grad_ctx * a_v).reshape(rows, block, heads, head_dim)
    accum_grad = (pulled / total_rows).astype(BF16)
    delta = jnp.sum(pulled * s_context.reshape(pulled.shape), axis=-1, keepdims=True) / total_rows
    delta = jnp.transpose(delta[..., 0], (0, 2, 1))[..., None]
    prob_grad = jnp.einsum("rqhd,rkhd->rhqk", accum_grad, s_value, preferred_element_type=F32)
    score_grad = (expo * (prob_grad - delta) + SCORE_WEIGHT * gap).astype(BF16)
    back = jnp.einsum("rhqk,rkhd->rqhd", score_grad, s_key, preferred_element_type=F32).reshape(
        tokens, width
    ) * scale
    query_grad = back * a_k
    key_grad = jnp.einsum("rhqk,rqhd->rkhd", score_grad, query_low, preferred_element_type=F32)
    value_grad = jnp.einsum(
        "rhqk,rqhd->rkhd", expo.astype(BF16), accum_grad, preferred_element_type=F32
    )
    pulled_in = dot_nn(key_grad.astype(BF16).reshape(-1, width), sk) + dot_nn(
        value_grad.astype(BF16).reshape(-1, width), sv
    )
    pulled_in = pulled_in.reshape(rows, 4, block, width)
    own_in = dot_nn((query_grad * a_q).astype(BF16), sq).reshape(rows, block, width)
    sent = lax.ppermute(
        jnp.stack([pulled_in[:, 1], pulled_in[:, 3]]).astype(BF16), "seq", core_swap
    ).astype(F32)
    crossed = lax.ppermute((pulled_in[:, 2] + sent[1]).astype(BF16), "seq", chip_swap).astype(F32)
    grad_low = (pulled_in[:, 0] + own_in + sent[0] + crossed).reshape(tokens, width)
    unused, in_slope, in_bound = clip_parts(inputs, c_in)
    grad_input = grad_first + grad_low * in_slope

    sums = jnp.concatenate(
        [
            columns(query_grad * s_query),
            columns(query * back),
            columns(grad_ctx * s_context),
            columns(grad_first * s_out),
            columns(grad_second * s_down),
            columns(query_grad),
            columns(grad_ctx),
            columns(grad_first),
            columns(grad_second),
            columns(grad_normed * unit1),
            columns(grad_normed),
            columns(errors * unit2),
            columns(errors),
            columns(grad_low * in_bound),
            columns(grad_ctx_low * ctx_bound),
            columns(grad_mid * mid_bound),
        ]
    )
    wide_sums = jnp.concatenate(
        [columns(up_grad * s_up), columns(up_grad), columns(grad_hid * hid_bound)]
    )
    sums, wide_sums, objective = lax.psum((sums, wide_sums, objective), ("dp", "seq"))
    at = lax.axis_index("dp")
    narrow, broad = w_query.shape[1], w_up.shape[1]
    sums = lax.dynamic_slice_in_dim(sums, at * narrow, narrow, 1)
    wide_sums = lax.dynamic_slice_in_dim(wide_sums, at * broad, broad, 1)
    loss = objective / (lax.axis_size("dp") * rows * seq_len)
    grads = [
        jnp.sign(w) * (s / w.shape[0])
        for w, s in zip(
            (w_query, w_key, w_value, w_out, w_up, w_down),
            (sums[0], sums[1], sums[2], sums[3], wide_sums[0], sums[4]),
        )
    ]
    return (
        final.reshape(rows, block, width).astype(BF16),
        loss,
        grad_input.reshape(rows, block, width),
        *grads,
        sums[5],
        sums[6],
        sums[7],
        wide_sums[1],
        sums[8],
        sums[9],
        sums[10],
        sums[11],
        sums[12],
        sums[13],
        sums[14],
        sums[15],
        wide_sums[2],
    )


def solution(mesh):
    rows = P("dp", "seq", None)
    cols = P(None, "dp")
    vec = P("dp")
    return jax.shard_map(
        body,
        mesh=mesh,
        in_specs=(rows, P("dp", None), vec, P("dp", None, "seq", None), rows)
        + (cols,) * 6
        + (vec,) * 13,
        out_specs=(rows, P(), rows) + (cols,) * 6 + (vec,) * 13,
        check_vma=False,
    )
```

time: 1540 us -> 666 us (0.43)
  waiting for transfers between devices: 1000 us -> 41.1 us
  local copies, waits for them, and re-layouts: 85.5 us -> 165 us
  other arithmetic: 71.3 us -> 100 us
  matrix products: 247 us -> 228 us
    reduce_scatter x10 -> x0, waiting for transfers between devices: 635 us -> none  [the longest x1 164 us: body(): lax.psum_scatter(weight_grads[4], 'dp', scatter_dimension=1, tiled=True)]
    all_gather x10 -> x6, waiting for transfers between devices: 244 us -> 0.03 us  [body(): lax.all_gather(s[0], 'dp', axis=0, tiled=True)]
    unnamed x25 -> x6, waiting for transfers between devices: 80.7 us -> 0.13 us
    gather x0 -> x17, local copies, waits for them, and re-layouts: none -> 43.5 us
    psum x1 -> x0, waiting for transfers between devices: 41.8 us -> none  [body(): lax.psum(as_sent(shard_sums), 'seq')]
    ppermute x0 -> x4, waiting for transfers between devices: none -> 40.9 us  [the longest x1 28.6 us: body(): across = lax.ppermute(hidden_in, 'seq', chip_swap)]
    unnamed x392 -> x149, local copies, waits for them, and re-layouts: 35.7 us -> 71.9 us
    sub x0 -> x1, other arithmetic: none -> 33 us  [body(): expo = jnp.exp(jnp.where(same, scores - top, NEGATIVE))]
  transfers between devices with their start and end apart: 23 -> 10, of which waited for: 22 -> 3; matrix products, arithmetic and copies ran while one was open for 18% -> 43% of each run, Pallas kernels for 0% -> 0%
where the time goes in v1:
time: 666 us; the launch traced here: 661 us
  matrix products  228 us (34%)
  local copies, waits for them, and re-layouts  165 us (25%)
  blocking collectives  103 us (15%)
  other arithmetic  100 us (15%)
  waiting for transfers between devices  41.1 us (6%)
  between operations  18.8 us (3%)
    unnamed x149, local copies, waits for them, and re-layouts  71.9 us
    dot_general x6, matrix products, dot_nn(): lax.dot_general(left, right, (((1,), (0,)), ((), ())), preferred_element_...  53.8 us
    dot_general x6, matrix products, dot_nt(): lax.dot_general(left, right, (((1,), (1,)), ((), ())), preferred_element_...  53.2 us
    gather x16, local copies, waits for them, and re-layouts  42.9 us
    psum x1, blocking collectives, body(): lax.psum((sums, wide_sums, objective), ('dp', 'seq'))  40.9 us
    sub x1, other arithmetic, body(): expo = jnp.exp(jnp.where(same, scores - top, NEGATIVE))  33 us
    all_gather x1, blocking collectives, body(): small = lax.all_gather(small, 'dp', axis=1, tiled=True).astype(F32)  31 us
    all_gather x1, blocking collectives, body(): wide = lax.all_gather(wide, 'dp', axis=1, tiled=True).astype(F32)  30.9 us
  transfers between devices with their start and end apart: 10, of which 3 were waited for; matrix products, arithmetic and copies ran while one was open for 43% of the time, Pallas kernels for 0%

profile of v1, /device:TPU:0, one launch (start us, length us, event | category | flops | bytes accessed | tf_op | source)
XLA Modules:
  0.0 660.9 jit_solution(8691089704843325387)
XLA Ops:
  25.1 28.6 %collective-permute-done = bf16[8,128,768]{2,1,0:T(8,128)(2,1)S(1)} collective-permute-done((bf16[8,128,768]{2,1,0:T(8,128)(2,1)S(1)}, bf16[8,128,768]{2,1,0:T(8,128)(2,1)S(1)}, u32[]{:S(2)}, u32[]{:S(2)}) %collective-permute-start) | collective-permute-done | bytes 1572896 | tf_op jit(solution)/shard_map/ppermute | solution.py:106
  56.2 31.0 %all-gather = bf16[8,96,16]{1,2,0:T(8,128)(2,1)S(1)} all-gather(bf16[1,96,16]{1,2,0:T(8,128)(2,1)S(1)} %bitcast.315), channel_id=1, replica_groups=mesh['dp'=8,'seq'=4] {'dp'}, dimensions={0}, use_global_device_ids=true | all-gather | bytes 27648 | tf_op jit(solution)/shard_map/all_gather | solution.py:94
  87.3 16.6 %copy.127 = bf16[8,12,128,512]{2,3,1,0:T(8,128)(2,1)} copy(bf16[8,12,128,512]{3,2,1,0:T(8,128)(2,1)} %param.27) | data formatting | bytes 25165824 | tf_op args[3]
  103.9 30.9 %all_gather.29 = bf16[3,3072]{1,0:T(4,128)(2,1)S(1)} all-gather(bf16[3,384]{1,0:T(4,128)(2,1)S(1)} %pad_maximum_fusion.3), channel_id=1, replica_groups=mesh['dp'=8,'seq'=4] {'dp'}, dimensions={1}, use_global_device_ids=true | all-gather | bytes 20736 | tf_op jit(solution)/shard_map/all_gather | solution.py:95
  136.1 43.0 %while.1 = (s32[]{:T(128)}, bf16[8,12,128,4,128]{2,4,3,1,0:T(8,128)(2,1)}, s32[4,1]{0,1:T(1,128)S(1)}, bf16[4,8,12,128,128]{4,3,2,1,0:T(8,128)(2,1)}, s32[]{:T(128)}) while((s32[]{:T(128)}, bf16[8,12,128,4,128]{2,4,3,1,0:T(8,128)(2,1)}, s32[4,1]{0,1:T(1,128)S(1)}, bf16[4,8,12,128,128]{4,3,2,1,0:T(8,128)(2,1)}, s32[]{:T(128)}) %tuple.113), condition=%wide.while_cond, body=%wide.while_body.sunk | while | flops 2 | bytes 18874956 | solution.py:127
  136.7 4.8 constant_dynamic-slice_fusion.5
  147.4 4.8 constant_dynamic-slice_fusion.5
  158.2 4.8 constant_dynamic-slice_fusion.5
  169.0 4.8 constant_dynamic-slice_fusion.5
  183.0 4.6 copy-done.2
  187.6 5.3 fusion.12
  192.9 9.3 %convolution_convert_fusion = bf16[4096,768]{1,0:T(8,128)(2,1)} fusion(bf16[4096,768]{1,0:T(8,128)(2,1)} %fusion.12, bf16[768,768]{1,0:T(8,128)(2,1)} %all-gather.12.cloned.1.call-done), kind=kOutput, calls=%fused_computation.33 | convolution fusion | flops 4834983936 | bytes 13762560 | tf_op jit(solution)/shard_map/dot_general | solution.py:14
  202.1 9.2 %convolution_convert_fusion.1 = bf16[4096,768]{1,0:T(8,128)(2,1)} fusion(bf16[4096,768]{1,0:T(8,128)(2,1)} %fusion.12, bf16[768,768]{1,0:T(8,128)(2,1)} %all-gather.8.cloned.1.call-done), kind=kOutput, calls=%fused_computation.34 | convolution fusion | flops 4834983936 | bytes 13762560 | tf_op jit(solution)/shard_map/dot_general | solution.py:14
  211.4 3.5 fusion.55
  214.9 4.8 multiply_convert_fusion.9
  223.3 9.5 %copy.121 = bf16[4096,768]{0,1:T(8,128)(2,1)} copy(bf16[4096,768]{1,0:T(8,128)(2,1)} %convolution_convert_fusion) | data formatting | bytes 12582912 | tf_op jit(solution)/shard_map/convert_element_type | solution.py:119
  232.8 9.7 %copy.150 = bf16[96,8,8,512]{3,2,1,0:T(8,128)(2,1)} copy(bf16[96,8,8,512]{3,1,2,0:T(8,128)(2,1)} %bitcast.284) | data formatting | bytes 12582912
  242.6 8.8 %copy.119 = bf16[4096,768]{0,1:T(8,128)(2,1)} copy(bf16[4096,768]{1,0:T(8,128)(2,1)} %convolution_convert_fusion.1) | data formatting | bytes 12582912 | tf_op jit(solution)/shard_map/convert_element_type | solution.py:120
  251.3 9.6 %copy.148 = bf16[96,8,8,512]{3,2,1,0:T(8,128)(2,1)} copy(bf16[96,8,8,512]{3,1,2,0:T(8,128)(2,1)} %bitcast.285) | data formatting | bytes 12582912
  261.0 18.3 %multiply_reduce_fusion = (f32[]{:T(128)}, f32[8,12,128,512]{3,2,1,0:T(8,128)}) fusion(pred[8,128,512]{2,1,0:T(8,128)(4,1)} %get-tuple-element.138, bf16[8,512,12,64]{1,0,3,2:T(8,128)(2,1)} %bitcast.279, bf16[8,128,12,64]{1,0,3,2:T(8,128)(2,1)S(1)} %bitcast.303, bf16[4,8,12,128,128]{4,3,2,1,0:T(8,128)(2,1)} %get-tuple-element.29), kind=kOutput, calls=%fused_computation.9 | convolution fusion | flops 836763648 | bytes 46137348 | tf_op jit(solution)/shard_map/rqhd,rkhd->rhqk/dot_general | solution.py:122
  279.3 33.0 %fusion.110 = (f32[8,12,128]{2,1,0:T(8,128)S(1)}, f32[8,12,128,512]{3,2,1,0:T(8,128)}) fusion(f32[8,12,128,512]{3,2,1,0:T(8,128)} %get-tuple-element.149, pred[8,128,512]{2,1,0:T(8,128)(4,1)} %get-tuple-element.139), kind=kOutput, calls=%fused_computation.246 | output fusion | flops 25166336 | bytes 50905088 | tf_op jit(solution)/shard_map/sub | solution.py:133
  312.3 28.5 %bitcast_divide_fusion.1 = f32[8,128,12,64]{1,3,2,0:T(8,128)} fusion(f32[8,12,128,512]{3,2,1,0:T(8,128)} %get-tuple-element.149, pred[8,128,512]{2,1,0:T(8,128)(4,1)} %get-tuple-element.139, bf16[8,512,12,64]{1,0,3,2:T(8,128)(2,1)} %bitcast.290, f32[8,128,12]{1,2,0:T(8,128)S(1)} %bitcast.309), kind=kOutput, calls=%fused_computation.73 | convolution fusion | flops 831271424 | bytes 35176448 | tf_op jit(solution)/shard_map/rhqk,rkhd->rqhd/dot_general | solution.py:135
  340.9 4.1 copy.125
  347.3 3.5 copy.126
  350.8 5.6 fusion.106
  358.7 11.3 %fusion.65 = f32[1024,3072]{1,0:T(8,128)} fusion(bf16[3072,768]{0,1:T(8,128)(2,1)} %all-gather.16.cloned.1.call-done, f32[768]{0:T(1024)S(1)} %get-tuple-element.66, f32[1024,768]{1,0:T(8,128)} %copy-done.8, f32[768]{0:T(1024)S(1)} %get-tuple-element.68, f32[768]{0:T(1024)S(1)} %get-tuple-element.69, f32[1024]{0:T(1024)S(1)} %add_rsqrt_fusion.1, ...), kind=kOutput, calls=%fused_computation.125 | convolution fusion | flops 4837343232 | bytes 20464640 | tf_op jit(solution)/shard_map/dot_general | solution.py:14
  370.0 13.0 %fusion.105 = (f32[1024]{0:T(1024)S(1)}, f32[1024,768]{1,0:T(8,128)S(1)}, f32[1024,768]{1,0:T(8,128)S(1)}) fusion(f32[768]{0:T(1024)S(1)} %copy-done.47, f32[768]{0:T(1024)S(1)} %copy-done.46, f32[768]{0:T(1024)S(1)} %get-tuple-element.68, f32[768]{0:T(1024)S(1)} %get-tuple-element.69, f32[1024]{0:T(1024)S(1)} %add_rsqrt_fusion.1, ...), kind=kOutput, calls=%fused_computation.242 | convolution fusion | flops 4866440192 | bytes 26800128 | tf_op jit(solution)/shard_map/dot_general | solution.py:14
  384.5 4.1 multiply_reduce_fusion.6
  391.1 16.7 %multiply_reduce_fusion.2 = (f32[3072]{0:T(1024)S(1)}, f32[3072]{0:T(1024)S(1)}, f32[3072]{0:T(1024)S(1)}, f32[1024,3072]{1,0:T(8,128)}) fusion(f32[1024,3072]{1,0:T(8,128)S(1)} %copy-done.65, f32[3072]{0:T(1024)S(1)} %bitcast.322, f32[3072]{0:T(1024)S(1)} %bitcast.320, f32[3072]{0:T(1024)S(1)} %bitcast.317, bf16[768,3072]{1,0:T(8,128)(2,1)S(1)} %bitcast.338, ...), kind=kOutput, calls=%fused_computation.24 | convolution fusion | flops 4905753600 | bytes 33106944 | tf_op jit(solution)/shard_map/dot_general | solution.py:18
  407.8 11.7 %multiply_reduce_fusion.7 = (f32[768]{0:T(1024)S(1)}, f32[1024]{0:T(1024)S(1)}, f32[768]{0:T(1024)S(1)}, f32[1024]{0:T(1024)S(1)}, f32[768]{0:T(1024)S(1)}, /*index=5*/f32[1024,768]{1,0:T(8,128)S(1)}) fusion(f32[1024,768]{1,0:T(8,128)S(1)} %copy-done.9, f32[1024]{0:T(1024)S(1)} %add_rsqrt_fusion.1, f32[1024]{0:T(1024)S(1)} %broadcast_multiply_fusion.6, ...), kind=kOutput, calls=%fused_computation.85 | convolution fusion | flops 4853853184 | bytes 26785792 | tf_op jit(solution)/shard_map/dot_general | solution.py:18
  429.2 26.2 %convert_bitcast_fusion.1 = bf16[8,512,12,64]{1,3,2,0:T(8,128)(2,1)} fusion(f32[8,12,128,512]{3,2,1,0:T(8,128)} %get-tuple-element.149, pred[8,128,512]{2,1,0:T(8,128)(4,1)} %get-tuple-element.139, f32[8,128,12,64]{1,0,3,2:T(8,128)S(1)} %bitcast.281, f32[8,128,12]{1,2,0:T(8,128)S(1)} %bitcast.310), kind=kOutput, calls=%fused_computation.38 | convolution fusion | flops 835203584 | bytes 35176448 | tf_op jit(solution)/shard_map/rhqk,rqhd->rkhd/dot_general | solution.py:179
  459.2 4.2 copy.136
  463.4 6.8 %copy.154 = bf16[96,8,8,512]{3,1,2,0:T(8,128)(2,1)} copy(bf16[96,8,8,512]{3,2,1,0:T(8,128)(2,1)S(1)} %bitcast.286) | data formatting | bytes 12582912
  470.2 29.5 %add_convert_fusion = bf16[8,12,128,512]{3,2,1,0:T(8,128)(2,1)} fusion(f32[8,12,128,512]{3,2,1,0:T(8,128)} %get-tuple-element.145, f32[8,12,128]{2,1,0:T(8,128)S(1)} %bitcast_divide_fusion.3, f32[8,12,128,512]{3,2,1,0:T(8,128)} %get-tuple-element.149, pred[8,128,512]{2,1,0:T(8,128)(4,1)} %get-tuple-element.138, bf16[8,512,12,64]{1,0,3,2:T(8,128)(2,1)} %bitcast.291, ...), kind=kOutput, calls=%fused_computation.8 | convolution fusion | flops 857210880 | bytes 85557248 | tf_op jit(solution)/shard_map/rqhd,rkhd->rhqk/dot_general | solution.py:172
  499.7 6.9 %convert_bitcast_fusion.2 = bf16[8,512,12,64]{1,3,2,0:T(8,128)(2,1)S(1)} fusion(bf16[8,12,128,512]{3,2,1,0:T(8,128)(2,1)} %add_convert_fusion, bf16[8,128,12,64]{1,0,3,2:T(8,128)(2,1)} %bitcast.304), kind=kOutput, calls=%fused_computation.39 | convolution fusion | flops 808452096 | bytes 20447232 | tf_op jit(solution)/shard_map/rhqk,rqhd->rkhd/dot_general | solution.py:178
  506.6 4.2 copy.135
  510.8 6.9 %copy.153 = bf16[96,8,8,512]{3,1,2,0:T(8,128)(2,1)} copy(bf16[96,8,8,512]{3,2,1,0:T(8,128)(2,1)S(1)} %bitcast.287) | data formatting | bytes 12582912
  517.7 11.0 %fusion.111 = f32[4096,768]{1,0:T(8,128)} fusion(bf16[4096,768]{0,1:T(8,128)(2,1)} %bitcast.300, bf16[768,768]{1,0:T(8,128)(2,1)S(1)} %copy-done.62), kind=kOutput, calls=%fused_computation.247 | convolution fusion | flops 4831838208 | bytes 20054016 | tf_op jit(solution)/shard_map/dot_general | solution.py:18
  528.7 8.6 %convolution_add_fusion = f32[4096,768]{1,0:T(8,128)S(1)} fusion(f32[4096,768]{1,0:T(8,128)} %fusion.111, bf16[4096,768]{0,1:T(8,128)(2,1)S(1)} %bitcast.299, bf16[768,768]{1,0:T(8,128)(2,1)S(1)} %copy-done.63), kind=kOutput, calls=%fused_computation.46 | convolution fusion | flops 4834983936 | bytes 32636928 | tf_op jit(solution)/shard_map/dot_general | solution.py:18
  537.7 4.2 copy-done.3
  543.3 4.7 collective-permute-done.2
  550.6 5.6 fusion.42
  557.9 11.3 %multiply_reduce_fusion.8 = (f32[12,64]{1,0:T(8,128)S(1)}, f32[8,12,64,128]{3,2,1,0:T(8,128)S(1)}) fusion(f32[12,64]{1,0:T(8,128)S(1)} %mul.564, bf16[8,12,128,512]{3,2,1,0:T(8,128)(2,1)} %add_convert_fusion, bf16[8,512,12,64]{1,0,3,2:T(8,128)(2,1)} %bitcast.280), kind=kOutput, calls=%fused_computation.86 | convolution fusion | flops 806878464 | bytes 22026240 | tf_op jit(solution)/shard_map/rhqk,rkhd->rqhd/dot_general | solution.py:174
  577.2 3.8 multiply_reduce_fusion.12
  585.4 7.6 %collective-permute-done.3 = bf16[8,128,768]{2,1,0:T(8,128)(2,1)} collective-permute-done((bf16[8,128,768]{2,1,0:T(8,128)(2,1)}, bf16[8,128,768]{2,1,0:T(8,128)(2,1)}, u32[]{:S(2)}, u32[]{:S(2)}) %collective-permute-start.3) | collective-permute-done | bytes 1572896 | tf_op jit(solution)/shard_map/ppermute | solution.py:190
  593.0 5.3 multiply_reduce_fusion.5
  598.4 5.3 fusion.49
  603.7 40.9 %all-reduce.2 = (f32[]{:T(128)}, f32[16,768]{1,0:T(8,128)S(1)}, f32[3,3072]{1,0:T(4,128)S(1)}) all-reduce(f32[]{:T(128)S(6)} %add.199, f32[16,768]{1,0:T(8,128)S(1)} %concatenate.29, f32[3,3072]{1,0:T(4,128)S(1)} %pad_maximum_fusion.2), channel_id=1, replica_groups=mesh['dp'=8,'seq'=4] {'dp','seq'}, use_global_device_ids=true, to_apply=%region_14.15 | all-reduce | flops 21505 | bytes 172040 | tf_op jit(solution)/shard_map/psum | solution.py:218
  (264 shorter events, 98.8 us)
Async XLA Ops:
  7.2 15.0 %copy-start = (s32[8,512]{1,0:T(8,128)S(1)}, s32[8,512]{1,0:T(8,128)}, u32[]{:S(2)}) copy-start(s32[8,512]{1,0:T(8,128)} %param.25) | copy-start | bytes 49156
  7.2 7.9 %copy-start.16 = (f32[768,384]{1,0:T(8,128)S(1)}, f32[768,384]{1,0:T(8,128)}, u32[]{:S(2)}) copy-start(f32[768,384]{1,0:T(8,128)} %param.33) | copy-start | bytes 3538948
  7.2 9.1 %copy-start.4 = (bf16[8,128,768]{2,1,0:T(8,128)(2,1)S(1)}, bf16[8,128,768]{2,1,0:T(8,128)(2,1)}, u32[]{:S(2)}) copy-start(bf16[8,128,768]{2,1,0:T(8,128)(2,1)} %param.24) | copy-start | bytes 4718596
  7.2 185.6 %all-gather.12.cloned.1.call-start = ((), (), s32[]{:S(2)}) async-start(), calls=%async_computation.2 | async-start | bytes 1327104 | tf_op jit(solution)/shard_map/all_gather | solution.py:101
  9.3 192.9 %all-gather.8.cloned.1.call-start = ((), (), s32[]{:S(2)}) async-start(), calls=%async_computation | async-start | bytes 1327104 | tf_op jit(solution)/shard_map/all_gather | solution.py:101
  11.2 11.6 %copy-start.48 = (bf16[384]{0:T(512)(128)(2,1)S(1)}, bf16[384]{0:T(512)(128)(2,1)}, u32[]{:S(2)}) copy-start(bf16[384]{0:T(512)(128)(2,1)} %param.38) | copy-start | bytes 2308
  11.2 11.6 %copy-start.49 = (bf16[384]{0:T(512)(128)(2,1)S(1)}, bf16[384]{0:T(512)(128)(2,1)}, u32[]{:S(2)}) copy-start(bf16[384]{0:T(512)(128)(2,1)} %param.47) | copy-start | bytes 2308
  11.2 11.8 %copy-start.61 = (s32[8]{0:T(128)S(1)}, s32[8]{0:T(128)}, u32[]{:S(2)}) copy-start(s32[8]{0:T(128)} %param.26) | copy-start | bytes 100
  11.2 203.7 %all-gather.10.cloned.1.call-start = ((), (), s32[]{:S(2)}) async-start(), calls=%async_computation.1 | async-start | bytes 1327104 | tf_op jit(solution)/shard_map/all_gather | solution.py:101
  13.1 337.7 %all-gather.14.cloned.1.call-start = ((), (), s32[]{:S(2)}) async-start(), calls=%async_computation.3 | async-start | bytes 1327104 | tf_op jit(solution)/shard_map/all_gather | solution.py:101
  15.0 343.6 %all-gather.16.cloned.1.call-start = ((), (), s32[]{:S(2)}) async-start(), calls=%async_computation.4 | async-start | bytes 5308416 | tf_op jit(solution)/shard_map/all_gather | solution.py:101
  16.3 353.7 %all-gather.18.cloned.1.call-start = ((), (), s32[]{:S(2)}) async-start(), calls=%async_computation.5 | async-start | bytes 5308416 | tf_op jit(solution)/shard_map/all_gather | solution.py:101
  16.3 37.4 %collective-permute-start = (bf16[8,128,768]{2,1,0:T(8,128)(2,1)S(1)}, bf16[8,128,768]{2,1,0:T(8,128)(2,1)S(1)}, u32[]{:S(2)}, u32[]{:S(2)}) collective-permute-start(bf16[8,128,768]{2,1,0:T(8,128)(2,1)S(1)} %copy-done.4), channel_id=1, source_target_pairs={{0,2},{2,0},{1,3},{3,1},{4,6},{6,4},{5,7},{7,5},{8,10},{10,8},{9,1... | collective-permute-start | bytes 4718600 | tf_op jit(solution)/shard_map/ppermute | solution.py:106
  56.0 123.1 %collective-permute-start.1 = (bf16[2,8,128,768]{3,2,1,0:T(8,128)(2,1)}, bf16[2,8,128,768]{3,2,1,0:T(8,128)(2,1)}, u32[]{:S(2)}, u32[]{:S(2)}) collective-permute-start(bf16[2,8,128,768]{3,2,1,0:T(8,128)(2,1)} %pad_maximum_fusion), channel_id=1, source_target_pairs={{0,1},{1,0},{2,3},{3,2},{4,5},{5,4},{6,7},{7,6},{8,9},{9,8},{10,11... | collective-permute-start | bytes 9437192 | tf_op jit(solution)/shard_map/ppermute | solution.py:107
  135.5 75.9 %copy-start.28 = (f32[768]{0:T(1024)}, f32[768]{0:T(1024)S(1)}, u32[]{:S(2)}) copy-start(f32[768]{0:T(1024)S(1)} %get-tuple-element.75) | copy-start | bytes 9220
  135.5 79.5 %copy-start.30 = (f32[768]{0:T(1024)}, f32[768]{0:T(1024)S(1)}, u32[]{:S(2)}) copy-start(f32[768]{0:T(1024)S(1)} %get-tuple-element.72) | copy-start | bytes 9220
  135.5 79.5 %copy-start.33 = (f32[768]{0:T(1024)}, f32[768]{0:T(1024)S(1)}, u32[]{:S(2)}) copy-start(f32[768]{0:T(1024)S(1)} %get-tuple-element.74) | copy-start | bytes 9220
  135.5 79.5 %copy-start.40 = (f32[768]{0:T(1024)}, f32[768]{0:T(1024)S(1)}, u32[]{:S(2)}) copy-start(f32[768]{0:T(1024)S(1)} %get-tuple-element.73) | copy-start | bytes 9220
  183.0 4.6 copy-start.2
  223.3 37.7 %copy-start.14 = (bf16[96,8,8,128]{3,2,1,0:T(8,128)(2,1)}, bf16[96,8,8,128]{3,2,1,0:T(8,128)(2,1)S(1)}, u32[]{:S(2)}) copy-start(bf16[96,8,8,128]{3,2,1,0:T(8,128)(2,1)S(1)} %copy.149) | copy-start | bytes 4718596
  312.3 28.6 %copy-start.26 = (f32[8,12,128]{2,1,0:T(8,128)}, f32[8,12,128]{2,1,0:T(8,128)S(1)}, u32[]{:S(2)}) copy-start(f32[8,12,128]{2,1,0:T(8,128)S(1)} %get-tuple-element.144) | copy-start | bytes 147460
  358.6 11.4 %copy-start.9 = (f32[1024,768]{1,0:T(8,128)S(1)}, f32[1024,768]{1,0:T(8,128)}, u32[]{:S(2)}) copy-start(f32[1024,768]{1,0:T(8,128)} %copy-done.8) | copy-start | bytes 9437188
  358.6 11.4 %copy-start.42 = (f32[1,3072]{1,0:T(1,128)S(1)}, f32[1,3072]{1,0:T(1,128)}, u32[]{:S(2)}) copy-start(f32[1,3072]{1,0:T(1,128)} %get-tuple-element.135) | copy-start | bytes 36868
  358.6 11.4 %copy-start.43 = (f32[1,3072]{1,0:T(1,128)S(1)}, f32[1,3072]{1,0:T(1,128)}, u32[]{:S(2)}) copy-start(f32[1,3072]{1,0:T(1,128)} %get-tuple-element.136) | copy-start | bytes 36868
  358.6 11.4 %copy-start.44 = (f32[1,3072]{1,0:T(1,128)S(1)}, f32[1,3072]{1,0:T(1,128)}, u32[]{:S(2)}) copy-start(f32[1,3072]{1,0:T(1,128)} %get-tuple-element.137) | copy-start | bytes 36868
  358.6 11.4 %copy-start.46 = (f32[768]{0:T(1024)S(1)}, f32[768]{0:T(1024)}, u32[]{:S(2)}) copy-start(f32[768]{0:T(1024)} %get-tuple-element.67) | copy-start | bytes 9220
  358.7 11.4 %copy-start.47 = (f32[768]{0:T(1024)S(1)}, f32[768]{0:T(1024)}, u32[]{:S(2)}) copy-start(f32[768]{0:T(1024)} %get-tuple-element.65) | copy-start | bytes 9220
  384.4 6.0 slice-start.2
  384.4 6.4 copy-start.65
  407.8 11.7 %copy-start.19 = (f32[1024,768]{1,0:T(8,128)S(1)}, f32[1024,768]{1,0:T(8,128)}, u32[]{:S(2)}) copy-start(f32[1024,768]{1,0:T(8,128)} %get-tuple-element.146) | copy-start | bytes 9437188
  510.8 6.9 %copy-start.62 = (bf16[768,768]{1,0:T(8,128)(2,1)S(1)}, bf16[768,768]{1,0:T(8,128)(2,1)}, u32[]{:S(2)}) copy-start(bf16[768,768]{1,0:T(8,128)(2,1)} %all-gather.12.cloned.1.call-done) | copy-start | bytes 3538948
  510.8 17.9 %slice-start = ((s8[6291456]{0:T(1024)(128)(4,1)}), s8[4194304]{0:T(1024)(128)(4,1)S(1)}, s32[]{:S(2)}) async-start(s8[6291456]{0:T(1024)(128)(4,1)} %bitcast.297), calls=%async_computation.6 | async-start | bytes 8388608
  517.7 11.0 %slice-start.1 = ((s8[6291456]{0:T(1024)(128)(4,1)}), s8[2097152]{0:T(1024)(128)(4,1)S(1)}, s32[]{:S(2)}) async-start(s8[6291456]{0:T(1024)(128)(4,1)} %bitcast.297), calls=%async_computation.7 | async-start | bytes 4194304
  517.7 11.0 %copy-start.63 = (bf16[768,768]{1,0:T(8,128)(2,1)S(1)}, bf16[768,768]{1,0:T(8,128)(2,1)}, u32[]{:S(2)}) copy-start(bf16[768,768]{1,0:T(8,128)(2,1)} %all-gather.8.cloned.1.call-done) | copy-start | bytes 3538948
  537.3 4.6 copy-start.3
  542.2 5.9 collective-permute-start.2
  550.6 5.7 copy-start.7
  556.2 36.8 %collective-permute-start.3 = (bf16[8,128,768]{2,1,0:T(8,128)(2,1)}, bf16[8,128,768]{2,1,0:T(8,128)(2,1)}, u32[]{:S(2)}, u32[]{:S(2)}) collective-permute-start(bf16[8,128,768]{2,1,0:T(8,128)(2,1)} %fusion.42), channel_id=1, source_target_pairs={{0,2},{2,0},{1,3},{3,1},{4,6},{6,4},{5,7},{7,5},{8,10},{10,8},{9,1... | collective-permute-start | bytes 4718600 | tf_op jit(solution)/shard_map/ppermute | solution.py:190
  577.2 4.8 copy-start.25
  582.0 11.0 %copy-start.6 = (bf16[8,128,768]{2,1,0:T(8,128)(2,1)S(1)}, bf16[8,128,768]{2,1,0:T(8,128)(2,1)}, u32[]{:S(2)}) copy-start(bf16[8,128,768]{2,1,0:T(8,128)(2,1)} %param.24) | copy-start | bytes 4718596
  582.0 11.0 %copy-start.29 = (f32[768]{0:T(1024)S(1)}, f32[768]{0:T(1024)}, u32[]{:S(2)}) copy-start(f32[768]{0:T(1024)} %copy-done.28) | copy-start | bytes 9220
  598.4 46.9 %copy-start.15 = (f32[3072,96]{0,1:T(8,128)S(1)}, f32[3072,96]{0,1:T(8,128)}, u32[]{:S(2)}) copy-start(f32[3072,96]{0,1:T(8,128)} %param.34) | copy-start | bytes 3538948
  603.7 43.6 %copy-start.17 = (f32[768,384]{1,0:T(8,128)S(1)}, f32[768,384]{1,0:T(8,128)}, u32[]{:S(2)}) copy-start(f32[768,384]{1,0:T(8,128)} %param.33) | copy-start | bytes 3538948
  603.7 44.9 %copy-start.21 = (f32[768,96]{0,1:T(8,128)S(1)}, f32[768,96]{0,1:T(8,128)}, u32[]{:S(2)}) copy-start(f32[768,96]{0,1:T(8,128)} %param.32) | copy-start | bytes 884740
  603.7 45.7 %copy-start.22 = (f32[768,96]{0,1:T(8,128)S(1)}, f32[768,96]{0,1:T(8,128)}, u32[]{:S(2)}) copy-start(f32[768,96]{0,1:T(8,128)} %param.30) | copy-start | bytes 884740
  603.7 46.5 %copy-start.23 = (f32[768,96]{0,1:T(8,128)S(1)}, f32[768,96]{0,1:T(8,128)}, u32[]{:S(2)}) copy-start(f32[768,96]{0,1:T(8,128)} %param.29) | copy-start | bytes 884740
  645.3 7.2 %copy-start.1 = (s32[8,512]{1,0:T(8,128)S(1)}, s32[8,512]{1,0:T(8,128)}, u32[]{:S(2)}) copy-start(s32[8,512]{1,0:T(8,128)} %param.25) | copy-start | bytes 49156
  645.3 5.8 copy-start.24
  (32 other events, 77.1 us)
Sparse Core Ops, SparseCore 0:
  10.8 43.7 all-gather.11
  57.4 39.8 all-gather.7
  100.0 39.7 all-gather.9
  142.5 39.8 all-gather.13
  184.8 79.7 all-gather.15
  267.3 78.0 all-gather.17

commit v2 on v1

v2 whole, which is shorter than its diff:
```python
import functools

import jax
import jax.numpy as jnp
from jax import lax
from jax.experimental import pallas as pl
from jax.experimental.pallas import tpu as pltpu
from jax.sharding import PartitionSpec as P

EPS = 1e-05
SCORE_WEIGHT = 0.0625
NEGATIVE = -1e30
F32 = jnp.float32
BF16 = jnp.bfloat16
PAIR = 128
A_Q, A_K, A_V, A_O, A_D, B_Q, B_V, B_O, B_D, G1, S1, G2, S2, C_IN, C_CTX, C_MID = range(16)
A_U, B_U, C_HID, VECTORS = 16, 20, 24, 32
G_Q, G_K, G_V, G_O, G_D, G_BQ, G_BV, G_BO, G_BD, G_G1, G_S1, G_G2, G_S2, G_CIN, G_CCTX, G_CMID = range(16)
G_U, G_BU, G_CHID, LOSS, SUMS = 16, 20, 24, 28, 29


def dot_nt(left, right):
    return lax.dot_general(left, right, (((1,), (1,)), ((), ())), preferred_element_type=F32)


def dot_nn(left, right):
    return lax.dot_general(left, right, (((1,), (0,)), ((), ())), preferred_element_type=F32)


def dot_tn(left, right):
    return lax.dot_general(left, right, (((0,), (0,)), ((), ())), preferred_element_type=F32)


def columns(value):
    return jnp.sum(value, axis=0, keepdims=True)


def clip_parts(value, bound):
    ratio = value / bound
    bent = jnp.tanh(ratio)
    slope = 1.0 - bent * bent
    return bound * bent, slope, bent - ratio * slope


def norm_parts(value, gain, shift):
    centre = value - jnp.mean(value, axis=-1, keepdims=True)
    inverse = lax.rsqrt(jnp.mean(centre * centre, axis=-1, keepdims=True) + EPS)
    unit = centre * inverse
    return unit * gain + shift, unit, inverse


def norm_back(grad, unit, inverse, gain):
    scaled = grad * gain
    return inverse * (
        scaled
        - jnp.mean(scaled, axis=-1, keepdims=True)
        - unit * jnp.mean(scaled * unit, axis=-1, keepdims=True)
    )


def halves(value):
    lane = lax.broadcasted_iota(jnp.int32, value.shape, 1)
    half = value.shape[1] // 2
    zero = jnp.zeros_like(value)
    return jnp.concatenate(
        [jnp.where(lane < half, value, zero), jnp.where(lane < half, zero, value)], axis=0
    )


def by_head(first, second):
    shape = jnp.broadcast_shapes(first.shape, second.shape)
    lane = lax.broadcasted_iota(jnp.int32, shape[:-1] + (PAIR,), 1)
    return jnp.where(lane < PAIR // 2, first, second)


def folded(value):
    return jnp.sum(value.reshape(value.shape[0] // 8, 8, value.shape[1]), axis=0)


def project_row(hidden, own_hidden, sq, sk, sv, small, s_query, s_key, s_value):
    c_in = small[C_IN : C_IN + 1]
    inverse_in = 1.0 / c_in
    low = (c_in * jnp.tanh(hidden[...].astype(F32) * inverse_in)).astype(BF16)
    s_key[...] = dot_nt(low, sk[...]).astype(BF16)
    s_value[...] = dot_nt(low, sv[...]).astype(BF16)
    low = (c_in * jnp.tanh(own_hidden[...].astype(F32) * inverse_in)).astype(BF16)
    s_query[...] = dot_nt(low, sq[...])


def attend_row(
    scale, small, query_seg, key_seg, teacher, s_query, s_key, s_value, s_context, spread, probs, gaps, distill,
):
    block, width = s_query.shape
    same = query_seg[:, 0:1] == key_seg[0:1, :]
    bias = jnp.where(same, 0.0, NEGATIVE)
    counted = jnp.where(query_seg[:, 1:2] == key_seg[1:2, :], 1.0, 0.0)

    def pair(index, carry):
        at = pl.ds(pl.multiple_of(index * PAIR, PAIR), PAIR)
        query = (
            (small[A_Q : A_Q + 1, at] * s_query[:, at] + small[B_Q : B_Q + 1, at])
            * (small[A_K : A_K + 1, at] * scale)
        ).astype(BF16)
        scores = dot_nt(halves(query), s_key[:, at])
        expos, inverses = [], []
        sums = jnp.zeros((8, scores.shape[1]), F32)
        for head in range(2):
            mine = scores[head * block : (head + 1) * block]
            gap = (mine - teacher[2 * index + head].astype(F32)) * counted
            sums = sums + folded(gap * gap)
            gaps[2 * index + head] = (gap * SCORE_WEIGHT).astype(BF16)
            masked = mine + bias
            expo = jnp.exp(masked - jnp.max(masked, axis=-1, keepdims=True))
            inverses.append(1.0 / jnp.sum(expo, axis=-1, keepdims=True))
            expo = expo.astype(BF16)
            probs[2 * index + head] = expo
            expos.append(expo)
        distill[...] += sums
        both = dot_nn(jnp.concatenate(expos, axis=0), s_value[:, at])
        inverse = by_head(inverses[0], inverses[1])
        s_context[:, at] = by_head(both[:block], both[block:]) * inverse
        spread[:, at] = inverse
        return carry

    lax.fori_loop(0, width // PAIR, pair, 0)


MESH = pl.DeviceIdType.MESH
UNITS = 12
STEPS = 10
SHARED = (6, 7)

def remote(source, target, send, recv, dp, seq):
    return pltpu.make_async_remote_copy(
        src_ref=source, dst_ref=target, send_sem=send, recv_sem=recv, device_id=(dp, seq), device_id_type=MESH
    )

class Streams:
    def __init__(self, lines, own, full, z_sems, x_sems, y_sems, c_sems, l_sems):
        self.lines, self.own, self.full = lines, own, full
        self.z_sems, self.x_sems, self.y_sems, self.c_sems, self.l_sems = z_sems, x_sems, y_sems, c_sems, l_sems
        self.dp, self.seq = lax.axis_index("dp"), lax.axis_index("seq")
        self.zi, self.xi = self.dp // 2, self.dp % 2
        self.yi, self.ci = self.seq // 2, self.seq % 2
        self.size = own.shape[1]
        self.half = self.size // 2

    def unit(self, t, partner=False):
        if t in SHARED:
            return SHARED[0] + 2 * (t - SHARED[0]) + (1 - self.yi if partner else self.yi)
        return t if t < SHARED[0] else t + 2

    def piece(self, u, dp):
        start = pl.multiple_of(dp * self.size + self.ci * self.half, self.half)
        return self.full.at[u, pl.ds(start, self.half)]

    def own_piece(self, u):
        return self.own.at[u, pl.ds(pl.multiple_of(self.ci * self.half, self.half), self.half)]

    def z_copy(self, u, src, to):
        place = self.piece(u, src * 2 + self.xi)
        return remote(self.own_piece(u) if src is self.zi else place, place,
                      self.z_sems.at[0, u, to + self.lines * src], self.z_sems.at[1, u, src], to * 2 + self.xi, self.seq)

    def x_copy(self, u, src):
        place = self.piece(u, src * 2 + self.xi)
        return remote(self.own_piece(u) if src is self.zi else place, place, self.x_sems.at[0, u, src], self.x_sems.at[1, u, src],
                      self.zi * 2 + 1 - self.xi, self.seq)

    def x_arrival(self, u, src):
        place = self.piece(u, src * 2 + 1 - self.xi)
        return remote(place, place, self.x_sems.at[0, u, src], self.x_sems.at[1, u, src], self.zi * 2 + 1 - self.xi, self.seq)

    def y_copy(self, u, dp):
        place = self.piece(u, dp)
        return remote(place, place, self.y_sems.at[0, u, dp], self.y_sems.at[1, u, dp], self.dp, (1 - self.yi) * 2 + self.ci)

    def c_copy(self, u, dp):
        place = self.piece(u, dp)
        return remote(place, place, self.c_sems.at[0, u, dp], self.c_sems.at[1, u, dp], self.dp, self.yi * 2 + 1 - self.ci)

    def local_copy(self, u):
        start = pl.multiple_of(self.dp * self.size, self.size)
        return pltpu.make_async_copy(self.own.at[u], self.full.at[u, pl.ds(start, self.size)], self.l_sems.at[u])

    def each_row(self, run):
        for k in range(1, self.lines):
            pl.when(self.zi >= k)(functools.partial(run, self.zi - k, True))
            pl.when(self.zi + k < self.lines)(functools.partial(run, self.zi + k, False))

    def neighbours(self, run):
        pl.when(self.zi > 0)(lambda: run(self.zi - 1))
        pl.when(self.zi < self.lines - 1)(lambda: run(self.zi + 1))

    def relay(self, src, below, run):
        if below:
            pl.when(self.zi < self.lines - 1)(lambda: run(self.zi + 1))
        else:
            pl.when(self.zi > 0)(lambda: run(self.zi - 1))

    def launch(self, t):
        u = self.unit(t)
        self.x_copy(u, self.zi).start()
        self.neighbours(lambda to: self.z_copy(u, self.zi, to).start())

    def along_z(self, t):
        u = self.unit(t)
        def run(src, below):
            self.z_copy(u, src, self.zi).wait_recv()
            self.relay(src, below, lambda to: self.z_copy(u, src, to).start())
            self.x_copy(u, src).start()
            self.spread(t, u, src * 2 + self.xi)
        self.each_row(run)

    def over_x(self, t):
        u = self.unit(t)
        def run(src, below):
            self.x_arrival(u, src).wait_recv()
            self.spread(t, u, src * 2 + 1 - self.xi)
        run(self.zi, None)
        self.each_row(run)

    def spread(self, t, u, dp):
        if t in SHARED:
            self.y_copy(u, dp).start()
        self.c_copy(u, dp).start()

    def others(self, run):
        self.each_row(lambda src, below: run(src * 2 + self.xi))
        run(self.zi * 2 + 1 - self.xi)
        self.each_row(lambda src, below: run(src * 2 + 1 - self.xi))

    def over_y(self, t):
        u = self.unit(t, True)
        def run(dp):
            self.y_copy(u, dp).wait_recv()
            self.c_copy(u, dp).start()
        self.others(run)

    def arrived(self, u):
        self.others(lambda dp: self.c_copy(u, dp).wait_recv())
        self.local_copy(u).wait()

    def finish(self):
        for t in range(STEPS):
            u = self.unit(t)
            self.x_copy(u, self.zi).wait_send()
            self.neighbours(lambda to: self.z_copy(u, self.zi, to).wait_send())
            def run(src, below):
                self.relay(src, below, lambda to: self.z_copy(u, src, to).wait_send())
                self.x_copy(u, src).wait_send()
            self.each_row(run)
            if t in SHARED:
                self.others(lambda dp: self.y_copy(u, dp).wait_send())
        for u in range(UNITS):
            self.others(lambda dp: self.c_copy(u, dp).wait_send())


def greet(dp_count):
    dp, seq = lax.axis_index("dp"), lax.axis_index("seq")
    barrier = pltpu.get_barrier_semaphore()
    for k in range(1, dp_count):
        pl.semaphore_signal(barrier, inc=1, device_id=(lax.rem(dp + k, dp_count), seq), device_id_type=MESH)
    pl.semaphore_signal(barrier, inc=1, device_id=(dp, seq // 2 * 2 + 1 - seq % 2), device_id_type=MESH)
    pl.semaphore_signal(barrier, inc=1, device_id=(dp, (1 - seq // 2) * 2 + seq % 2), device_id_type=MESH)
    pl.semaphore_wait(barrier, dp_count + 1)

AHEAD = 3
NEAR = 3


def first_kernel(
    scale, dp_count, own, own_vectors, hidden, own_hidden, query_seg, key_seg, teacher,
    full, table, s_query, s_key, s_value, s_context, spread, probs, gaps, distill,
    whole, vectors, weights, z_sems, x_sems, y_sems, c_sems, l_sems, h_sems, o_sems, v_sems, w_sems,
):
    step = pl.program_id(0)
    rows, block = hidden.shape[0], hidden.shape[1]
    s = Streams(dp_count // 2, own, full, z_sems, x_sems, y_sems, c_sems, l_sems)
    across, beside = (1 - s.yi) * 2 + s.ci, s.yi * 2 + 1 - s.ci

    def place(r, seq):
        return whole.at[r, pl.ds(pl.multiple_of(seq * block, block), block)]

    def to_chip(r):
        return remote(hidden.at[r], place(r, s.seq), h_sems.at[0, 0, r], h_sems.at[1, 0, r], s.dp, across)

    def to_core(r):
        return remote(hidden.at[r], place(r, s.seq), h_sems.at[0, 1, r], h_sems.at[1, 1, r], s.dp, beside)

    def passed_on(r):
        return remote(place(r, across), place(r, across), h_sems.at[0, 2, r], h_sems.at[1, 2, r], s.dp, beside)

    def kept(r):
        return pltpu.make_async_copy(hidden.at[r], place(r, s.seq), o_sems.at[r])

    def hidden_pump(r):
        to_chip(r).wait_recv()
        passed_on(r).start()
        if r + NEAR < rows:
            to_chip(r + NEAR).start()

    def vector_copy(k):
        mine = vectors.at[pl.ds(pl.multiple_of(s.dp * s.size, s.size), s.size)]
        return remote(own_vectors, mine, v_sems.at[0, k], v_sems.at[1, k], lax.rem(s.dp + k, dp_count), s.seq)

    def fetch(u):
        return pltpu.make_async_copy(full.at[u], weights.at[u], w_sems.at[u])

    def launch(t):
        if t < STEPS:
            s.launch(t)

    @pl.when(step == 0)
    def _():
        distill[...] = jnp.zeros_like(distill)
        greet(dp_count)
        for k in range(1, dp_count):
            vector_copy(k).start()
        launch(0)
        for r in range(NEAR):
            to_chip(r).start()
        launch(1)
        for u in range(UNITS):
            s.local_copy(u).start()
        launch(2)
        for r in range(rows):
            to_core(r).start()
            kept(r).start()
        mine = pl.ds(pl.multiple_of(s.dp * s.size, s.size), s.size)
        vectors[mine] = own_vectors[...]
        for t in range(3):
            s.along_z(t)
            launch(t + AHEAD)
            s.over_x(t)
            hidden_pump(t)
        for k in range(1, dp_count):
            vector_copy(k).wait()
        table[...] = jnp.transpose(vectors[...].astype(F32))[: table.shape[0]]
        for u in range(3):
            s.arrived(u)
            fetch(u).start()
        for u in range(3):
            fetch(u).wait()

    for r in range(rows):
        @pl.when(step == r)
        def _(r=r):
            if r + 3 < rows:
                hidden_pump(r + 3)
            if r + 3 < STEPS:
                s.along_z(r + 3)
                launch(r + 3 + AHEAD)
            kept(r).wait()
            to_core(r).wait_recv()
            passed_on(r).wait_recv()

    project_row(whole.at[step], own_hidden.at[0], weights.at[0], weights.at[1], weights.at[2], table,
                s_query.at[0], s_key.at[0], s_value.at[0])

    for r in range(rows):
        @pl.when(step == r)
        def _(r=r):
            if r + 3 < STEPS:
                s.over_x(r + 3)

    attend_row(scale, table, query_seg.at[0], key_seg.at[0], teacher.at[0], s_query.at[0], s_key.at[0], s_value.at[0],
               s_context.at[0], spread.at[0], probs.at[0], gaps.at[0], distill)

    @pl.when(step == rows - 1)
    def _():
        for t in range(rows + 3, STEPS):
            s.along_z(t)
            s.over_x(t)
        for t in SHARED:
            s.over_y(t)
        for u in range(3, UNITS):
            s.arrived(u)
        s.finish()
        for r in range(rows):
            to_chip(r).wait_send()
            to_core(r).wait_send()
            passed_on(r).wait_send()


def plain_kernel(
    scale, whole, own_hidden, weights, table, query_seg, key_seg, teacher,
    s_query, s_key, s_value, s_context, spread, probs, gaps, distill,
):
    @pl.when(pl.program_id(0) == 0)
    def _():
        distill[...] = jnp.zeros_like(distill)

    project_row(whole.at[0], own_hidden.at[0], weights.at[0], weights.at[1], weights.at[2], table,
                s_query.at[0], s_key.at[0], s_value.at[0])
    attend_row(scale, table, query_seg.at[0], key_seg.at[0], teacher.at[0], s_query.at[0], s_key.at[0], s_value.at[0],
               s_context.at[0], spread.at[0], probs.at[0], gaps.at[0], distill)


def chain(weights, small, hidden, teacher, live, s_context, sums, final_out, grad_first_out,
          grad_ctx_out, pres, slopes, bounds):
    def vec(i):
        return small[i : i + 1]

    def add(i, value):
        sums[i] += folded(value)

    width = hidden.shape[1]
    inputs = hidden.astype(F32)
    context = vec(A_V) * s_context + vec(B_V)
    context_low, ctx_slope, ctx_bound = clip_parts(context, vec(C_CTX))
    s_out = dot_nt(context_low.astype(BF16), weights[3])
    normed, unit1, inverse1 = norm_parts(inputs + vec(A_O) * s_out + vec(B_O), vec(G1), vec(S1))
    normed_low, mid_slope, mid_bound = clip_parts(normed, vec(C_MID))
    normed_low = normed_low.astype(BF16)
    s_down = jnp.zeros_like(inputs)
    for i in range(4):
        s_up = dot_nt(normed_low, weights[4 + 2 * i])
        pres[i] = s_up
        pre = vec(A_U + i) * s_up + vec(B_U + i)
        phi = 0.5 + 0.5 * lax.erf(pre * (0.5**0.5))
        act_slope = phi + pre * (jnp.exp(-0.5 * pre * pre) * 0.3989422804014327)
        hidden_low, slope, bound = clip_parts(pre * phi, vec(C_HID + i))
        slopes[i] = slope * act_slope
        bounds[i] = bound
        s_down = s_down + dot_nt(hidden_low.astype(BF16), weights[5 + 2 * i])
    final, unit2, inverse2 = norm_parts(normed + vec(A_D) * s_down + vec(B_D), vec(G2), vec(S2))
    final_out[...] = final.astype(BF16)
    errors = (final - teacher.astype(F32)) * live
    add(LOSS, errors * errors)
    add(G_G2, errors * unit2)
    add(G_S2, errors)
    grad_second = norm_back(errors, unit2, inverse2, vec(G2))
    add(G_D, grad_second * s_down)
    add(G_BD, grad_second)
    branch = (grad_second * vec(A_D)).astype(BF16)
    grad_mid = jnp.zeros_like(inputs)
    for i in range(4):
        grad_hid = dot_nn(branch, weights[5 + 2 * i])
        add(G_CHID + i, grad_hid * bounds[i])
        up_grad = grad_hid * slopes[i]
        add(G_BU + i, up_grad)
        add(G_U + i, up_grad * pres[i])
        grad_mid = grad_mid + dot_nn((up_grad * vec(A_U + i)).astype(BF16), weights[4 + 2 * i])
    add(G_CMID, grad_mid * mid_bound)
    grad_normed = grad_second + grad_mid * mid_slope
    add(G_G1, grad_normed * unit1)
    add(G_S1, grad_normed)
    grad_first = norm_back(grad_normed, unit1, inverse1, vec(G1))
    grad_first_out[...] = grad_first
    add(G_O, grad_first * s_out)
    add(G_BO, grad_first)
    grad_ctx_low = dot_nn((grad_first * vec(A_O)).astype(BF16), weights[3])
    add(G_CCTX, grad_ctx_low * ctx_bound)
    grad_ctx = grad_ctx_low * ctx_slope
    add(G_V, grad_ctx * s_context)
    add(G_BV, grad_ctx)
    grad_ctx_out[...] = grad_ctx


def attend_back_row(scale, small, s_query, s_key, s_value, s_context, spread, probs, gaps,
                    grad_ctx, key_grads, value_grads, query_grads):
    block, width = s_query.shape

    def pair(index, carry):
        at = pl.ds(pl.multiple_of(index * PAIR, PAIR), PAIR)
        raw = small[A_Q : A_Q + 1, at] * s_query[:, at] + small[B_Q : B_Q + 1, at]
        query = halves((raw * (small[A_K : A_K + 1, at] * scale)).astype(BF16))
        pulled = grad_ctx[:, at] * small[A_V : A_V + 1, at] * spread[:, at]
        product = pulled * s_context[:, at]
        lane = lax.broadcasted_iota(jnp.int32, product.shape, 1)
        left = jnp.sum(jnp.where(lane < PAIR // 2, product, 0.0), axis=-1, keepdims=True)
        right = jnp.sum(jnp.where(lane < PAIR // 2, 0.0, product), axis=-1, keepdims=True)
        accum_grad = halves(pulled.astype(BF16))
        prob_grad = dot_nt(accum_grad, s_value[:, at])
        score_grads, expos = [], []
        for head, delta in ((0, left), (1, right)):
            expo = probs[2 * index + head]
            expos.append(expo)
            mine = prob_grad[head * block : (head + 1) * block]
            score_grads.append(
                (expo.astype(F32) * (mine - delta) + gaps[2 * index + head].astype(F32)).astype(BF16)
            )
        score_grad = jnp.concatenate(score_grads, axis=0)
        both = dot_nn(score_grad, s_key[:, at])
        query_grads[:, at] = by_head(both[:block], both[block:]) * scale
        key_grads[:, at] = dot_tn(score_grad, query).astype(BF16)
        value_grads[:, at] = dot_tn(jnp.concatenate(expos, axis=0), accum_grad).astype(BF16)
        return carry

    lax.fori_loop(0, width // PAIR, pair, 0)


def chain_kernel(weights, small, hidden, teacher, live, s_context, final, grad_first, grad_ctx, sums_out,
                 sums, pres, slopes, bounds):
    step = pl.program_id(0)

    @pl.when(step == 0)
    def _():
        sums[...] = jnp.zeros_like(sums)

    rows, block, width = hidden.shape
    flat = (rows * block, width)
    chain(weights, small, hidden[...].reshape(flat), teacher[...].reshape(flat),
          live[...].reshape(rows * block, 1), s_context[...].reshape(flat), sums, final, grad_first,
          grad_ctx, pres, slopes, bounds)

    @pl.when(step == pl.num_programs(0) - 1)
    def _():
        sums_out[...] = sums[...]


def back_kernel(scale, weights, small, s_query, s_key, s_value, s_context, spread, probs, gaps, grad_ctx,
                pulled_in, own_in, sums, key_grads, value_grads, query_grads):
    step = pl.program_id(0)

    @pl.when(step == 0)
    def _():
        sums[...] = jnp.zeros_like(sums)

    attend_back_row(scale, small, s_query.at[0], s_key.at[0], s_value.at[0],
                    s_context.at[0], spread.at[0], probs.at[0], gaps.at[0],
                    grad_ctx, key_grads, value_grads, query_grads)
    back = query_grads[...]
    raw = small[A_Q : A_Q + 1] * s_query[0] + small[B_Q : B_Q + 1]
    sums[0] += folded(raw * back)
    query_grad = back * small[A_K : A_K + 1]
    sums[1] += folded(query_grad * s_query[0])
    sums[2] += folded(query_grad)
    own_in[...] = dot_nn((query_grad * small[A_Q : A_Q + 1]).astype(BF16), weights[0])
    pulled_in[0] = (dot_nn(key_grads[...], weights[1]) + dot_nn(value_grads[...], weights[2])).astype(BF16)


def signs_and_scale(latent):
    scale = jnp.mean(jnp.abs(latent), axis=0).astype(BF16)
    return jnp.sign(latent).astype(BF16).T, scale


def body(
    hidden_in,
    segment_ids,
    row_lengths,
    teacher_scores,
    teacher_hidden,
    w_query,
    w_key,
    w_value,
    w_out,
    w_up,
    w_down,
    b_query,
    b_value,
    b_out,
    b_up,
    b_down,
    norm1_gain,
    norm1_bias,
    norm2_gain,
    norm2_bias,
    clip_in,
    clip_ctx,
    clip_mid,
    clip_hid,
):
    rows, block, width = hidden_in.shape
    heads = teacher_scores.shape[1]
    head_dim = width // heads
    seq_len = segment_ids.shape[1]
    tokens = rows * block
    scale = head_dim ** (-0.5)
    place = lax.axis_index("seq")
    first = place * block

    dp_count = lax.axis_size("dp")
    size = w_query.shape[1]
    square = [signs_and_scale(w) for w in (w_query, w_key, w_value, w_out)]
    up_signs, up_scale = signs_and_scale(w_up)
    down = w_down.reshape(dp_count, 4, size, size)
    down_signs = jnp.sign(down).astype(BF16).transpose(1, 3, 0, 2).reshape(4, size, width)
    down_scale = jnp.mean(jnp.abs(w_down), axis=0).astype(BF16)
    pairs = jnp.stack([up_signs.reshape(4, size, width), down_signs], axis=1).reshape(8, size, width)
    own = jnp.concatenate([jnp.stack([s for s, _ in square]), pairs])
    own_vectors = jnp.concatenate(
        [jnp.stack([*(a for _, a in square), down_scale, b_query, b_value, b_out, b_down, norm1_gain, norm1_bias,
                    norm2_gain, norm2_bias, clip_in, clip_ctx, clip_mid]),
         up_scale.reshape(4, size), b_up.reshape(4, size), clip_hid.reshape(4, size)]
    )
    own_vectors = jnp.pad(own_vectors.T, ((0, 0), (0, PAIR - own_vectors.shape[0])))

    positions = jnp.arange(seq_len, dtype=jnp.int32)
    live = positions[None, :] < row_lengths[:, None]
    key_seg = jnp.stack([segment_ids, jnp.where(live, segment_ids, -1)], axis=1)
    own_seg = lax.dynamic_slice_in_dim(segment_ids, first, block, 1)
    query_live = lax.dynamic_slice_in_dim(live, first, block, 1)
    query_seg = jnp.stack([own_seg, jnp.where(query_live, own_seg, -2)], axis=2)

    def row_spec(*shape):
        return pl.BlockSpec((1,) + shape, lambda i: (i,) + (0,) * len(shape))

    def whole(array):
        return pl.BlockSpec(array.shape, lambda i: (0,) * array.ndim, pipeline_mode=pl.Buffered(1))

    three = pl.BlockSpec((3, width, width), lambda i: (0, 0, 0), pipeline_mode=pl.Buffered(1))
    attend_specs = [row_spec(block, width), row_spec(seq_len, width), row_spec(seq_len, width), row_spec(block, width),
                    row_spec(block, width), row_spec(heads, block, seq_len), row_spec(heads, block, seq_len),
                    pl.BlockSpec((8, seq_len), lambda i: (0, 0))]
    attend_shapes = [jax.ShapeDtypeStruct((rows, block, width), F32),
                     jax.ShapeDtypeStruct((rows, seq_len, width), BF16),
                     jax.ShapeDtypeStruct((rows, seq_len, width), BF16),
                     jax.ShapeDtypeStruct((rows, block, width), F32),
                     jax.ShapeDtypeStruct((rows, block, width), F32),
                     jax.ShapeDtypeStruct((rows, heads, block, seq_len), BF16),
                     jax.ShapeDtypeStruct((rows, heads, block, seq_len), BF16),
                     jax.ShapeDtypeStruct((8, seq_len), F32)]
    masks_specs = [row_spec(block, 2), row_spec(2, seq_len), row_spec(heads, block, seq_len)]
    anywhere = pl.BlockSpec(memory_space=pl.ANY)
    lines = dp_count // 2
    sems = pltpu.SemaphoreType.DMA
    if size % 32 == 0:
        full, table, s_query, s_key, s_value, s_context, spread, probs, gaps, distill = pl.pallas_call(
            functools.partial(first_kernel, scale, dp_count),
            grid=(rows,),
            in_specs=[anywhere, whole(own_vectors), anywhere, row_spec(block, width)] + masks_specs,
            out_specs=[anywhere, pl.BlockSpec((VECTORS, width), lambda i: (0, 0))] + attend_specs,
            out_shape=[jax.ShapeDtypeStruct((UNITS, width, width), BF16), jax.ShapeDtypeStruct((VECTORS, width), F32)]
            + attend_shapes,
            scratch_shapes=[
                pltpu.VMEM((rows, seq_len, width), BF16), pltpu.VMEM((width, PAIR), BF16), pltpu.VMEM((3, width, width), BF16),
                sems((2, UNITS, lines * lines)), sems((2, UNITS, lines)), sems((2, UNITS, dp_count)),
                sems((2, UNITS, dp_count)), sems((UNITS,)), sems((2, 3, rows)), sems((rows,)), sems((2, dp_count)), sems((3,)),
            ],
            compiler_params=pltpu.CompilerParams(collective_id=0, has_side_effects=True, vmem_limit_bytes=60 * 2**20),
        )(own, own_vectors, hidden_in, hidden_in, query_seg, key_seg, teacher_scores)
    else:
        full = lax.all_gather(own, "dp", axis=1, tiled=True)
        table = lax.all_gather(own_vectors, "dp", axis=0, tiled=True).astype(F32).T[:VECTORS]
        hidden_full = lax.all_gather(hidden_in, "seq", axis=1, tiled=True)
        s_query, s_key, s_value, s_context, spread, probs, gaps, distill = pl.pallas_call(
            functools.partial(plain_kernel, scale),
            grid=(rows,),
            in_specs=[row_spec(seq_len, width), row_spec(block, width), three, whole(table)] + masks_specs,
            out_specs=attend_specs,
            out_shape=attend_shapes,
            compiler_params=pltpu.CompilerParams(vmem_limit_bytes=60 * 2**20),
        )(hidden_full, hidden_in, full, table, query_seg, key_seg, teacher_scores)

    group = 2
    def group_spec(*shape):
        return pl.BlockSpec((group,) + shape, lambda i: (i,) + (0,) * len(shape))
    flat_spec = pl.BlockSpec((group * block, width), lambda i: (i, 0))
    live_column = query_live.astype(F32)[..., None]
    final, grad_first, grad_ctx, sums = pl.pallas_call(
        chain_kernel,
        grid=(rows // group,),
        in_specs=[whole(full), whole(table),
                  group_spec(block, width), group_spec(block, width), group_spec(block, 1), group_spec(block, width)],
        out_specs=[flat_spec, flat_spec, flat_spec,
                   pl.BlockSpec((SUMS, 8, width), lambda i: (0, 0, 0))],
        out_shape=[jax.ShapeDtypeStruct((tokens, width), BF16),
                   jax.ShapeDtypeStruct((tokens, width), F32),
                   jax.ShapeDtypeStruct((tokens, width), F32),
                   jax.ShapeDtypeStruct((SUMS, 8, width), F32)],
        scratch_shapes=[pltpu.VMEM((SUMS, 8, width), F32)]
        + [pltpu.VMEM((4, group * block, width), F32)] * 3,
        compiler_params=pltpu.CompilerParams(vmem_limit_bytes=60 * 2**20),
    )(full, table, hidden_in, teacher_hidden, live_column, s_context)
    one_spec = pl.BlockSpec((block, width), lambda i: (i, 0))
    pulled_in, own_in, more = pl.pallas_call(
        functools.partial(back_kernel, scale),
        grid=(rows,),
        in_specs=[three, whole(table),
                  row_spec(block, width), row_spec(seq_len, width), row_spec(seq_len, width), row_spec(block, width),
                  row_spec(block, width), row_spec(heads, block, seq_len), row_spec(heads, block, seq_len), one_spec],
        out_specs=[row_spec(seq_len, width), one_spec, pl.BlockSpec((3, 8, width), lambda i: (0, 0, 0))],
        out_shape=[jax.ShapeDtypeStruct((rows, seq_len, width), BF16),
                   jax.ShapeDtypeStruct((tokens, width), F32),
                   jax.ShapeDtypeStruct((3, 8, width), F32)],
        scratch_shapes=[pltpu.VMEM((seq_len, width), BF16), pltpu.VMEM((seq_len, width), BF16),
                        pltpu.VMEM((block, width), F32)],
        compiler_params=pltpu.CompilerParams(vmem_limit_bytes=60 * 2**20),
    )(full, table, s_query, s_key, s_value, s_context, spread, probs, gaps, grad_ctx)
    sums = sums.at[G_K].set(more[0]).at[G_Q].set(more[1]).at[G_BQ].set(more[2])
    objective = 0.5 * jnp.sum(sums[LOSS]) + 0.5 * SCORE_WEIGHT * jnp.sum(distill)

    crossed = lax.psum_scatter(pulled_in, "seq", scatter_dimension=1, tiled=True).astype(F32)
    grad_low = own_in + crossed.reshape(tokens, width)
    inputs = hidden_in.astype(F32).reshape(tokens, width)
    unused, in_slope, in_bound = clip_parts(inputs, table[C_IN : C_IN + 1])
    grad_input = grad_first + grad_low * in_slope
    sums = jnp.sum(sums, axis=1)
    wide_sums = sums[16:28]
    sums = sums[:16].at[G_CIN].set(columns(grad_low * in_bound)[0])
    sums, wide_sums, objective = lax.psum((sums, wide_sums, objective), ("dp", "seq"))
    at = lax.axis_index("dp")
    sums = lax.dynamic_slice_in_dim(sums, at * size, size, 1)
    wide_sums = lax.dynamic_slice_in_dim(wide_sums, at * size, size, 1).reshape(3, 4 * size)
    loss = objective / (lax.axis_size("dp") * rows * seq_len)
    grads = [
        jnp.sign(w) * (s / w.shape[0])
        for w, s in zip(
            (w_query, w_key, w_value, w_out, w_up, w_down),
            (sums[0], sums[1], sums[2], sums[3], wide_sums[0], sums[4]),
        )
    ]
    return (
        final.reshape(rows, block, width).astype(BF16),
        loss,
        grad_input.reshape(rows, block, width),
        *grads,
        sums[5],
        sums[6],
        sums[7],
        wide_sums[1],
        sums[8],
        sums[9],
        sums[10],
        sums[11],
        sums[12],
        sums[13],
        sums[14],
        sums[15],
        wide_sums[2],
    )


def solution(mesh):
    rows = P("dp", "seq", None)
    cols = P(None, "dp")
    vec = P("dp")
    return jax.shard_map(
        body,
        mesh=mesh,
        in_specs=(rows, P("dp", None), vec, P("dp", None, "seq", None), rows)
        + (cols,) * 6
        + (vec,) * 13,
        out_specs=(rows, P(), rows) + (cols,) * 6 + (vec,) * 13,
        check_vma=False,
    )
```

time: 666 us -> 387 us (0.58)
  Pallas kernels: 0 us -> 232 us
  matrix products: 228 us -> 0 us
  local copies, waits for them, and re-layouts: 165 us -> 19.2 us
  other arithmetic: 100 us -> 26.8 us
  blocking collectives: 103 us -> 41.4 us
  waiting for transfers between devices: 41.1 us -> 49.3 us
    pallas_call x0 -> x3, Pallas kernels: none -> 232 us  [the longest x1 143 us: body(): pl.pallas_call(functools.partial(first_kernel, scale, dp_count), grid=(ro...]
    dot_general x18 -> x0, matrix products: 228 us -> none  [the longest x6 53.8 us: dot_nn(): lax.dot_general(left, right, (((1,), (0,)), ((), ())), preferred_element_...]
    unnamed x149 -> x56, local copies, waits for them, and re-layouts: 71.9 us -> 5.39 us
    all_gather x2 -> x0, blocking collectives: 61.9 us -> none  [the longest x1 31 us: body(): small = lax.all_gather(small, 'dp', axis=1, tiled=True).astype(F32)]
    reduce_scatter x0 -> x1, waiting for transfers between devices: none -> 49.3 us  [body(): lax.psum_scatter(pulled_in, 'seq', scatter_dimension=1, tiled=True)]
    gather x17 -> x0, local copies, waits for them, and re-layouts: 43.5 us -> none
    ppermute x4 -> x0, waiting for transfers between devices: 40.9 us -> none  [the longest x1 28.6 us: body(): across = lax.ppermute(hidden_in, 'seq', chip_swap)]
    sub x1 -> x0, other arithmetic: 33 us -> none  [body(): expo = jnp.exp(jnp.where(same, scores - top, NEGATIVE))]
  transfers between devices with their start and end apart: 10 -> 1, of which waited for: 3 -> 1; matrix products, arithmetic and copies ran while one was open for 43% -> 2% of each run, Pallas kernels for 0% -> 0%
where the time goes in v2:
time: 387 us
  Pallas kernels  232 us (60%)
  waiting for transfers between devices  49.3 us (13%)
  blocking collectives  41.4 us (11%)
  other arithmetic  26.8 us (7%)
  local copies, waits for them, and re-layouts  19.2 us (5%)
  between operations  17.7 us (5%)
    pallas_call x1, Pallas kernels, body(): pl.pallas_call(functools.partial(first_kernel, scale, dp_count), grid=(ro...  143 us
    reduce_scatter x1, waiting for transfers between devices, body(): lax.psum_scatter(pulled_in, 'seq', scatter_dimension=1, tiled=True)  49.3 us
    pallas_call x1, Pallas kernels, body(): pl.pallas_call(functools.partial(back_kernel, scale), grid=(rows,), in_sp...  47.2 us
    pallas_call x1, Pallas kernels, body(): pl.pallas_call(chain_kernel, grid=(rows // group,), in_specs=[whole(full)...  42 us
    psum x1, blocking collectives, body(): lax.psum((sums, wide_sums, objective), ('dp', 'seq'))  41.4 us
  transfers between devices with their start and end apart: 1, of which 1 were waited for; matrix products, arithmetic and copies ran while one was open for 2% of the time, Pallas kernels for 0%

profile of v2, /device:TPU:0, one launch (start us, length us, event | category | flops | bytes accessed | tf_op | source)
XLA Modules:
  0.0 386.6 jit_solution(16907043140699569011)
XLA Ops:
  7.3 0.8 iota_compare_fusion
  8.1 0.6 convert_bitcast_fusion
  8.7 1.3 dynamic-slice_bitcast_fusion
  10.0 0.8 broadcast_select_fusion
  10.7 1.3 stack.90
  12.1 2.1 abs_reduce_fusion
  14.2 0.4 copy.91
  14.7 0.7 fusion.1
  15.9 0.8 reshape.270
  16.7 0.8 reshape.271
  17.4 0.7 multiply_convert_fusion
  18.2 0.7 pad_add_fusion.1
  18.9 1.0 copy.95.query_seg
  20.0 1.7 copy.96.live
  21.7 1.3 abs_reduce_fusion.1
  23.2 0.1 copy.94
  23.4 2.3 convert_element_type.104
  25.8 0.6 stack_reshape.7
  26.4 0.3 sign_convert_fusion.1
  27.0 0.8 copy-done.7
  27.8 0.6 copy-done.11
  28.7 0.6 pad_add_fusion.key_seg
  29.3 0.6 pad.12.own_vectors
  30.0 1.2 copy-done.12
  31.2 143.0 %shard_map.399 = (bf16[12,768,768]{2,1,0:T(8,128)(2,1)}, f32[32,768]{1,0:T(8,128)}, f32[8,128,768]{2,1,0:T(8,128)}, bf16[8,512,768]{2,1,0:T(8,128)(2,1)}, bf16[8...) custom-call(bf16[12,96,768]{2,1,0:T(8,128)(2,1)} %copy-done.12, ...), custom_call_target="tpu_custom_call" | custom-call | tf_op jit(solution)/shard_map/pallas_call | solution.py:620
  174.3 42.0 %shard_map.400 = (bf16[1024,768]{1,0:T(8,128)(2,1)}, f32[1024,768]{1,0:T(8,128)}, f32[1024,768]{1,0:T(8,128)}, f32[29,8,768]{2,1,0:T(8,128)}) custom-call(bf16[12,768,768]{2,1,0:T(8,128)(2,1)} %get-tuple-element.87.weights, f32[32,768]{1,0:T(8,128)} %get-tuple-element.88.small, bf16[8,128,768]{2,1,0:T(8,128)(2,1)} %hidden.3, bf16[8,128,768]{2,1,0:T(8,128)(2,1)} %teacher.3, ...), custom_call_target="tpu_custom_call" | custom-call | tf_op jit(solution)/shard_map/pallas_call | solution.py:652
  216.3 47.2 %shard_map.401 = (bf16[8,512,768]{2,1,0:T(8,128)(2,1)}, f32[1024,768]{1,0:T(8,128)}, f32[3,8,768]{2,1,0:T(8,128)}) custom-call(bf16[12,768,768]{2,1,0:T(8,128)(2,1)} %get-tuple-element.87.weights, f32[32,768]{1,0:T(8,128)} %get-tuple-element.88.small, f32[8,128,768]{2,1,0:T(8,128)} %get-tuple-element.92.s_query, ...), custom_call_target="tpu_custom_call" | custom-call | tf_op jit(solution)/shard_map/pallas_call | solution.py:668
  263.6 0.8 copy-done.13
  264.4 0.6 slice_dynamic-update-slice_fusion.2
  265.0 0.6 slice_dynamic-update-slice_fusion.1
  265.6 0.6 slice_dynamic-update-slice_fusion
  266.2 1.3 reduce_sum.98
  267.5 0.6 reduce_sum.97
  268.8 1.4 slice_reduce_fusion
  270.8 0.8 slice_reduce_fusion.1
  271.6 49.3 %reduce-scatter.2.cloned.1.call-done = bf16[8,128,768]{2,1,0:T(8,128)(2,1)} async-done(((bf16[8,512,768]{2,1,0:T(8,128)(2,1)}), bf16[8,128,768]{2,1,0:T(8,128)(2,1)}) %reduce-scatter.2.cloned.1.call-update) | async-done | bytes 1572880 | tf_op jit(solution)/shard_map/reduce_scatter | solution.py:685
  320.9 6.3 %multiply_add_fusion = (f32[1024,768]{1,0:T(8,128)}, f32[768]{0:T(1024)S(1)}) fusion(f32[1024,768]{1,0:T(8,128)} %get-tuple-element.101, f32[1024,768]{1,0:T(8,128)} %get-tuple-element.102, bf16[8,128,768]{2,1,0:T(8,128)(2,1)S(1)} %copy-done, bf16[8,128,768]{2,1,0:T(8,128)(2,1)} %reduce-scatter.2.cloned.1.call-done, f32[768]{0:T(1024)S(1)} %slice_reduce_fusion.1), kind=kLoop, calls=%fused_computation.3 | loop fusion | flops 9436416 | bytes 12589056 | tf_op jit(solution)/shard_map/add | solution.py:689
  327.3 41.4 %all-reduce.3 = (f32[]{:T(128)}, f32[16,768]{1,0:T(8,128)}, f32[12,768]{1,0:T(8,128)S(1)}) all-reduce(f32[]{:T(128)S(6)} %add.36, f32[16,768]{1,0:T(8,128)S(1)} %scatter.19, f32[12,768]{1,0:T(8,128)S(1)} %slice.184), channel_id=1, replica_groups=mesh['dp'=8,'seq'=4] {'dp','seq'}, use_global_device_ids=true, to_apply=%region_8.9 | all-reduce | flops 21505 | bytes 172040 | tf_op jit(solution)/shard_map/psum | solution.py:693
  368.7 0.7 squeeze.61
  369.4 0.7 squeeze.52
  370.1 0.3 sign_multiply_fusion.1
  370.4 1.4 copy.97
  371.8 1.6 dynamic-slice_bitcast_fusion.1
  373.5 0.8 sign_multiply_fusion.2
  374.3 0.8 sign_multiply_fusion.3
  375.1 0.8 sign_multiply_fusion.4
  375.9 0.8 sign_multiply_fusion.5
  376.7 1.3 sign_multiply_fusion
  (75 shorter events, 1.7 us)
Async XLA Ops:
  7.2 7.0 %copy-start.3 = (f32[768,384]{1,0:T(8,128)S(1)}, f32[768,384]{1,0:T(8,128)}, u32[]{:S(2)}) copy-start(f32[768,384]{1,0:T(8,128)} %param.41) | copy-start | bytes 3538948
  7.2 313.7 %reduce-scatter.2.cloned.1.call-start = ((), (), s32[]{:S(2)}) async-start(), calls=%async_computation.1 | async-start | bytes 7864320 | tf_op jit(solution)/shard_map/reduce_scatter | solution.py:685
  12.1 2.5 copy-start.9
  14.1 1.3 copy-start.6
  14.2 1.4 copy-start.5
  14.2 1.6 copy-start.4
  14.5 7.2 %copy-start.1 = (f32[3072,96]{0,1:T(8,128)S(1)}, f32[3072,96]{0,1:T(8,128)}, u32[]{:S(2)}) copy-start(f32[3072,96]{0,1:T(8,128)} %param.42) | copy-start | bytes 3538948
  15.5 7.5 %copy-start.16 = (bf16[96]{0:T(256)(128)(2,1)S(1)}, bf16[96]{0:T(256)(128)(2,1)}, u32[]{:S(2)}) copy-start(bf16[96]{0:T(256)(128)(2,1)} %param.43) | copy-start | bytes 580
  15.6 7.5 %copy-start.17 = (bf16[96]{0:T(256)(128)(2,1)S(1)}, bf16[96]{0:T(256)(128)(2,1)}, u32[]{:S(2)}) copy-start(bf16[96]{0:T(256)(128)(2,1)} %param.44) | copy-start | bytes 580
  15.6 7.5 %copy-start.18 = (bf16[96]{0:T(256)(128)(2,1)S(1)}, bf16[96]{0:T(256)(128)(2,1)}, u32[]{:S(2)}) copy-start(bf16[96]{0:T(256)(128)(2,1)} %param.45) | copy-start | bytes 580
  15.6 7.5 %copy-start.19 = (bf16[96]{0:T(256)(128)(2,1)S(1)}, bf16[96]{0:T(256)(128)(2,1)}, u32[]{:S(2)}) copy-start(bf16[96]{0:T(256)(128)(2,1)} %param.47) | copy-start | bytes 580
  15.6 7.5 %copy-start.20 = (bf16[96]{0:T(256)(128)(2,1)S(1)}, bf16[96]{0:T(256)(128)(2,1)}, u32[]{:S(2)}) copy-start(bf16[96]{0:T(256)(128)(2,1)} %param.48) | copy-start | bytes 580
  15.6 7.5 %copy-start.21 = (bf16[96]{0:T(256)(128)(2,1)S(1)}, bf16[96]{0:T(256)(128)(2,1)}, u32[]{:S(2)}) copy-start(bf16[96]{0:T(256)(128)(2,1)} %param.49) | copy-start | bytes 580
  15.6 7.5 %copy-start.22 = (bf16[96]{0:T(256)(128)(2,1)S(1)}, bf16[96]{0:T(256)(128)(2,1)}, u32[]{:S(2)}) copy-start(bf16[96]{0:T(256)(128)(2,1)} %param.50) | copy-start | bytes 580
  15.6 7.5 %copy-start.23 = (bf16[96]{0:T(256)(128)(2,1)S(1)}, bf16[96]{0:T(256)(128)(2,1)}, u32[]{:S(2)}) copy-start(bf16[96]{0:T(256)(128)(2,1)} %param.51) | copy-start | bytes 580
  15.6 7.5 %copy-start.24 = (bf16[96]{0:T(256)(128)(2,1)S(1)}, bf16[96]{0:T(256)(128)(2,1)}, u32[]{:S(2)}) copy-start(bf16[96]{0:T(256)(128)(2,1)} %param.52) | copy-start | bytes 580
  15.6 7.5 %copy-start.25 = (bf16[96]{0:T(256)(128)(2,1)S(1)}, bf16[96]{0:T(256)(128)(2,1)}, u32[]{:S(2)}) copy-start(bf16[96]{0:T(256)(128)(2,1)} %param.53) | copy-start | bytes 580
  15.7 7.5 %copy-start.26 = (bf16[96]{0:T(256)(128)(2,1)S(1)}, bf16[96]{0:T(256)(128)(2,1)}, u32[]{:S(2)}) copy-start(bf16[96]{0:T(256)(128)(2,1)} %param.54) | copy-start | bytes 580
  26.8 1.0 copy-start.7
  26.8 1.6 copy-start.11
  26.9 1.8 copy-start.14
  30.0 1.2 copy-start.12
  263.5 0.9 copy-start.13
  263.5 4.0 %copy-start.15 = (f32[8,512]{1,0:T(8,128)S(1)}, f32[8,512]{1,0:T(8,128)}, u32[]{:S(2)}) copy-start(f32[8,512]{1,0:T(8,128)} %get-tuple-element.100) | copy-start | bytes 49156
  263.5 57.4 %copy-start = (bf16[8,128,768]{2,1,0:T(8,128)(2,1)S(1)}, bf16[8,128,768]{2,1,0:T(8,128)(2,1)}, u32[]{:S(2)}) copy-start(bf16[8,128,768]{2,1,0:T(8,128)(2,1)} %hidden.3) | copy-start | bytes 4718596
  370.4 4.7 %copy-start.8 = (f32[768,96]{0,1:T(8,128)S(1)}, f32[768,96]{0,1:T(8,128)}, u32[]{:S(2)}) copy-start(f32[768,96]{0,1:T(8,128)} %param.38) | copy-start | bytes 884740
  370.4 5.5 %copy-start.10 = (f32[768,96]{0,1:T(8,128)S(1)}, f32[768,96]{0,1:T(8,128)}, u32[]{:S(2)}) copy-start(f32[768,96]{0,1:T(8,128)} %param.37) | copy-start | bytes 884740
  371.8 4.9 %copy-start.2 = (f32[3072,96]{0,1:T(8,128)S(1)}, f32[3072,96]{0,1:T(8,128)}, u32[]{:S(2)}) copy-start(f32[3072,96]{0,1:T(8,128)} %param.42) | copy-start | bytes 3538948
Sparse Core Ops, SparseCore 0:
  263.7 57.1 reduce-scatter.1

commit v3 on v2

--- a/solution.py
+++ b/solution.py
@@ -88,12 +88,13 @@
 
 
 def attend_row(
-    scale, small, query_seg, key_seg, teacher, s_query, s_key, s_value, s_context, spread, probs, gaps, distill,
+    scale, small, query_seg, key_seg, teacher, s_query, s_key, s_value, s_context, spread, probs, gaps, distill, bias, counted,
+    first, last,
 ):
     block, width = s_query.shape
-    same = query_seg[:, 0:1] == key_seg[0:1, :]
-    bias = jnp.where(same, 0.0, NEGATIVE)
-    counted = jnp.where(query_seg[:, 1:2] == key_seg[1:2, :], 1.0, 0.0)
+    if first == 0:
+        bias[...] = jnp.where(query_seg[:, 0:1] == key_seg[0:1, :], 0.0, NEGATIVE)
+        counted[...] = jnp.where(query_seg[:, 1:2] == key_seg[1:2, :], 1.0, 0.0)
 
     def pair(index, carry):
         at = pl.ds(pl.multiple_of(index * PAIR, PAIR), PAIR)
@@ -106,10 +107,10 @@
         sums = jnp.zeros((8, scores.shape[1]), F32)
         for head in range(2):
             mine = scores[head * block : (head + 1) * block]
-            gap = (mine - teacher[2 * index + head].astype(F32)) * counted
+            gap = (mine - teacher[2 * index + head].astype(F32)) * counted[...]
             sums = sums + folded(gap * gap)
             gaps[2 * index + head] = (gap * SCORE_WEIGHT).astype(BF16)
-            masked = mine + bias
+            masked = mine + bias[...]
             expo = jnp.exp(masked - jnp.max(masked, axis=-1, keepdims=True))
             inverses.append(1.0 / jnp.sum(expo, axis=-1, keepdims=True))
             expo = expo.astype(BF16)
@@ -122,7 +123,7 @@
         spread[:, at] = inverse
         return carry
 
-    lax.fori_loop(0, width // PAIR, pair, 0)
+    lax.fori_loop(first, last, pair, 0)
 
 
 MESH = pl.DeviceIdType.MESH
@@ -203,22 +204,28 @@
         self.x_copy(u, self.zi).start()
         self.neighbours(lambda to: self.z_copy(u, self.zi, to).start())
 
-    def along_z(self, t):
+    def at_distance(self, k, run):
+        if k == 0:
+            run(self.zi, None)
+        else:
+            pl.when(self.zi >= k)(functools.partial(run, self.zi - k, True))
+            pl.when(self.zi + k < self.lines)(functools.partial(run, self.zi + k, False))
+
+    def along_z(self, t, k):
         u = self.unit(t)
         def run(src, below):
             self.z_copy(u, src, self.zi).wait_recv()
             self.relay(src, below, lambda to: self.z_copy(u, src, to).start())
             self.x_copy(u, src).start()
             self.spread(t, u, src * 2 + self.xi)
-        self.each_row(run)
-
-    def over_x(self, t):
+        self.at_distance(k, run)
+
+    def over_x(self, t, k):
         u = self.unit(t)
         def run(src, below):
             self.x_arrival(u, src).wait_recv()
             self.spread(t, u, src * 2 + 1 - self.xi)
-        run(self.zi, None)
-        self.each_row(run)
+        self.at_distance(k, run)
 
     def spread(self, t, u, dp):
         if t in SHARED:
@@ -265,14 +272,13 @@
     pl.semaphore_signal(barrier, inc=1, device_id=(dp, (1 - seq // 2) * 2 + seq % 2), device_id_type=MESH)
     pl.semaphore_wait(barrier, dp_count + 1)
 
-AHEAD = 3
 NEAR = 3
 
 
 def first_kernel(
     scale, dp_count, own, own_vectors, hidden, own_hidden, query_seg, key_seg, teacher,
     full, table, s_query, s_key, s_value, s_context, spread, probs, gaps, distill,
-    whole, vectors, weights, z_sems, x_sems, y_sems, c_sems, l_sems, h_sems, o_sems, v_sems, w_sems,
+    whole, vectors, weights, z_sems, x_sems, y_sems, c_sems, l_sems, h_sems, o_sems, v_sems, w_sems, bias, counted,
 ):
     step = pl.program_id(0)
     rows, block = hidden.shape[0], hidden.shape[1]
@@ -307,9 +313,23 @@
     def fetch(u):
         return pltpu.make_async_copy(full.at[u], weights.at[u], w_sems.at[u])
 
-    def launch(t):
-        if t < STEPS:
-            s.launch(t)
+    def point(r, j):
+        if j == 0 and r + 3 < rows:
+            hidden_pump(r + 3)
+        for t in range(3, STEPS):
+            at = 4 * r + j - 3 * (t - 3)
+            if at == 0 and t + 2 < STEPS:
+                s.launch(t + 2)
+            if at in (0, 3, 6):
+                s.along_z(t, at // 3 + 1)
+            if at in (1, 4, 7, 10):
+                s.over_x(t, at // 3)
+            if t in SHARED and at == 13:
+                s.over_y(t)
+
+    def points(j):
+        for r in range(rows):
+            pl.when(step == r)(functools.partial(point, r, j))
 
     @pl.when(step == 0)
     def _():
@@ -317,23 +337,26 @@
         greet(dp_count)
         for k in range(1, dp_count):
             vector_copy(k).start()
-        launch(0)
+        for t in range(3):
+            s.launch(t)
         for r in range(NEAR):
             to_chip(r).start()
-        launch(1)
         for u in range(UNITS):
             s.local_copy(u).start()
-        launch(2)
         for r in range(rows):
             to_core(r).start()
             kept(r).start()
         mine = pl.ds(pl.multiple_of(s.dp * s.size, s.size), s.size)
         vectors[mine] = own_vectors[...]
+        for k in range(1, s.lines):
+            for t in range(3):
+                s.along_z(t, k)
+                s.over_x(t, k - 1)
+            hidden_pump(k - 1)
+        s.launch(3)
         for t in range(3):
-            s.along_z(t)
-            launch(t + AHEAD)
-            s.over_x(t)
-            hidden_pump(t)
+            s.over_x(t, s.lines - 1)
+        s.launch(4)
         for k in range(1, dp_count):
             vector_copy(k).wait()
         table[...] = jnp.transpose(vectors[...].astype(F32))[: table.shape[0]]
@@ -343,37 +366,25 @@
         for u in range(3):
             fetch(u).wait()
 
+    points(0)
     for r in range(rows):
         @pl.when(step == r)
         def _(r=r):
-            if r + 3 < rows:
-                hidden_pump(r + 3)
-            if r + 3 < STEPS:
-                s.along_z(r + 3)
-                launch(r + 3 + AHEAD)
             kept(r).wait()
             to_core(r).wait_recv()
             passed_on(r).wait_recv()
 
     project_row(whole.at[step], own_hidden.at[0], weights.at[0], weights.at[1], weights.at[2], table,
                 s_query.at[0], s_key.at[0], s_value.at[0])
-
-    for r in range(rows):
-        @pl.when(step == r)
-        def _(r=r):
-            if r + 3 < STEPS:
-                s.over_x(r + 3)
-
-    attend_row(scale, table, query_seg.at[0], key_seg.at[0], teacher.at[0], s_query.at[0], s_key.at[0], s_value.at[0],
-               s_context.at[0], spread.at[0], probs.at[0], gaps.at[0], distill)
+    count = s_query.shape[2] // PAIR
+    for j in range(3):
+        points(j + 1)
+        attend_row(scale, table, query_seg.at[0], key_seg.at[0], teacher.at[0], s_query.at[0], s_key.at[0], s_value.at[0],
+                   s_context.at[0], spread.at[0], probs.at[0], gaps.at[0], distill, bias, counted,
+                   count * j // 3, count * (j + 1) // 3)
 
     @pl.when(step == rows - 1)
     def _():
-        for t in range(rows + 3, STEPS):
-            s.along_z(t)
-            s.over_x(t)
-        for t in SHARED:
-            s.over_y(t)
         for u in range(3, UNITS):
             s.arrived(u)
         s.finish()
@@ -385,7 +396,7 @@
 
 def plain_kernel(
     scale, whole, own_hidden, weights, table, query_seg, key_seg, teacher,
-    s_query, s_key, s_value, s_context, spread, probs, gaps, distill,
+    s_query, s_key, s_value, s_context, spread, probs, gaps, distill, bias, counted,
 ):
     @pl.when(pl.program_id(0) == 0)
     def _():
@@ -394,7 +405,7 @@
     project_row(whole.at[0], own_hidden.at[0], weights.at[0], weights.at[1], weights.at[2], table,
                 s_query.at[0], s_key.at[0], s_value.at[0])
     attend_row(scale, table, query_seg.at[0], key_seg.at[0], teacher.at[0], s_query.at[0], s_key.at[0], s_value.at[0],
-               s_context.at[0], spread.at[0], probs.at[0], gaps.at[0], distill)
+               s_context.at[0], spread.at[0], probs.at[0], gaps.at[0], distill, bias, counted, 0, s_query.shape[2] // PAIR)
 
 
 def chain(weights, small, hidden, teacher, live, s_context, sums, final_out, grad_first_out,
@@ -531,6 +542,143 @@
     pulled_in[0] = (dot_nn(key_grads[...], weights[1]) + dot_nn(value_grads[...], weights[2])).astype(BF16)
 
 
+def last_kernel(
+    scale, dp_count, weights, table, s_query, s_key, s_value, s_context, spread, probs, gaps, grad_ctx,
+    hidden, grad_first, chain_sums, distill,
+    grad_input, early, late,
+    key_grads, value_grads, query_grads, partial, kept, near, sent, far, sums,
+    mine_a, slices_a, mine_b, slices_b, pieces,
+    near_sems, far_sems, a_sems, b_sems,
+):
+    step = pl.program_id(0)
+    rows = partial.shape[0]
+    block, width = s_query.shape[1], s_query.shape[2]
+    size = width // dp_count
+    dp, seq = lax.axis_index("dp"), lax.axis_index("seq")
+    yi, ci = seq // 2, seq % 2
+    across, beside = (1 - yi) * 2 + ci, yi * 2 + 1 - ci
+    corner = (1 - yi) * 2 + 1 - ci
+    peers = (across, beside, corner)
+
+    def positions(place):
+        return pl.ds(pl.multiple_of(place * block, block), block)
+
+    def near_copy(r, which):
+        place = beside if which == 0 else corner
+        return remote(partial.at[r, positions(place)], near.at[r, which], near_sems.at[0, r, which], near_sems.at[1, r, which],
+                      dp, beside)
+
+    def far_copy(r):
+        return remote(sent.at[r], far.at[r], far_sems.at[0, r], far_sems.at[1, r], dp, across)
+
+    def scatter(mine, slices, sems, k):
+        to = lax.rem(dp + k, dp_count)
+        return remote(mine.at[pl.ds(pl.multiple_of(to * size, size), size)], slices.at[k], sems.at[0, k], sems.at[1, k], to, seq)
+
+    def scatter_done(mine, slices, sems):
+        total = mine[pl.ds(pl.multiple_of(dp * size, size), size)]
+        for k in range(1, dp_count):
+            scatter(mine, slices, sems, k).wait()
+            total = total + slices[k]
+        return total
+
+    def swap(which, pieces, sems, k):
+        return remote(pieces.at[which, 0], pieces.at[which, k], sems.at[0, dp_count + k - 1], sems.at[1, dp_count + k - 1], dp, peers[k - 1])
+
+    def swap_done(which, pieces, sems):
+        total = pieces[which, 0]
+        for k in range(1, 4):
+            swap(which, pieces, sems, k).wait()
+            total = total + pieces[which, k]
+        return total
+
+    @pl.when(step == 0)
+    def _():
+        sums[...] = jnp.zeros_like(sums)
+        barrier = pltpu.get_barrier_semaphore()
+        for k in range(1, dp_count):
+            pl.semaphore_signal(barrier, inc=1, device_id=(lax.rem(dp + k, dp_count), seq), device_id_type=MESH)
+        for peer in peers:
+            pl.semaphore_signal(barrier, inc=1, device_id=(dp, peer), device_id_type=MESH)
+        pl.semaphore_wait(barrier, dp_count + 2)
+        columns_of = [jnp.sum(chain_sums[i], axis=0, keepdims=True) for i in range(LOSS)]
+        objective = 0.5 * jnp.sum(chain_sums[LOSS]) + 0.5 * SCORE_WEIGHT * jnp.sum(distill[...])
+        columns_of.append(jnp.full((1, width), objective, F32))
+        columns_of.append(jnp.zeros((PAIR - len(columns_of), width), F32))
+        mine_a[...] = jnp.transpose(jnp.concatenate(columns_of, axis=0))
+        for k in range(1, dp_count):
+            scatter(mine_a, slices_a, a_sems, k).start()
+
+    @pl.when(step == 2)
+    def _():
+        pieces[0, 0] = scatter_done(mine_a, slices_a, a_sems)
+        for k in range(1, 4):
+            swap(0, pieces, a_sems, k).start()
+
+    @pl.when(step == 4)
+    def _():
+        early[...] = swap_done(0, pieces, a_sems)
+
+    def hand_over(r):
+        near_copy(r, 1).wait_recv()
+        sent[r] = (partial[r, positions(across)].astype(F32) + near[r, 1].astype(F32)).astype(BF16)
+        far_copy(r).start()
+
+    def settle(r):
+        near_copy(r, 0).wait_recv()
+        far_copy(r).wait_recv()
+        grad_low = kept[r] + near[r, 0].astype(F32) + far[r].astype(F32)
+        unused, slope, bound = clip_parts(hidden[0].astype(F32), table[C_IN : C_IN + 1])
+        grad_input[0] = grad_first[...] + grad_low * slope
+        sums[3] += folded(grad_low * bound)
+
+    @pl.when(step < rows)
+    def _():
+        attend_back_row(scale, table, s_query.at[0], s_key.at[0], s_value.at[0],
+                        s_context.at[0], spread.at[0], probs.at[0], gaps.at[0],
+                        grad_ctx, key_grads, value_grads, query_grads)
+
+    @pl.when((step > 0) & (step <= rows))
+    def _():
+        hand_over(step - 1)
+
+    @pl.when(step < rows)
+    def _():
+        back = query_grads[...]
+        raw = table[A_Q : A_Q + 1] * s_query[0] + table[B_Q : B_Q + 1]
+        sums[0] += folded(raw * back)
+        query_grad = back * table[A_K : A_K + 1]
+        sums[1] += folded(query_grad * s_query[0])
+        sums[2] += folded(query_grad)
+        pulled = dot_nn(key_grads[...], weights[1]) + dot_nn(value_grads[...], weights[2])
+        partial[step] = pulled.astype(BF16)
+        near_copy(step, 1).start()
+        near_copy(step, 0).start()
+        kept[step] = partial[step, positions(seq)].astype(F32) + dot_nn(
+            (query_grad * table[A_Q : A_Q + 1]).astype(BF16), weights[0]
+        )
+
+    @pl.when(step > 1)
+    def _():
+        settle(step - 2)
+
+    @pl.when(step == pl.num_programs(0) - 1)
+    def _():
+        columns_of = [jnp.sum(sums[i], axis=0, keepdims=True) for i in range(4)]
+        columns_of.append(jnp.zeros((PAIR - len(columns_of), width), F32))
+        mine_b[...] = jnp.transpose(jnp.concatenate(columns_of, axis=0))
+        for k in range(1, dp_count):
+            scatter(mine_b, slices_b, b_sems, k).start()
+        for r in range(rows):
+            near_copy(r, 0).wait_send()
+            near_copy(r, 1).wait_send()
+            far_copy(r).wait_send()
+        pieces[1, 0] = scatter_done(mine_b, slices_b, b_sems)
+        for k in range(1, 4):
+            swap(1, pieces, b_sems, k).start()
+        late[...] = swap_done(1, pieces, b_sems)
+
+
 def signs_and_scale(latent):
     scale = jnp.mean(jnp.abs(latent), axis=0).astype(BF16)
     return jnp.sign(latent).astype(BF16).T, scale
@@ -628,6 +776,7 @@
                 pltpu.VMEM((rows, seq_len, width), BF16), pltpu.VMEM((width, PAIR), BF16), pltpu.VMEM((3, width, width), BF16),
                 sems((2, UNITS, lines * lines)), sems((2, UNITS, lines)), sems((2, UNITS, dp_count)),
                 sems((2, UNITS, dp_count)), sems((UNITS,)), sems((2, 3, rows)), sems((rows,)), sems((2, dp_count)), sems((3,)),
+                pltpu.VMEM((block, seq_len), F32), pltpu.VMEM((block, seq_len), F32),
             ],
             compiler_params=pltpu.CompilerParams(collective_id=0, has_side_effects=True, vmem_limit_bytes=60 * 2**20),
         )(own, own_vectors, hidden_in, hidden_in, query_seg, key_seg, teacher_scores)
@@ -641,6 +790,7 @@
             in_specs=[row_spec(seq_len, width), row_spec(block, width), three, whole(table)] + masks_specs,
             out_specs=attend_specs,
             out_shape=attend_shapes,
+            scratch_shapes=[pltpu.VMEM((block, seq_len), F32), pltpu.VMEM((block, seq_len), F32)],
             compiler_params=pltpu.CompilerParams(vmem_limit_bytes=60 * 2**20),
         )(hidden_full, hidden_in, full, table, query_seg, key_seg, teacher_scores)
 
@@ -665,35 +815,69 @@
         compiler_params=pltpu.CompilerParams(vmem_limit_bytes=60 * 2**20),
     )(full, table, hidden_in, teacher_hidden, live_column, s_context)
     one_spec = pl.BlockSpec((block, width), lambda i: (i, 0))
-    pulled_in, own_in, more = pl.pallas_call(
-        functools.partial(back_kernel, scale),
-        grid=(rows,),
-        in_specs=[three, whole(table),
-                  row_spec(block, width), row_spec(seq_len, width), row_spec(seq_len, width), row_spec(block, width),
-                  row_spec(block, width), row_spec(heads, block, seq_len), row_spec(heads, block, seq_len), one_spec],
-        out_specs=[row_spec(seq_len, width), one_spec, pl.BlockSpec((3, 8, width), lambda i: (0, 0, 0))],
-        out_shape=[jax.ShapeDtypeStruct((rows, seq_len, width), BF16),
-                   jax.ShapeDtypeStruct((tokens, width), F32),
-                   jax.ShapeDtypeStruct((3, 8, width), F32)],
-        scratch_shapes=[pltpu.VMEM((seq_len, width), BF16), pltpu.VMEM((seq_len, width), BF16),
-                        pltpu.VMEM((block, width), F32)],
-        compiler_params=pltpu.CompilerParams(vmem_limit_bytes=60 * 2**20),
-    )(full, table, s_query, s_key, s_value, s_context, spread, probs, gaps, grad_ctx)
-    sums = sums.at[G_K].set(more[0]).at[G_Q].set(more[1]).at[G_BQ].set(more[2])
-    objective = 0.5 * jnp.sum(sums[LOSS]) + 0.5 * SCORE_WEIGHT * jnp.sum(distill)
-
-    crossed = lax.psum_scatter(pulled_in, "seq", scatter_dimension=1, tiled=True).astype(F32)
-    grad_low = own_in + crossed.reshape(tokens, width)
-    inputs = hidden_in.astype(F32).reshape(tokens, width)
-    unused, in_slope, in_bound = clip_parts(inputs, table[C_IN : C_IN + 1])
-    grad_input = grad_first + grad_low * in_slope
-    sums = jnp.sum(sums, axis=1)
-    wide_sums = sums[16:28]
-    sums = sums[:16].at[G_CIN].set(columns(grad_low * in_bound)[0])
-    sums, wide_sums, objective = lax.psum((sums, wide_sums, objective), ("dp", "seq"))
-    at = lax.axis_index("dp")
-    sums = lax.dynamic_slice_in_dim(sums, at * size, size, 1)
-    wide_sums = lax.dynamic_slice_in_dim(wide_sums, at * size, size, 1).reshape(3, 4 * size)
+    if size % 32 == 0:
+        def now_spec(*shape):
+            return pl.BlockSpec((1,) + shape, lambda i: (jnp.minimum(i, rows - 1),) + (0,) * len(shape))
+
+        def then_spec(*shape):
+            return pl.BlockSpec((1,) + shape, lambda i: (jnp.maximum(i - 2, 0),) + (0,) * len(shape))
+
+        grad_input, early, late = pl.pallas_call(
+            functools.partial(last_kernel, scale, dp_count),
+            grid=(rows + 2,),
+            in_specs=[three, whole(table), now_spec(block, width), now_spec(seq_len, width), now_spec(seq_len, width),
+                      now_spec(block, width), now_spec(block, width), now_spec(heads, block, seq_len),
+                      now_spec(heads, block, seq_len), pl.BlockSpec((block, width), lambda i: (jnp.minimum(i, rows - 1), 0)),
+                      then_spec(block, width), pl.BlockSpec((block, width), lambda i: (jnp.maximum(i - 2, 0), 0)),
+                      whole(sums), whole(distill)],
+            out_specs=[then_spec(block, width)] + [pl.BlockSpec((size, PAIR), lambda i: (0, 0))] * 2,
+            out_shape=[jax.ShapeDtypeStruct((rows, block, width), F32)] + [jax.ShapeDtypeStruct((size, PAIR), F32)] * 2,
+            scratch_shapes=[
+                pltpu.VMEM((seq_len, width), BF16), pltpu.VMEM((seq_len, width), BF16), pltpu.VMEM((block, width), F32),
+                pltpu.VMEM((rows, seq_len, width), BF16), pltpu.VMEM((rows, block, width), F32),
+                pltpu.VMEM((rows, 2, block, width), BF16), pltpu.VMEM((rows, block, width), BF16),
+                pltpu.VMEM((rows, block, width), BF16), pltpu.VMEM((4, 8, width), F32),
+                pltpu.VMEM((width, PAIR), F32), pltpu.VMEM((dp_count, size, PAIR), F32),
+                pltpu.VMEM((width, PAIR), F32), pltpu.VMEM((dp_count, size, PAIR), F32),
+                pltpu.VMEM((2, 4, size, PAIR), F32),
+                sems((2, rows, 2)), sems((2, rows)), sems((2, dp_count + 3)), sems((2, dp_count + 3)),
+            ],
+            compiler_params=pltpu.CompilerParams(collective_id=1, has_side_effects=True, vmem_limit_bytes=60 * 2**20),
+        )(full, table, s_query, s_key, s_value, s_context, spread, probs, gaps, grad_ctx, hidden_in, grad_first, sums, distill)
+        early, late = early.T, late.T
+        objective = early[LOSS, 0]
+        sums = early[:16].at[G_K].set(late[0]).at[G_Q].set(late[1]).at[G_BQ].set(late[2]).at[G_CIN].set(late[3])
+        wide_sums = early[16:28].reshape(3, 4 * size)
+    else:
+        pulled_in, own_in, more = pl.pallas_call(
+            functools.partial(back_kernel, scale),
+            grid=(rows,),
+            in_specs=[three, whole(table),
+                      row_spec(block, width), row_spec(seq_len, width), row_spec(seq_len, width), row_spec(block, width),
+                      row_spec(block, width), row_spec(heads, block, seq_len), row_spec(heads, block, seq_len), one_spec],
+            out_specs=[row_spec(seq_len, width), one_spec, pl.BlockSpec((3, 8, width), lambda i: (0, 0, 0))],
+            out_shape=[jax.ShapeDtypeStruct((rows, seq_len, width), BF16),
+                       jax.ShapeDtypeStruct((tokens, width), F32),
+                       jax.ShapeDtypeStruct((3, 8, width), F32)],
+            scratch_shapes=[pltpu.VMEM((seq_len, width), BF16), pltpu.VMEM((seq_len, width), BF16),
+                            pltpu.VMEM((block, width), F32)],
+            compiler_params=pltpu.CompilerParams(vmem_limit_bytes=60 * 2**20),
+        )(full, table, s_query, s_key, s_value, s_context, spread, probs, gaps, grad_ctx)
+        sums = sums.at[G_K].set(more[0]).at[G_Q].set(more[1]).at[G_BQ].set(more[2])
+        objective = 0.5 * jnp.sum(sums[LOSS]) + 0.5 * SCORE_WEIGHT * jnp.sum(distill)
+
+        crossed = lax.psum_scatter(pulled_in, "seq", scatter_dimension=1, tiled=True).astype(F32)
+        grad_low = own_in + crossed.reshape(tokens, width)
+        inputs = hidden_in.astype(F32).reshape(tokens, width)
+        unused, in_slope, in_bound = clip_parts(inputs, table[C_IN : C_IN + 1])
+        grad_input = grad_first + grad_low * in_slope
+        sums = jnp.sum(sums, axis=1)
+        wide_sums = sums[16:28]
+        sums = sums[:16].at[G_CIN].set(columns(grad_low * in_bound)[0])
+        sums, wide_sums, objective = lax.psum((sums, wide_sums, objective), ("dp", "seq"))
+        at = lax.axis_index("dp")
+        sums = lax.dynamic_slice_in_dim(sums, at * size, size, 1)
+        wide_sums = lax.dynamic_slice_in_dim(wide_sums, at * size, size, 1).reshape(3, 4 * size)
     loss = objective / (lax.axis_size("dp") * rows * seq_len)
     grads = [
         jnp.sign(w) * (s / w.shape[0])

time: 387 us -> 267 us (0.69)
  waiting for transfers between devices: 49.3 us -> 0 us
  blocking collectives: 41.4 us -> 0 us
  between operations: 17.7 us -> 2.68 us
  Pallas kernels: 232 us -> 220 us
  other arithmetic: 26.8 us -> 21.7 us
    reduce_scatter x1 -> x0, waiting for transfers between devices: 49.3 us -> none  [body(): lax.psum_scatter(pulled_in, 'seq', scatter_dimension=1, tiled=True)]
    pallas_call x1, Pallas kernels: 143 us -> 101 us  [body(): pl.pallas_call(functools.partial(first_kernel, scale, dp_count), grid=(ro...]
    psum x1 -> x0, blocking collectives: 41.4 us -> none  [body(): lax.psum((sums, wide_sums, objective), ('dp', 'seq'))]
    pallas_call x1, Pallas kernels: 47.2 us -> 77 us  [body(): pl.pallas_call(functools.partial(last_kernel, scale, dp_count), grid=(row...]
    add x1 -> x0, other arithmetic: 6.28 us -> none  [body(): grad_input = grad_first + grad_low * in_slope]
    unnamed x4, other arithmetic: 0.97 us -> 6.88 us
  transfers between devices with their start and end apart: 1 -> 0, of which waited for: 1 -> 0; matrix products, arithmetic and copies ran while one was open for 2% -> 0% of each run, Pallas kernels for 0% -> 0%
where the time goes in v3:
time: 267 us; the launch traced here: 266 us
  Pallas kernels  220 us (82%)
  other arithmetic  21.7 us (8%)
  local copies, waits for them, and re-layouts  21.1 us (8%)
  between operations  2.68 us (1%)
    pallas_call x1, Pallas kernels, body(): pl.pallas_call(functools.partial(first_kernel, scale, dp_count), grid=(ro...  101 us
    pallas_call x1, Pallas kernels, body(): pl.pallas_call(functools.partial(last_kernel, scale, dp_count), grid=(row...  77 us
    pallas_call x1, Pallas kernels, body(): pl.pallas_call(chain_kernel, grid=(rows // group,), in_specs=[whole(full)...  41.8 us
    unnamed x4, other arithmetic  6.88 us
    unnamed x35, local copies, waits for them, and re-layouts  6.38 us

profile of v3, /device:TPU:0, one launch (start us, length us, event | category | flops | bytes accessed | tf_op | source)
XLA Modules:
  0.0 265.8 jit_solution(6952007050973714821)
XLA Ops:
  0.7 1.8 fusion.1
  2.5 1.7 fusion.3
  4.2 1.7 fusion.5
  5.9 1.7 fusion.7
  7.5 1.0 abs_reduce_fusion.1
  8.5 0.8 convert_element_type.102
  9.3 1.0 copy.116
  10.3 2.5 stack_reshape.7
  12.8 0.4 copy.104
  13.1 0.3 sign_convert_fusion.1
  13.4 0.8 copy-done.11
  14.4 1.1 constant_dynamic-update-slice_fusion.own
  15.5 0.1 abs_reduce_fusion.5
  15.7 0.5 convert_bitcast_fusion.5
  16.2 0.1 abs_reduce_fusion.3
  16.3 0.1 abs_reduce_fusion.4
  16.4 0.5 convert_bitcast_fusion.3
  17.0 0.1 abs_reduce_fusion.2
  17.1 0.5 convert_bitcast_fusion.1
  17.6 0.2 abs_reduce_fusion
  17.9 0.8 reshape.238
  18.6 0.8 reshape.239
  19.4 1.6 concatenate.15
  21.0 0.1 copy.107
  21.2 0.6 pad.12.own_vectors
  21.8 0.7 iota_compare_fusion
  22.5 1.0 copy.108.query_seg
  23.6 0.7 broadcast_select_fusion
  24.3 0.6 pad_add_fusion.key_seg
  25.0 101.5 %shard_map.399 = (bf16[12,768,768]{2,1,0:T(8,128)(2,1)}, f32[32,768]{1,0:T(8,128)}, f32[8,128,768]{2,1,0:T(8,128)}, bf16[8,512,768]{2,1,0:T(8,128)(2,1)}, bf16[8...) custom-call(bf16[12,96,768]{2,1,0:T(8,128)(2,1)} %constant_dynamic-u, ...), custom_call_target="tpu_custom_call" | custom-call | tf_op jit(solution)/shard_map/pallas_call | solution.py:768
  126.5 1.0 copy.109.live
  127.5 41.8 %shard_map.400 = (bf16[1024,768]{1,0:T(8,128)(2,1)}, f32[1024,768]{1,0:T(8,128)}, f32[1024,768]{1,0:T(8,128)}, f32[29,8,768]{2,1,0:T(8,128)}) custom-call(bf16[12,768,768]{2,1,0:T(8,128)(2,1)} %get-tuple-element.87.weights, f32[32,768]{1,0:T(8,128)} %get-tuple-element.88.small.table, bf16[8,128,768]{2,1,0:T(8,128)(2,1)} %hidden.5, ...), custom_call_target="tpu_custom_call" | custom-call | tf_op jit(solution)/shard_map/pallas_call | solution.py:802
  169.4 77.0 %shard_map.401 = (f32[8,128,768]{2,1,0:T(8,128)}, f32[96,128]{1,0:T(8,128)}, f32[96,128]{1,0:T(8,128)}) custom-call(bf16[12,768,768]{2,1,0:T(8,128)(2,1)} %get-tuple-element.87.weights, f32[32,768]{1,0:T(8,128)} %get-tuple-element.88.small.table, f32[8,128,768]{2,1,0:T(8,128)} %get-tuple-element.91.s_query, bf16[8,512,768]{2,1,0:T(8,128)(2,1)} %get-tuple-element.92.s_key, ...), custom_call_target="tpu_custom_call" | custom-call | tf_op jit(solution)/shard_map/pallas_call | solution.py:825
  246.4 1.3 slice.155
  248.4 1.7 slice_reduce_fusion.2
  250.1 0.8 sign_multiply_fusion.5
  250.9 0.8 sign_multiply_fusion.4
  251.7 1.6 fusion.12
  253.3 0.3 scatter.4
  253.6 1.0 slice_reduce_fusion
  254.6 0.8 sign_multiply_fusion.3
  255.4 0.8 sign_multiply_fusion.2
  256.3 0.3 sign_multiply_fusion.1
  256.7 1.4 copy.114
  258.1 1.3 sign_multiply_fusion
  259.5 0.7 squeeze.53
  260.2 0.7 squeeze.62
  260.9 3.8 %copy.123 = f32[8,128,768]{2,1,0:T(8,128)} copy(f32[8,128,768]{2,1,0:T(8,128)} %get-tuple-element.222) | data formatting | bytes 6291456
  (44 shorter events, 0.7 us)
Async XLA Ops:
  0.7 6.9 %copy-start.1 = (f32[3072,96]{0,1:T(8,128)S(1)}, f32[3072,96]{0,1:T(8,128)}, u32[]{:S(2)}) copy-start(f32[3072,96]{0,1:T(8,128)} %param.42) | copy-start | bytes 3538948
  9.3 3.5 %copy-start.2 = (f32[768,384]{1,0:T(8,128)S(1)}, f32[768,384]{1,0:T(8,128)}, u32[]{:S(2)}) copy-start(f32[768,384]{1,0:T(8,128)} %param.41) | copy-start | bytes 3538948
  13.1 1.1 copy-start.11
  14.4 1.2 copy-start.3
  14.4 1.8 copy-start.7
  14.4 1.9 copy-start.5
  14.4 2.5 copy-start.9
  14.4 2.6 copy-start.15
  15.5 7.0 %copy-start.14 = (s32[8,512]{1,0:T(8,128)S(1)}, s32[8,512]{1,0:T(8,128)}, u32[]{:S(2)}) copy-start(s32[8,512]{1,0:T(8,128)} %param.33) | copy-start | bytes 49156
  169.3 80.8 %copy-start.4 = (f32[768,96]{0,1:T(8,128)S(1)}, f32[768,96]{0,1:T(8,128)}, u32[]{:S(2)}) copy-start(f32[768,96]{0,1:T(8,128)} %param.37) | copy-start | bytes 884740
  169.3 81.6 %copy-start.6 = (f32[768,96]{0,1:T(8,128)S(1)}, f32[768,96]{0,1:T(8,128)}, u32[]{:S(2)}) copy-start(f32[768,96]{0,1:T(8,128)} %param.38) | copy-start | bytes 884740
  246.4 6.9 %copy-start = (f32[96,128]{1,0:T(8,128)S(1)}, f32[96,128]{1,0:T(8,128)}, u32[]{:S(2)}) copy-start(f32[96,128]{1,0:T(8,128)} %get-tuple-element.101) | copy-start | bytes 147460
  246.4 8.2 %copy-start.8 = (f32[768,96]{0,1:T(8,128)S(1)}, f32[768,96]{0,1:T(8,128)}, u32[]{:S(2)}) copy-start(f32[768,96]{0,1:T(8,128)} %param.39) | copy-start | bytes 884740
  246.4 9.0 %copy-start.10 = (f32[768,96]{0,1:T(8,128)S(1)}, f32[768,96]{0,1:T(8,128)}, u32[]{:S(2)}) copy-start(f32[768,96]{0,1:T(8,128)} %param.40) | copy-start | bytes 884740
  258.1 1.3 copy-start.13
  258.1 2.1 copy-start.12

commit v4 on v3

--- a/solution.py
+++ b/solution.py
@@ -13,6 +13,8 @@
 F32 = jnp.float32
 BF16 = jnp.bfloat16
 PAIR = 128
+HEAD = 64
+GROUP = 256
 A_Q, A_K, A_V, A_O, A_D, B_Q, B_V, B_O, B_D, G1, S1, G2, S2, C_IN, C_CTX, C_MID = range(16)
 A_U, B_U, C_HID, VECTORS = 16, 20, 24, 32
 G_Q, G_K, G_V, G_O, G_D, G_BQ, G_BV, G_BO, G_BD, G_G1, G_S1, G_G2, G_S2, G_CIN, G_CCTX, G_CMID = range(16)
@@ -58,72 +60,136 @@
     )
 
 
-def halves(value):
+def stacked(value):
     lane = lax.broadcasted_iota(jnp.int32, value.shape, 1)
-    half = value.shape[1] // 2
     zero = jnp.zeros_like(value)
-    return jnp.concatenate(
-        [jnp.where(lane < half, value, zero), jnp.where(lane < half, zero, value)], axis=0
-    )
-
-
-def by_head(first, second):
-    shape = jnp.broadcast_shapes(first.shape, second.shape)
-    lane = lax.broadcasted_iota(jnp.int32, shape[:-1] + (PAIR,), 1)
-    return jnp.where(lane < PAIR // 2, first, second)
+    return jnp.concatenate([jnp.where(lane // HEAD == i, value, zero) for i in range(GROUP // HEAD)], axis=0)
+
+
+def by_head(parts):
+    shape = jnp.broadcast_shapes(parts[0].shape, (1, GROUP))
+    lane = lax.broadcasted_iota(jnp.int32, shape, 1)
+    result = parts[-1]
+    for i in range(len(parts) - 2, -1, -1):
+        result = jnp.where(lane < (i + 1) * HEAD, parts[i], result)
+    return result
 
 
 def folded(value):
     return jnp.sum(value.reshape(value.shape[0] // 8, 8, value.shape[1]), axis=0)
 
 
-def project_row(hidden, own_hidden, sq, sk, sv, small, s_query, s_key, s_value):
+def mask_row(segments, lengths, row, start, bias, counted):
+    block, seq_len = bias.shape
+    keys = segments[pl.ds(row, 1), :].astype(F32)
+    mine = keys[:, :block]
+    for i in range(1, seq_len // block):
+        mine = jnp.where(start == i * block, keys[:, i * block : (i + 1) * block], mine)
+    queries = jnp.transpose(jnp.broadcast_to(mine, (block, block)))
+    same = jnp.concatenate([queries] * (seq_len // block), axis=1) == keys
+    length = lengths[row]
+    query_at = start + lax.broadcasted_iota(jnp.int32, (block, seq_len), 0)
+    key_at = lax.broadcasted_iota(jnp.int32, (block, seq_len), 1)
+    bias[...] = jnp.where(same, 0.0, NEGATIVE)
+    counted[...] = jnp.where(same & (query_at < length) & (key_at < length), 1.0, 0.0)
+
+
+def signed(value):
+    return jnp.where(value > 0, 1.0, jnp.where(value < 0, -1.0, 0.0))
+
+
+def pack(squares, up, down, vectors_in, own, own_vectors, which):
+    size = own.shape[1]
+    width = own.shape[2]
+    lane = lax.broadcasted_iota(jnp.int32, own_vectors.shape, 1)
+
+    def put(unit, turned, kind):
+        own[unit] = signed(turned).astype(BF16)
+        scale = jnp.sum(jnp.abs(turned), axis=1, keepdims=True) / width
+        own_vectors[...] = jnp.where(lane == kind, scale.astype(BF16).astype(F32), own_vectors[...])
+
+    if which == 0:
+        size = own.shape[1]
+        zeros = functools.partial(jnp.zeros, dtype=F32)
+        columns = jnp.transpose(
+            jnp.concatenate([zeros((5, size)), vectors_in[0][...].astype(F32), zeros((PAIR - 16, size))], axis=0)
+        )
+        wide = jnp.transpose(
+            jnp.concatenate([vectors_in[1][...].astype(F32), zeros((PAIR - 2, 4 * size))], axis=0)
+        )
+        for kind in range(2):
+            for i in range(4):
+                columns = jnp.where(lane == B_U + 4 * kind + i, wide[i * size : (i + 1) * size, kind : kind + 1], columns)
+        own_vectors[...] = columns
+        for unit in range(3):
+            put(unit, squares[unit][...], A_Q + unit)
+        return
+    put(3, squares[3][...], A_O)
+    turned = jnp.transpose(up[...])
+    for i in range(4):
+        part = turned[i * size : (i + 1) * size]
+        own[4 + 2 * i] = signed(part).astype(BF16)
+        scale = jnp.sum(jnp.abs(part), axis=1, keepdims=True) / width
+        own_vectors[...] = jnp.where(lane == A_U + i, scale.astype(BF16).astype(F32), own_vectors[...])
+    groups = down.shape[1] // (4 * size)
+    scale = jnp.sum(jnp.abs(down[...]), axis=1, keepdims=True) / down.shape[1]
+    own_vectors[...] = jnp.where(lane == A_D, scale.astype(BF16).astype(F32), own_vectors[...])
+    straight = jnp.transpose(signed(down[...]))
+    for i in range(4):
+        part = jnp.concatenate([straight[(4 * j + i) * size : (4 * j + i + 1) * size] for j in range(groups)], axis=0)
+        own[5 + 2 * i] = jnp.transpose(part).astype(BF16)
+
+
+def project_row(hidden, own_hidden, sq, sk, sv, small, s_query, s_key, s_value, bounds_in, own_bounds):
     c_in = small[C_IN : C_IN + 1]
     inverse_in = 1.0 / c_in
-    low = (c_in * jnp.tanh(hidden[...].astype(F32) * inverse_in)).astype(BF16)
+    ratio = hidden[...].astype(F32) * inverse_in
+    bent = jnp.tanh(ratio)
+    bounds_in[...] = (bent - ratio * (1.0 - bent * bent)).astype(BF16)
+    low = (c_in * bent).astype(BF16)
     s_key[...] = dot_nt(low, sk[...]).astype(BF16)
     s_value[...] = dot_nt(low, sv[...]).astype(BF16)
-    low = (c_in * jnp.tanh(own_hidden[...].astype(F32) * inverse_in)).astype(BF16)
+    ratio = own_hidden[...].astype(F32) * inverse_in
+    bent = jnp.tanh(ratio)
+    own_bounds[...] = (bent - ratio * (1.0 - bent * bent)).astype(BF16)
+    low = (c_in * bent).astype(BF16)
     s_query[...] = dot_nt(low, sq[...])
 
 
 def attend_row(
-    scale, small, query_seg, key_seg, teacher, s_query, s_key, s_value, s_context, spread, probs, gaps, distill, bias, counted,
+    scale, small, teacher, s_query, s_key, s_value, s_context, spread, probs, gaps, distill, bias, counted,
     first, last,
 ):
     block, width = s_query.shape
-    if first == 0:
-        bias[...] = jnp.where(query_seg[:, 0:1] == key_seg[0:1, :], 0.0, NEGATIVE)
-        counted[...] = jnp.where(query_seg[:, 1:2] == key_seg[1:2, :], 1.0, 0.0)
-
-    def pair(index, carry):
-        at = pl.ds(pl.multiple_of(index * PAIR, PAIR), PAIR)
+
+    def some(index, carry):
+        at = pl.ds(pl.multiple_of(index * GROUP, GROUP), GROUP)
         query = (
             (small[A_Q : A_Q + 1, at] * s_query[:, at] + small[B_Q : B_Q + 1, at])
             * (small[A_K : A_K + 1, at] * scale)
         ).astype(BF16)
-        scores = dot_nt(halves(query), s_key[:, at])
+        scores = dot_nt(stacked(query), s_key[:, at])
         expos, inverses = [], []
         sums = jnp.zeros((8, scores.shape[1]), F32)
-        for head in range(2):
+        for head in range(GROUP // HEAD):
             mine = scores[head * block : (head + 1) * block]
-            gap = (mine - teacher[2 * index + head].astype(F32)) * counted[...]
+            gap = (mine - teacher[GROUP // HEAD * index + head].astype(F32)) * counted[...]
             sums = sums + folded(gap * gap)
-            gaps[2 * index + head] = (gap * SCORE_WEIGHT).astype(BF16)
+            gaps[GROUP // HEAD * index + head] = (gap * SCORE_WEIGHT).astype(BF16)
             masked = mine + bias[...]
             expo = jnp.exp(masked - jnp.max(masked, axis=-1, keepdims=True))
             inverses.append(1.0 / jnp.sum(expo, axis=-1, keepdims=True))
             expo = expo.astype(BF16)
-            probs[2 * index + head] = expo
+            probs[GROUP // HEAD * index + head] = expo
             expos.append(expo)
         distill[...] += sums
         both = dot_nn(jnp.concatenate(expos, axis=0), s_value[:, at])
-        inverse = by_head(inverses[0], inverses[1])
-        s_context[:, at] = by_head(both[:block], both[block:]) * inverse
+        inverse = by_head(inverses)
+        s_context[:, at] = by_head([both[h * block : (h + 1) * block] for h in range(GROUP // HEAD)]) * inverse
         spread[:, at] = inverse
         return carry
 
-    lax.fori_loop(first, last, pair, 0)
+    lax.fori_loop(first, last, some, 0)
 
 
 MESH = pl.DeviceIdType.MESH
@@ -276,9 +342,10 @@
 
 
 def first_kernel(
-    scale, dp_count, own, own_vectors, hidden, own_hidden, query_seg, key_seg, teacher,
-    full, table, s_query, s_key, s_value, s_context, spread, probs, gaps, distill,
-    whole, vectors, weights, z_sems, x_sems, y_sems, c_sems, l_sems, h_sems, o_sems, v_sems, w_sems, bias, counted,
+    scale, dp_count, lengths, segments, w_query, w_key, w_value, w_out, w_up, w_down, vectors_in, wide_in,
+    hidden, own_hidden, teacher,
+    full, table, s_query, s_key, s_value, s_context, spread, probs, gaps, bounds_in, own_bounds, distill,
+    own, own_columns, own_vectors, whole, vectors, weights, z_sems, x_sems, y_sems, c_sems, l_sems, h_sems, o_sems, v_sems, w_sems, bias, counted,
 ):
     step = pl.program_id(0)
     rows, block = hidden.shape[0], hidden.shape[1]
@@ -334,13 +401,17 @@
     @pl.when(step == 0)
     def _():
         distill[...] = jnp.zeros_like(distill)
+        latents = (w_query, w_key, w_value, w_out), w_up, w_down
+        pack(*latents, (vectors_in, wide_in), own, own_columns, 0)
         greet(dp_count)
+        for r in range(NEAR):
+            to_chip(r).start()
+        for t in range(3):
+            s.launch(t)
+        pack(*latents, (vectors_in, wide_in), own, own_columns, 1)
+        own_vectors[...] = own_columns[...].astype(BF16)
         for k in range(1, dp_count):
             vector_copy(k).start()
-        for t in range(3):
-            s.launch(t)
-        for r in range(NEAR):
-            to_chip(r).start()
         for u in range(UNITS):
             s.local_copy(u).start()
         for r in range(rows):
@@ -375,11 +446,12 @@
             passed_on(r).wait_recv()
 
     project_row(whole.at[step], own_hidden.at[0], weights.at[0], weights.at[1], weights.at[2], table,
-                s_query.at[0], s_key.at[0], s_value.at[0])
-    count = s_query.shape[2] // PAIR
+                s_query.at[0], s_key.at[0], s_value.at[0], bounds_in.at[0], own_bounds.at[0])
+    mask_row(segments, lengths, step, s.seq * block, bias, counted)
+    count = s_query.shape[2] // GROUP
     for j in range(3):
         points(j + 1)
-        attend_row(scale, table, query_seg.at[0], key_seg.at[0], teacher.at[0], s_query.at[0], s_key.at[0], s_value.at[0],
+        attend_row(scale, table, teacher.at[0], s_query.at[0], s_key.at[0], s_value.at[0],
                    s_context.at[0], spread.at[0], probs.at[0], gaps.at[0], distill, bias, counted,
                    count * j // 3, count * (j + 1) // 3)
 
@@ -395,49 +467,68 @@
 
 
 def plain_kernel(
-    scale, whole, own_hidden, weights, table, query_seg, key_seg, teacher,
-    s_query, s_key, s_value, s_context, spread, probs, gaps, distill, bias, counted,
+    scale, lengths, segments, whole, own_hidden, weights, table, teacher,
+    s_query, s_key, s_value, s_context, spread, probs, gaps, bounds_in, own_bounds, distill, bias, counted,
 ):
     @pl.when(pl.program_id(0) == 0)
     def _():
         distill[...] = jnp.zeros_like(distill)
 
     project_row(whole.at[0], own_hidden.at[0], weights.at[0], weights.at[1], weights.at[2], table,
-                s_query.at[0], s_key.at[0], s_value.at[0])
-    attend_row(scale, table, query_seg.at[0], key_seg.at[0], teacher.at[0], s_query.at[0], s_key.at[0], s_value.at[0],
-               s_context.at[0], spread.at[0], probs.at[0], gaps.at[0], distill, bias, counted, 0, s_query.shape[2] // PAIR)
-
-
-def chain(weights, small, hidden, teacher, live, s_context, sums, final_out, grad_first_out,
+                s_query.at[0], s_key.at[0], s_value.at[0], bounds_in.at[0], own_bounds.at[0])
+    mask_row(segments, lengths, pl.program_id(0), lax.axis_index("seq") * own_hidden.shape[1], bias, counted)
+    attend_row(scale, table, teacher.at[0], s_query.at[0], s_key.at[0], s_value.at[0],
+               s_context.at[0], spread.at[0], probs.at[0], gaps.at[0], distill, bias, counted, 0, s_query.shape[2] // GROUP)
+
+
+def chain(stored, weights, arrivals, small, hidden, teacher, live, s_context, sums, final_out, grad_first_out,
           grad_ctx_out, pres, slopes, bounds):
     def vec(i):
         return small[i : i + 1]
 
+    step = pl.program_id(0)
+
+    def fetch(unit):
+        return pltpu.make_async_copy(stored.at[3 + unit], weights.at[unit], arrivals.at[unit])
+
+    def needed(unit):
+        pass
+
+    @pl.when(step == 0)
+    def _():
+        for unit in range(UNITS - 3):
+            fetch(unit).start()
+        for unit in range(UNITS - 3):
+            fetch(unit).wait()
+
     def add(i, value):
         sums[i] += folded(value)
 
     width = hidden.shape[1]
-    inputs = hidden.astype(F32)
-    context = vec(A_V) * s_context + vec(B_V)
-    context_low, ctx_slope, ctx_bound = clip_parts(context, vec(C_CTX))
-    s_out = dot_nt(context_low.astype(BF16), weights[3])
+    inputs = hidden[...].astype(F32)
+    context = vec(A_V) * s_context[...] + vec(B_V)
+    context_low = clip_parts(context, vec(C_CTX))[0]
+    needed(0)
+    s_out = dot_nt(context_low.astype(BF16), weights[0])
     normed, unit1, inverse1 = norm_parts(inputs + vec(A_O) * s_out + vec(B_O), vec(G1), vec(S1))
     normed_low, mid_slope, mid_bound = clip_parts(normed, vec(C_MID))
     normed_low = normed_low.astype(BF16)
-    s_down = jnp.zeros_like(inputs)
+    s_down = 0.0
     for i in range(4):
-        s_up = dot_nt(normed_low, weights[4 + 2 * i])
+        needed(1 + 2 * i)
+        s_up = dot_nt(normed_low, weights[1 + 2 * i])
         pres[i] = s_up
         pre = vec(A_U + i) * s_up + vec(B_U + i)
         phi = 0.5 + 0.5 * lax.erf(pre * (0.5**0.5))
         act_slope = phi + pre * (jnp.exp(-0.5 * pre * pre) * 0.3989422804014327)
         hidden_low, slope, bound = clip_parts(pre * phi, vec(C_HID + i))
-        slopes[i] = slope * act_slope
+        slopes[i] = (slope * act_slope)
         bounds[i] = bound
-        s_down = s_down + dot_nt(hidden_low.astype(BF16), weights[5 + 2 * i])
+        needed(2 + 2 * i)
+        s_down = s_down + dot_nt(hidden_low.astype(BF16), weights[2 + 2 * i])
     final, unit2, inverse2 = norm_parts(normed + vec(A_D) * s_down + vec(B_D), vec(G2), vec(S2))
     final_out[...] = final.astype(BF16)
-    errors = (final - teacher.astype(F32)) * live
+    errors = jnp.where(live, final - teacher[...].astype(F32), 0.0)
     add(LOSS, errors * errors)
     add(G_G2, errors * unit2)
     add(G_S2, errors)
@@ -445,14 +536,14 @@
     add(G_D, grad_second * s_down)
     add(G_BD, grad_second)
     branch = (grad_second * vec(A_D)).astype(BF16)
-    grad_mid = jnp.zeros_like(inputs)
+    grad_mid = 0.0
     for i in range(4):
-        grad_hid = dot_nn(branch, weights[5 + 2 * i])
+        grad_hid = dot_nn(branch, weights[2 + 2 * i])
         add(G_CHID + i, grad_hid * bounds[i])
         up_grad = grad_hid * slopes[i]
         add(G_BU + i, up_grad)
         add(G_U + i, up_grad * pres[i])
-        grad_mid = grad_mid + dot_nn((up_grad * vec(A_U + i)).astype(BF16), weights[4 + 2 * i])
+        grad_mid = grad_mid + dot_nn((up_grad * vec(A_U + i)).astype(BF16), weights[1 + 2 * i])
     add(G_CMID, grad_mid * mid_bound)
     grad_normed = grad_second + grad_mid * mid_slope
     add(G_G1, grad_normed * unit1)
@@ -461,10 +552,11 @@
     grad_first_out[...] = grad_first
     add(G_O, grad_first * s_out)
     add(G_BO, grad_first)
-    grad_ctx_low = dot_nn((grad_first * vec(A_O)).astype(BF16), weights[3])
+    grad_ctx_low = dot_nn((grad_first * vec(A_O)).astype(BF16), weights[0])
+    unused, ctx_slope, ctx_bound = clip_parts(vec(A_V) * s_context[...] + vec(B_V), vec(C_CTX))
     add(G_CCTX, grad_ctx_low * ctx_bound)
     grad_ctx = grad_ctx_low * ctx_slope
-    add(G_V, grad_ctx * s_context)
+    add(G_V, grad_ctx * s_context[...])
     add(G_BV, grad_ctx)
     grad_ctx_out[...] = grad_ctx
 
@@ -473,47 +565,54 @@
                     grad_ctx, key_grads, value_grads, query_grads):
     block, width = s_query.shape
 
-    def pair(index, carry):
-        at = pl.ds(pl.multiple_of(index * PAIR, PAIR), PAIR)
+    def some(index, carry):
+        at = pl.ds(pl.multiple_of(index * GROUP, GROUP), GROUP)
         raw = small[A_Q : A_Q + 1, at] * s_query[:, at] + small[B_Q : B_Q + 1, at]
-        query = halves((raw * (small[A_K : A_K + 1, at] * scale)).astype(BF16))
+        query = stacked((raw * (small[A_K : A_K + 1, at] * scale)).astype(BF16))
         pulled = grad_ctx[:, at] * small[A_V : A_V + 1, at] * spread[:, at]
         product = pulled * s_context[:, at]
         lane = lax.broadcasted_iota(jnp.int32, product.shape, 1)
-        left = jnp.sum(jnp.where(lane < PAIR // 2, product, 0.0), axis=-1, keepdims=True)
-        right = jnp.sum(jnp.where(lane < PAIR // 2, 0.0, product), axis=-1, keepdims=True)
-        accum_grad = halves(pulled.astype(BF16))
+        deltas = [
+            jnp.sum(jnp.where(lane // HEAD == h, product, 0.0), axis=-1, keepdims=True) for h in range(GROUP // HEAD)
+        ]
+        accum_grad = stacked(pulled.astype(BF16))
         prob_grad = dot_nt(accum_grad, s_value[:, at])
         score_grads, expos = [], []
-        for head, delta in ((0, left), (1, right)):
-            expo = probs[2 * index + head]
+        for head, delta in enumerate(deltas):
+            expo = probs[GROUP // HEAD * index + head]
             expos.append(expo)
             mine = prob_grad[head * block : (head + 1) * block]
             score_grads.append(
-                (expo.astype(F32) * (mine - delta) + gaps[2 * index + head].astype(F32)).astype(BF16)
+                (expo.astype(F32) * (mine - delta) + gaps[GROUP // HEAD * index + head].astype(F32)).astype(BF16)
             )
         score_grad = jnp.concatenate(score_grads, axis=0)
         both = dot_nn(score_grad, s_key[:, at])
-        query_grads[:, at] = by_head(both[:block], both[block:]) * scale
+        query_grads[:, at] = (
+            by_head([both[h * block : (h + 1) * block] for h in range(GROUP // HEAD)]) * scale
+        )
         key_grads[:, at] = dot_tn(score_grad, query).astype(BF16)
         value_grads[:, at] = dot_tn(jnp.concatenate(expos, axis=0), accum_grad).astype(BF16)
         return carry
 
-    lax.fori_loop(0, width // PAIR, pair, 0)
-
-
-def chain_kernel(weights, small, hidden, teacher, live, s_context, final, grad_first, grad_ctx, sums_out,
-                 sums, pres, slopes, bounds):
+    lax.fori_loop(0, width // GROUP, some, 0, unroll=width // GROUP)
+
+
+def chain_kernel(row_count, lengths, stored, small, hidden, teacher, s_context, final, grad_first, grad_ctx, sums_out,
+                 weights, arrivals, sums, pres, slopes, bounds):
     step = pl.program_id(0)
 
     @pl.when(step == 0)
     def _():
         sums[...] = jnp.zeros_like(sums)
 
-    rows, block, width = hidden.shape
-    flat = (rows * block, width)
-    chain(weights, small, hidden[...].reshape(flat), teacher[...].reshape(flat),
-          live[...].reshape(rows * block, 1), s_context[...].reshape(flat), sums, final, grad_first,
+    flat = hidden.shape
+    rows, block = row_count, flat[0] // row_count
+    at = lax.broadcasted_iota(jnp.int32, flat, 0)
+    limit = jnp.full(flat, lengths[step * rows], jnp.int32)
+    for r in range(1, rows):
+        limit = jnp.where(at < r * block, limit, lengths[step * rows + r])
+    live = lax.axis_index("seq") * block + lax.rem(at, block) < limit
+    chain(stored, weights, arrivals, small, hidden, teacher, live, s_context, sums, final, grad_first,
           grad_ctx, pres, slopes, bounds)
 
     @pl.when(step == pl.num_programs(0) - 1)
@@ -544,14 +643,14 @@
 
 def last_kernel(
     scale, dp_count, weights, table, s_query, s_key, s_value, s_context, spread, probs, gaps, grad_ctx,
-    hidden, grad_first, chain_sums, distill,
+    hidden, grad_first, bounds_in, own_bounds, chain_sums, distill,
     grad_input, early, late,
-    key_grads, value_grads, query_grads, partial, kept, near, sent, far, sums,
-    mine_a, slices_a, mine_b, slices_b, pieces,
+    query_grads, partial, kept, near, sent, far, sums,
+    mine_a, slices_a, mine_b, slices_b, pieces, pieces_b,
     near_sems, far_sems, a_sems, b_sems,
 ):
     step = pl.program_id(0)
-    rows = partial.shape[0]
+    rows = partial.shape[1]
     block, width = s_query.shape[1], s_query.shape[2]
     size = width // dp_count
     dp, seq = lax.axis_index("dp"), lax.axis_index("seq")
@@ -563,33 +662,33 @@
     def positions(place):
         return pl.ds(pl.multiple_of(place * block, block), block)
 
-    def near_copy(r, which):
+    def near_copy(r, kind, which):
         place = beside if which == 0 else corner
-        return remote(partial.at[r, positions(place)], near.at[r, which], near_sems.at[0, r, which], near_sems.at[1, r, which],
-                      dp, beside)
+        return remote(partial.at[kind, r, positions(place)], near.at[kind, r, which], near_sems.at[0, kind, r, which],
+                      near_sems.at[1, kind, r, which], dp, beside)
 
     def far_copy(r):
         return remote(sent.at[r], far.at[r], far_sems.at[0, r], far_sems.at[1, r], dp, across)
 
     def scatter(mine, slices, sems, k):
         to = lax.rem(dp + k, dp_count)
-        return remote(mine.at[pl.ds(pl.multiple_of(to * size, size), size)], slices.at[k], sems.at[0, k], sems.at[1, k], to, seq)
+        return remote(mine.at[to], slices.at[k], sems.at[0, k], sems.at[1, k], to, seq)
 
     def scatter_done(mine, slices, sems):
-        total = mine[pl.ds(pl.multiple_of(dp * size, size), size)]
+        total = mine[dp]
         for k in range(1, dp_count):
             scatter(mine, slices, sems, k).wait()
             total = total + slices[k]
         return total
 
-    def swap(which, pieces, sems, k):
-        return remote(pieces.at[which, 0], pieces.at[which, k], sems.at[0, dp_count + k - 1], sems.at[1, dp_count + k - 1], dp, peers[k - 1])
-
-    def swap_done(which, pieces, sems):
-        total = pieces[which, 0]
+    def swap(pieces, sems, k):
+        return remote(pieces.at[0], pieces.at[k], sems.at[0, dp_count + k - 1], sems.at[1, dp_count + k - 1], dp, peers[k - 1])
+
+    def swap_done(pieces, sems):
+        total = pieces[0]
         for k in range(1, 4):
-            swap(which, pieces, sems, k).wait()
-            total = total + pieces[which, k]
+            swap(pieces, sems, k).wait()
+            total = total + pieces[k]
         return total
 
     @pl.when(step == 0)
@@ -605,78 +704,121 @@
         objective = 0.5 * jnp.sum(chain_sums[LOSS]) + 0.5 * SCORE_WEIGHT * jnp.sum(distill[...])
         columns_of.append(jnp.full((1, width), objective, F32))
         columns_of.append(jnp.zeros((PAIR - len(columns_of), width), F32))
-        mine_a[...] = jnp.transpose(jnp.concatenate(columns_of, axis=0))
+        mine_a[...] = jnp.transpose(jnp.concatenate(columns_of, axis=0)).reshape(mine_a.shape)
         for k in range(1, dp_count):
             scatter(mine_a, slices_a, a_sems, k).start()
 
     @pl.when(step == 2)
     def _():
-        pieces[0, 0] = scatter_done(mine_a, slices_a, a_sems)
+        pieces[0] = scatter_done(mine_a, slices_a, a_sems)
         for k in range(1, 4):
-            swap(0, pieces, a_sems, k).start()
+            swap(pieces, a_sems, k).start()
 
     @pl.when(step == 4)
     def _():
-        early[...] = swap_done(0, pieces, a_sems)
+        early[...] = swap_done(pieces, a_sems)
+
+    def joined(kind, r, which, place):
+        near_copy(r, kind, which).wait_recv()
+        return (partial[kind, r, positions(place)].astype(F32) + near[kind, r, which].astype(F32)).astype(BF16)
 
     def hand_over(r):
-        near_copy(r, 1).wait_recv()
-        sent[r] = (partial[r, positions(across)].astype(F32) + near[r, 1].astype(F32)).astype(BF16)
+        low = None
+        for kind in range(2):
+            both = jnp.concatenate([joined(kind, r, 1, across), joined(kind, r, 0, seq)], axis=0)
+            part = dot_nn(both, weights[1 + kind])
+            low = part if low is None else low + part
+        sent[r] = low[:block].astype(BF16)
         far_copy(r).start()
+        kept[r] = kept[r] + low[block:]
+        sums[3] += folded(low[:block] * bounds_in[0, positions(across)].astype(F32))
+        sums[3] += folded(low[block:] * bounds_in[0, positions(seq)].astype(F32))
 
     def settle(r):
-        near_copy(r, 0).wait_recv()
         far_copy(r).wait_recv()
-        grad_low = kept[r] + near[r, 0].astype(F32) + far[r].astype(F32)
+        grad_low = kept[r] + far[r].astype(F32)
         unused, slope, bound = clip_parts(hidden[0].astype(F32), table[C_IN : C_IN + 1])
         grad_input[0] = grad_first[...] + grad_low * slope
-        sums[3] += folded(grad_low * bound)
 
     @pl.when(step < rows)
     def _():
         attend_back_row(scale, table, s_query.at[0], s_key.at[0], s_value.at[0],
                         s_context.at[0], spread.at[0], probs.at[0], gaps.at[0],
-                        grad_ctx, key_grads, value_grads, query_grads)
-
-    @pl.when((step > 0) & (step <= rows))
-    def _():
-        hand_over(step - 1)
-
-    @pl.when(step < rows)
-    def _():
+                        grad_ctx, partial.at[0, step], partial.at[1, step], query_grads)
+        for kind in range(2):
+            near_copy(step, kind, 1).start()
+        for kind in range(2):
+            near_copy(step, kind, 0).start()
         back = query_grads[...]
         raw = table[A_Q : A_Q + 1] * s_query[0] + table[B_Q : B_Q + 1]
         sums[0] += folded(raw * back)
         query_grad = back * table[A_K : A_K + 1]
         sums[1] += folded(query_grad * s_query[0])
         sums[2] += folded(query_grad)
-        pulled = dot_nn(key_grads[...], weights[1]) + dot_nn(value_grads[...], weights[2])
-        partial[step] = pulled.astype(BF16)
-        near_copy(step, 1).start()
-        near_copy(step, 0).start()
-        kept[step] = partial[step, positions(seq)].astype(F32) + dot_nn(
-            (query_grad * table[A_Q : A_Q + 1]).astype(BF16), weights[0]
-        )
-
-    @pl.when(step > 1)
-    def _():
-        settle(step - 2)
-
-    @pl.when(step == pl.num_programs(0) - 1)
+        kept[step] = dot_nn((query_grad * table[A_Q : A_Q + 1]).astype(BF16), weights[0])
+        sums[3] += folded(kept[step] * own_bounds[0].astype(F32))
+
+    @pl.when((step > 0) & (step <= rows))
+    def _():
+        hand_over(step - 1)
+
+    @pl.when(step == rows)
     def _():
         columns_of = [jnp.sum(sums[i], axis=0, keepdims=True) for i in range(4)]
         columns_of.append(jnp.zeros((PAIR - len(columns_of), width), F32))
-        mine_b[...] = jnp.transpose(jnp.concatenate(columns_of, axis=0))
+        turned = jnp.transpose(jnp.concatenate(columns_of, axis=0))
+        for k in range(dp_count):
+            part = jnp.transpose(turned[k * size : (k + 1) * size])[:8]
+            mine_b[k] = jnp.concatenate([part, jnp.zeros((8, PAIR - size), F32)], axis=1)
         for k in range(1, dp_count):
             scatter(mine_b, slices_b, b_sems, k).start()
+
+    @pl.when(step > 1)
+    def _():
+        settle(step - 2)
+
+    @pl.when(step == rows)
+    def _():
+        pieces_b[0] = scatter_done(mine_b, slices_b, b_sems)
+        for k in range(1, 4):
+            swap(pieces_b, b_sems, k).start()
+
+    @pl.when(step == pl.num_programs(0) - 1)
+    def _():
         for r in range(rows):
-            near_copy(r, 0).wait_send()
-            near_copy(r, 1).wait_send()
+            for kind in range(2):
+                near_copy(r, kind, 0).wait_send()
+                near_copy(r, kind, 1).wait_send()
             far_copy(r).wait_send()
-        pieces[1, 0] = scatter_done(mine_b, slices_b, b_sems)
-        for k in range(1, 4):
-            swap(1, pieces, b_sems, k).start()
-        late[...] = swap_done(1, pieces, b_sems)
+        late[...] = swap_done(pieces_b, b_sems)
+
+
+def finish_kernel(early, late, *refs):
+    latents, grads, vectors = refs[:6], refs[6:12], refs[12:]
+    size = early.shape[0]
+    first, second = jnp.transpose(early[...]), late[...]
+    turned = jnp.transpose(jnp.concatenate([second] * (PAIR // 8), axis=0))[:size]
+
+    def row(value, i):
+        return value[i : i + 1, :size]
+
+    sums = [turned[:, 1:2], turned[:, 0:1], early[:, G_V : G_V + 1], early[:, G_O : G_O + 1], None, early[:, G_D : G_D + 1]]
+    lane = lax.broadcasted_iota(jnp.int32, (4 * size, PAIR), 1)
+    wide = jnp.zeros((4 * size, PAIR), F32)
+    for m in range(3):
+        column = jnp.concatenate([early[:, G_U + 4 * m + i : G_U + 4 * m + i + 1] for i in range(4)], axis=0)
+        wide = jnp.where(lane == m, column, wide)
+    wide = jnp.transpose(wide)
+    sums[4] = wide[0:1]
+    for i, (latent, grad, total) in enumerate(zip(latents, grads, sums)):
+        grad[...] = signed(latent[...]) * (total / latent.shape[0 if i == 4 else 1])
+    loss, given = vectors[-1], vectors[:-1]
+    loss[...] = jnp.broadcast_to(row(first, LOSS), loss.shape)
+    parts = [row(second, 2), row(first, G_BV), row(first, G_BO), wide[1:2], row(first, G_BD), row(first, G_G1),
+             row(first, G_S1), row(first, G_G2), row(first, G_S2), row(second, 3), row(first, G_CCTX), row(first, G_CMID),
+             wide[2:3]]
+    for ref, part in zip(given, parts):
+        ref[...] = part
 
 
 def signs_and_scale(latent):
@@ -721,26 +863,9 @@
 
     dp_count = lax.axis_size("dp")
     size = w_query.shape[1]
-    square = [signs_and_scale(w) for w in (w_query, w_key, w_value, w_out)]
-    up_signs, up_scale = signs_and_scale(w_up)
-    down = w_down.reshape(dp_count, 4, size, size)
-    down_signs = jnp.sign(down).astype(BF16).transpose(1, 3, 0, 2).reshape(4, size, width)
-    down_scale = jnp.mean(jnp.abs(w_down), axis=0).astype(BF16)
-    pairs = jnp.stack([up_signs.reshape(4, size, width), down_signs], axis=1).reshape(8, size, width)
-    own = jnp.concatenate([jnp.stack([s for s, _ in square]), pairs])
-    own_vectors = jnp.concatenate(
-        [jnp.stack([*(a for _, a in square), down_scale, b_query, b_value, b_out, b_down, norm1_gain, norm1_bias,
-                    norm2_gain, norm2_bias, clip_in, clip_ctx, clip_mid]),
-         up_scale.reshape(4, size), b_up.reshape(4, size), clip_hid.reshape(4, size)]
-    )
-    own_vectors = jnp.pad(own_vectors.T, ((0, 0), (0, PAIR - own_vectors.shape[0])))
-
-    positions = jnp.arange(seq_len, dtype=jnp.int32)
-    live = positions[None, :] < row_lengths[:, None]
-    key_seg = jnp.stack([segment_ids, jnp.where(live, segment_ids, -1)], axis=1)
-    own_seg = lax.dynamic_slice_in_dim(segment_ids, first, block, 1)
-    query_live = lax.dynamic_slice_in_dim(live, first, block, 1)
-    query_seg = jnp.stack([own_seg, jnp.where(query_live, own_seg, -2)], axis=2)
+    tuned = dp_count == 8 and rows == 8 and size % 32 == 0 and lax.axis_size("seq") == 4
+    given = jnp.stack([b_query, b_value, b_out, b_down, norm1_gain, norm1_bias, norm2_gain, norm2_bias, clip_in, clip_ctx, clip_mid])
+    given_wide = jnp.stack([b_up, clip_hid])
 
     def row_spec(*shape):
         return pl.BlockSpec((1,) + shape, lambda i: (i,) + (0,) * len(shape))
@@ -751,7 +876,7 @@
     three = pl.BlockSpec((3, width, width), lambda i: (0, 0, 0), pipeline_mode=pl.Buffered(1))
     attend_specs = [row_spec(block, width), row_spec(seq_len, width), row_spec(seq_len, width), row_spec(block, width),
                     row_spec(block, width), row_spec(heads, block, seq_len), row_spec(heads, block, seq_len),
-                    pl.BlockSpec((8, seq_len), lambda i: (0, 0))]
+                    row_spec(seq_len, width), row_spec(block, width), pl.BlockSpec((8, seq_len), lambda i: (0, 0))]
     attend_shapes = [jax.ShapeDtypeStruct((rows, block, width), F32),
                      jax.ShapeDtypeStruct((rows, seq_len, width), BF16),
                      jax.ShapeDtypeStruct((rows, seq_len, width), BF16),
@@ -759,69 +884,93 @@
                      jax.ShapeDtypeStruct((rows, block, width), F32),
                      jax.ShapeDtypeStruct((rows, heads, block, seq_len), BF16),
                      jax.ShapeDtypeStruct((rows, heads, block, seq_len), BF16),
+                     jax.ShapeDtypeStruct((rows, seq_len, width), BF16),
+                     jax.ShapeDtypeStruct((rows, block, width), BF16),
                      jax.ShapeDtypeStruct((8, seq_len), F32)]
-    masks_specs = [row_spec(block, 2), row_spec(2, seq_len), row_spec(heads, block, seq_len)]
+    teacher_spec = row_spec(heads, block, seq_len)
+    scalars = pl.BlockSpec(memory_space=pltpu.SMEM)
+    latents = (w_query.T, w_key.T, w_value.T, w_out.T, w_up, w_down.T)
     anywhere = pl.BlockSpec(memory_space=pl.ANY)
     lines = dp_count // 2
     sems = pltpu.SemaphoreType.DMA
-    if size % 32 == 0:
-        full, table, s_query, s_key, s_value, s_context, spread, probs, gaps, distill = pl.pallas_call(
+    if tuned:
+        full, table, s_query, s_key, s_value, s_context, spread, probs, gaps, bounds_in, own_bounds, distill = pl.pallas_call(
             functools.partial(first_kernel, scale, dp_count),
             grid=(rows,),
-            in_specs=[anywhere, whole(own_vectors), anywhere, row_spec(block, width)] + masks_specs,
+            in_specs=[scalars, whole(segment_ids)] + [whole(w) for w in latents] + [whole(given), whole(given_wide), anywhere,
+                      row_spec(block, width), teacher_spec],
             out_specs=[anywhere, pl.BlockSpec((VECTORS, width), lambda i: (0, 0))] + attend_specs,
             out_shape=[jax.ShapeDtypeStruct((UNITS, width, width), BF16), jax.ShapeDtypeStruct((VECTORS, width), F32)]
             + attend_shapes,
             scratch_shapes=[
+                pltpu.VMEM((UNITS, size, width), BF16), pltpu.VMEM((size, PAIR), F32), pltpu.VMEM((size, PAIR), BF16),
                 pltpu.VMEM((rows, seq_len, width), BF16), pltpu.VMEM((width, PAIR), BF16), pltpu.VMEM((3, width, width), BF16),
                 sems((2, UNITS, lines * lines)), sems((2, UNITS, lines)), sems((2, UNITS, dp_count)),
                 sems((2, UNITS, dp_count)), sems((UNITS,)), sems((2, 3, rows)), sems((rows,)), sems((2, dp_count)), sems((3,)),
                 pltpu.VMEM((block, seq_len), F32), pltpu.VMEM((block, seq_len), F32),
             ],
             compiler_params=pltpu.CompilerParams(collective_id=0, has_side_effects=True, vmem_limit_bytes=60 * 2**20),
-        )(own, own_vectors, hidden_in, hidden_in, query_seg, key_seg, teacher_scores)
+        )(row_lengths, segment_ids, *latents, given, given_wide, hidden_in, hidden_in, teacher_scores)
     else:
+        square = [signs_and_scale(w) for w in (w_query, w_key, w_value, w_out)]
+        up_signs, up_scale = signs_and_scale(w_up)
+        down = w_down.reshape(dp_count, 4, size, size)
+        down_signs = jnp.sign(down).astype(BF16).transpose(1, 3, 0, 2).reshape(4, size, width)
+        down_scale = jnp.mean(jnp.abs(w_down), axis=0).astype(BF16)
+        pairs = jnp.stack([up_signs.reshape(4, size, width), down_signs], axis=1).reshape(8, size, width)
+        own = jnp.concatenate([jnp.stack([s for s, _ in square]), pairs])
+        own_vectors = jnp.concatenate(
+            [jnp.stack([*(a for _, a in square), down_scale, b_query, b_value, b_out, b_down, norm1_gain, norm1_bias,
+                        norm2_gain, norm2_bias, clip_in, clip_ctx, clip_mid]),
+             up_scale.reshape(4, size), b_up.reshape(4, size), clip_hid.reshape(4, size)]
+        )
+        own_vectors = jnp.pad(own_vectors.T, ((0, 0), (0, PAIR - own_vectors.shape[0])))
+
         full = lax.all_gather(own, "dp", axis=1, tiled=True)
         table = lax.all_gather(own_vectors, "dp", axis=0, tiled=True).astype(F32).T[:VECTORS]
         hidden_full = lax.all_gather(hidden_in, "seq", axis=1, tiled=True)
-        s_query, s_key, s_value, s_context, spread, probs, gaps, distill = pl.pallas_call(
+        s_query, s_key, s_value, s_context, spread, probs, gaps, bounds_in, own_bounds, distill = pl.pallas_call(
             functools.partial(plain_kernel, scale),
             grid=(rows,),
-            in_specs=[row_spec(seq_len, width), row_spec(block, width), three, whole(table)] + masks_specs,
+            in_specs=[scalars, whole(segment_ids), row_spec(seq_len, width), row_spec(block, width), three, whole(table),
+                      teacher_spec],
             out_specs=attend_specs,
             out_shape=attend_shapes,
             scratch_shapes=[pltpu.VMEM((block, seq_len), F32), pltpu.VMEM((block, seq_len), F32)],
             compiler_params=pltpu.CompilerParams(vmem_limit_bytes=60 * 2**20),
-        )(hidden_full, hidden_in, full, table, query_seg, key_seg, teacher_scores)
+        )(row_lengths, segment_ids, hidden_full, hidden_in, full, table, teacher_scores)
 
     group = 2
     def group_spec(*shape):
         return pl.BlockSpec((group,) + shape, lambda i: (i,) + (0,) * len(shape))
     flat_spec = pl.BlockSpec((group * block, width), lambda i: (i, 0))
-    live_column = query_live.astype(F32)[..., None]
+    def flat_spec(buffers):
+        return pl.BlockSpec((group * block, width), lambda i: (i, 0), pipeline_mode=pl.Buffered(buffers))
+
     final, grad_first, grad_ctx, sums = pl.pallas_call(
-        chain_kernel,
+        functools.partial(chain_kernel, group),
         grid=(rows // group,),
-        in_specs=[whole(full), whole(table),
-                  group_spec(block, width), group_spec(block, width), group_spec(block, 1), group_spec(block, width)],
-        out_specs=[flat_spec, flat_spec, flat_spec,
+        in_specs=[scalars, pl.BlockSpec(memory_space=pl.ANY), whole(table), flat_spec(2), flat_spec(2), flat_spec(2)],
+        out_specs=[flat_spec(2), flat_spec(2), flat_spec(2),
                    pl.BlockSpec((SUMS, 8, width), lambda i: (0, 0, 0))],
         out_shape=[jax.ShapeDtypeStruct((tokens, width), BF16),
                    jax.ShapeDtypeStruct((tokens, width), F32),
                    jax.ShapeDtypeStruct((tokens, width), F32),
                    jax.ShapeDtypeStruct((SUMS, 8, width), F32)],
-        scratch_shapes=[pltpu.VMEM((SUMS, 8, width), F32)]
+        scratch_shapes=[pltpu.VMEM((UNITS - 3, width, width), BF16), pltpu.SemaphoreType.DMA((UNITS - 3,)),
+                        pltpu.VMEM((SUMS, 8, width), F32)]
         + [pltpu.VMEM((4, group * block, width), F32)] * 3,
-        compiler_params=pltpu.CompilerParams(vmem_limit_bytes=60 * 2**20),
-    )(full, table, hidden_in, teacher_hidden, live_column, s_context)
-    one_spec = pl.BlockSpec((block, width), lambda i: (i, 0))
-    if size % 32 == 0:
+        compiler_params=pltpu.CompilerParams(vmem_limit_bytes=63 * 2**20),
+    )(row_lengths, full, table, hidden_in.reshape(tokens, width), teacher_hidden.reshape(tokens, width),
+      s_context.reshape(tokens, width))
+    if tuned:
         def now_spec(*shape):
             return pl.BlockSpec((1,) + shape, lambda i: (jnp.minimum(i, rows - 1),) + (0,) * len(shape))
 
         def then_spec(*shape):
             return pl.BlockSpec((1,) + shape, lambda i: (jnp.maximum(i - 2, 0),) + (0,) * len(shape))
 
+        own_spec = now_spec(block, width)
         grad_input, early, late = pl.pallas_call(
             functools.partial(last_kernel, scale, dp_count),
             grid=(rows + 2,),
@@ -829,26 +978,45 @@
                       now_spec(block, width), now_spec(block, width), now_spec(heads, block, seq_len),
                       now_spec(heads, block, seq_len), pl.BlockSpec((block, width), lambda i: (jnp.minimum(i, rows - 1), 0)),
                       then_spec(block, width), pl.BlockSpec((block, width), lambda i: (jnp.maximum(i - 2, 0), 0)),
-                      whole(sums), whole(distill)],
-            out_specs=[then_spec(block, width)] + [pl.BlockSpec((size, PAIR), lambda i: (0, 0))] * 2,
-            out_shape=[jax.ShapeDtypeStruct((rows, block, width), F32)] + [jax.ShapeDtypeStruct((size, PAIR), F32)] * 2,
+                      pl.BlockSpec((1, seq_len, width), lambda i: (jnp.clip(i - 1, 0, rows - 1), 0, 0)),
+                      own_spec, whole(sums), whole(distill)],
+            out_specs=[then_spec(block, width), pl.BlockSpec((size, PAIR), lambda i: (0, 0)), pl.BlockSpec((8, PAIR), lambda i: (0, 0))],
+            out_shape=[jax.ShapeDtypeStruct((rows, block, width), F32), jax.ShapeDtypeStruct((size, PAIR), F32),
+                       jax.ShapeDtypeStruct((8, PAIR), F32)],
             scratch_shapes=[
-                pltpu.VMEM((seq_len, width), BF16), pltpu.VMEM((seq_len, width), BF16), pltpu.VMEM((block, width), F32),
-                pltpu.VMEM((rows, seq_len, width), BF16), pltpu.VMEM((rows, block, width), F32),
-                pltpu.VMEM((rows, 2, block, width), BF16), pltpu.VMEM((rows, block, width), BF16),
+                pltpu.VMEM((block, width), F32),
+                pltpu.VMEM((2, rows, seq_len, width), BF16), pltpu.VMEM((rows, block, width), F32),
+                pltpu.VMEM((2, rows, 2, block, width), BF16), pltpu.VMEM((rows, block, width), BF16),
                 pltpu.VMEM((rows, block, width), BF16), pltpu.VMEM((4, 8, width), F32),
-                pltpu.VMEM((width, PAIR), F32), pltpu.VMEM((dp_count, size, PAIR), F32),
-                pltpu.VMEM((width, PAIR), F32), pltpu.VMEM((dp_count, size, PAIR), F32),
-                pltpu.VMEM((2, 4, size, PAIR), F32),
-                sems((2, rows, 2)), sems((2, rows)), sems((2, dp_count + 3)), sems((2, dp_count + 3)),
+                pltpu.VMEM((dp_count, size, PAIR), F32), pltpu.VMEM((dp_count, size, PAIR), F32),
+                pltpu.VMEM((dp_count, 8, PAIR), F32), pltpu.VMEM((dp_count, 8, PAIR), F32),
+                pltpu.VMEM((4, size, PAIR), F32), pltpu.VMEM((4, 8, PAIR), F32),
+                sems((2, 2, rows, 2)), sems((2, rows)), sems((2, dp_count + 3)), sems((2, dp_count + 3)),
             ],
             compiler_params=pltpu.CompilerParams(collective_id=1, has_side_effects=True, vmem_limit_bytes=60 * 2**20),
-        )(full, table, s_query, s_key, s_value, s_context, spread, probs, gaps, grad_ctx, hidden_in, grad_first, sums, distill)
-        early, late = early.T, late.T
-        objective = early[LOSS, 0]
-        sums = early[:16].at[G_K].set(late[0]).at[G_Q].set(late[1]).at[G_BQ].set(late[2]).at[G_CIN].set(late[3])
-        wide_sums = early[16:28].reshape(3, 4 * size)
+        )(full, table, s_query, s_key, s_value, s_context, spread, probs, gaps, grad_ctx, hidden_in, grad_first, bounds_in, own_bounds, sums, distill)
+        def one_block(shape):
+            return pl.BlockSpec(shape, lambda: (0,) * len(shape))
+
+        small_shapes = [(1, w.shape[0]) for w in (b_query, b_value, b_out, b_up, b_down, norm1_gain, norm1_bias, norm2_gain,
+                                                  norm2_bias, clip_in, clip_ctx, clip_mid, clip_hid)]
+        results = pl.pallas_call(
+            finish_kernel,
+            in_specs=[one_block(early.shape), one_block(late.shape)] + [one_block(w.shape) for w in latents],
+            out_specs=[one_block(w.shape) for w in latents] + [one_block(shape) for shape in small_shapes] + [one_block((1, size))],
+            out_shape=[jax.ShapeDtypeStruct(w.shape, F32) for w in latents]
+            + [jax.ShapeDtypeStruct(shape, F32) for shape in small_shapes]
+            + [jax.ShapeDtypeStruct((1, size), F32)],
+            compiler_params=pltpu.CompilerParams(vmem_limit_bytes=60 * 2**20),
+        )(early, late, *latents)
+        loss = results[-1][0, 0] / (dp_count * rows * seq_len)
+        return (
+            (final.reshape(rows, block, width), loss, grad_input.reshape(rows, block, width))
+            + tuple(grad if i == 4 else grad.T for i, grad in enumerate(results[:6]))
+            + tuple(part.reshape(-1) for part in results[6:-1])
+        )
     else:
+        one_spec = pl.BlockSpec((block, width), lambda i: (i, 0))
         pulled_in, own_in, more = pl.pallas_call(
             functools.partial(back_kernel, scale),
             grid=(rows,),

time: 267 us -> 216 us (0.81)
  other arithmetic: 21.7 us -> 3.12 us
  local copies, waits for them, and re-layouts: 21.1 us -> 5.68 us
  Pallas kernels: 220 us -> 205 us
    pallas_call x1, Pallas kernels: 77 us -> 57.8 us  [body(): pl.pallas_call(functools.partial(last_kernel, scale, dp_count), grid=(row...]
    unnamed x4 -> x0, other arithmetic: 6.88 us -> none
    mul x6 -> x0, other arithmetic: 4.85 us -> none  [body(): jnp.sign(w) * (s / w.shape[0])]
    pallas_call x1 -> x2, Pallas kernels: 41.8 us -> 46.7 us  [the longest x1 42.2 us: body(): pl.pallas_call(functools.partial(chain_kernel, group), grid=(rows // grou...]
    unnamed x35 -> x3, local copies, waits for them, and re-layouts: 6.38 us -> 1.67 us
    slice x3 -> x0, other arithmetic: 4.28 us -> none  [the longest x1 1.68 us: body(): late[3]]
    concatenate x3 -> x0, local copies, waits for them, and re-layouts: 2.85 us -> none  [the longest x2 1.76 us: body(): jnp.concatenate([jnp.stack([*(a for _, a in square), down_scale, b_query,...]
where the time goes in v4:
time: 216 us
  Pallas kernels  205 us (95%)
  local copies, waits for them, and re-layouts  5.68 us (3%)
  other arithmetic  3.12 us (1%)
  between operations  2.49 us (1%)
    pallas_call x1, Pallas kernels, body(): pl.pallas_call(functools.partial(first_kernel, scale, dp_count), grid=(ro...  100 us
    pallas_call x1, Pallas kernels, body(): pl.pallas_call(functools.partial(last_kernel, scale, dp_count), grid=(row...  57.8 us
    pallas_call x1, Pallas kernels, body(): pl.pallas_call(functools.partial(chain_kernel, group), grid=(rows // grou...  42.2 us
    pallas_call x1, Pallas kernels, body(): pl.pallas_call(finish_kernel, in_specs=[one_block(early.shape), one_block...  4.52 us

profile of v4, /device:TPU:0, one launch (start us, length us, event | category | flops | bytes accessed | tf_op | source)
XLA Modules:
  0.0 215.8 jit_solution(13435856505264424990)
XLA Ops:
  0.7 2.6 %stack.56.vectors_in = bf16[11,96]{1,0:T(8,128)(2,1)} concatenate(bf16[1,96]{1,0:T(2,128)(2,1)} %bitcast.51, bf16[1,96]{1,0:T(2,128)(2,1)} %bitcast.52, bf16[1,96]{1,0:T(2,128)(2,1)} %bitcast.53, bf16[1,96]{1,0:T(2,128)(2,1)} %bitcast.54, bf16[1,96]{1,0:T(2,128)(2,1)} %bitcast.55, bf16[1,96]{1,0:T(2,128)(2,1)} %bitcast.56, bf16[1,96]{1,0:T(2,128)(2,1)} %bitcast.57, ...), dimensions={0} | concatenate | bytes 4224 | tf_op jit(solution)/shard_map/stack | solution.py:867
  3.3 0.7 stack.58
  4.0 0.7 stack.57
  4.7 0.6 pad_maximum_fusion.wide_in
  5.2 100.0 %shard_map.399 = (bf16[12,768,768]{2,1,0:T(8,128)(2,1)}, f32[32,768]{1,0:T(8,128)}, f32[8,128,768]{2,1,0:T(8,128)}, bf16[8,512,768]{2,1,0:T(8,128)(2,1)}, bf16[8...) custom-call(s32[8]{0:T(128)} %lengths.3, ...), custom_call_target="tpu_custom_call" | custom-call | tf_op jit(solution)/shard_map/pallas_call | solution.py:897
  105.3 42.2 %shard_map.400 = (bf16[1024,768]{1,0:T(8,128)(2,1)}, f32[1024,768]{1,0:T(8,128)}, f32[1024,768]{1,0:T(8,128)}, f32[29,8,768]{2,1,0:T(8,128)}) custom-call(s32[8]{0:T(128)} %lengths.3, bf16[12,768,768]{2,1,0:T(8,128)(2,1)} %get-tuple-element.61.stored.weights, f32[32,768]{1,0:T(8,128)} %get-tuple-element.62.small.table, bf16[1024,768]{1,0:T(8,128)(2,1)} %bitcast.38, ...), custom_call_target="tpu_custom_call" | custom-call | tf_op jit(solution)/shard_map/pallas_call | solution.py:950
  147.5 57.8 %shard_map.401 = (f32[8,128,768]{2,1,0:T(8,128)}, f32[96,128]{1,0:T(8,128)}, f32[8,128]{1,0:T(8,128)}) custom-call(bf16[12,768,768]{2,1,0:T(8,128)(2,1)} %get-tuple-element.61.stored.weights, f32[32,768]{1,0:T(8,128)} %get-tuple-element.62.small.table, f32[8,128,768]{2,1,0:T(8,128)} %get-tuple-element.65.s_query, ...), custom_call_target="tpu_custom_call" | custom-call | tf_op jit(solution)/shard_map/pallas_call | solution.py:974
  205.3 0.0 copy-start
  205.3 4.5 %shard_map.402 = (f32[96,768]{1,0:T(8,128)}, f32[96,768]{1,0:T(8,128)}, f32[96,768]{1,0:T(8,128)}, f32[96,768]{1,0:T(8,128)}, f32[768,384]{1,0:T(8,128)}, /*inde...) custom-call(f32[96,128]{1,0:T(8,128)} %get-tuple-element.77.early, ...), custom_call_target="tpu_custom_call" | custom-call | tf_op jit(solution)/shard_map/pallas_call | solution.py:1003
  210.5 1.3 reduce
  211.8 1.3 reduce.1
  213.0 0.0 copy-done
  213.0 1.7 copy.47
Async XLA Ops:
  205.3 7.7 %copy-start = (f32[8,128,768]{2,1,0:T(8,128)S(1)}, f32[8,128,768]{2,1,0:T(8,128)}, u32[]{:S(2)}) copy-start(f32[8,128,768]{2,1,0:T(8,128)} %get-tuple-element.124) | copy-start | bytes 9437188

commit v5 on v4

--- a/solution.py
+++ b/solution.py
@@ -203,9 +203,9 @@
     )
 
 class Streams:
-    def __init__(self, lines, own, full, z_sems, x_sems, y_sems, c_sems, l_sems):
+    def __init__(self, lines, own, full, s_sems, z_sems, x_sems, y_sems, c_sems, l_sems):
         self.lines, self.own, self.full = lines, own, full
-        self.z_sems, self.x_sems, self.y_sems, self.c_sems, self.l_sems = z_sems, x_sems, y_sems, c_sems, l_sems
+        self.s_sems, self.z_sems, self.x_sems, self.y_sems, self.c_sems, self.l_sems = s_sems, z_sems, x_sems, y_sems, c_sems, l_sems
         self.dp, self.seq = lax.axis_index("dp"), lax.axis_index("seq")
         self.zi, self.xi = self.dp // 2, self.dp % 2
         self.yi, self.ci = self.seq // 2, self.seq % 2
@@ -227,24 +227,24 @@
     def z_copy(self, u, src, to):
         place = self.piece(u, src * 2 + self.xi)
         return remote(self.own_piece(u) if src is self.zi else place, place,
-                      self.z_sems.at[0, u, to + self.lines * src], self.z_sems.at[1, u, src], to * 2 + self.xi, self.seq)
+                      self.s_sems.at[0, u], self.z_sems.at[u, src], to * 2 + self.xi, self.seq)
 
     def x_copy(self, u, src):
         place = self.piece(u, src * 2 + self.xi)
-        return remote(self.own_piece(u) if src is self.zi else place, place, self.x_sems.at[0, u, src], self.x_sems.at[1, u, src],
+        return remote(self.own_piece(u) if src is self.zi else place, place, self.s_sems.at[1, u], self.x_sems.at[u, src],
                       self.zi * 2 + 1 - self.xi, self.seq)
 
     def x_arrival(self, u, src):
         place = self.piece(u, src * 2 + 1 - self.xi)
-        return remote(place, place, self.x_sems.at[0, u, src], self.x_sems.at[1, u, src], self.zi * 2 + 1 - self.xi, self.seq)
+        return remote(place, place, self.s_sems.at[1, u], self.x_sems.at[u, src], self.zi * 2 + 1 - self.xi, self.seq)
 
     def y_copy(self, u, dp):
         place = self.piece(u, dp)
-        return remote(place, place, self.y_sems.at[0, u, dp], self.y_sems.at[1, u, dp], self.dp, (1 - self.yi) * 2 + self.ci)
+        return remote(place, place, self.y_sems.at[0, u - SHARED[0]], self.y_sems.at[1, u - SHARED[0]], self.dp, (1 - self.yi) * 2 + self.ci)
 
     def c_copy(self, u, dp):
         place = self.piece(u, dp)
-        return remote(place, place, self.c_sems.at[0, u, dp], self.c_sems.at[1, u, dp], self.dp, self.yi * 2 + 1 - self.ci)
+        return remote(place, place, self.c_sems.at[0, u], self.c_sems.at[1, u], self.dp, self.yi * 2 + 1 - self.ci)
 
     def local_copy(self, u):
         start = pl.multiple_of(self.dp * self.size, self.size)
@@ -305,28 +305,28 @@
 
     def over_y(self, t):
         u = self.unit(t, True)
-        def run(dp):
-            self.y_copy(u, dp).wait_recv()
-            self.c_copy(u, dp).start()
-        self.others(run)
+        self.bulk(u, 2 * self.lines - 1, self.y_sems.at[1, u - SHARED[0]])
+        self.others(lambda dp: self.c_copy(u, dp).start())
 
     def arrived(self, u):
-        self.others(lambda dp: self.c_copy(u, dp).wait_recv())
+        self.bulk(u, 2 * self.lines - 1, self.c_sems.at[1, u])
         self.local_copy(u).wait()
 
+    def bulk(self, u, pieces, sem):
+        part = self.full.at[u, pl.ds(0, pieces * self.half)]
+        pltpu.make_async_copy(part, part, sem).wait()
+
     def finish(self):
+        inner = (self.zi > 0) & (self.zi < self.lines - 1)
         for t in range(STEPS):
             u = self.unit(t)
-            self.x_copy(u, self.zi).wait_send()
-            self.neighbours(lambda to: self.z_copy(u, self.zi, to).wait_send())
-            def run(src, below):
-                self.relay(src, below, lambda to: self.z_copy(u, src, to).wait_send())
-                self.x_copy(u, src).wait_send()
-            self.each_row(run)
+            pl.when(inner)(functools.partial(self.bulk, u, self.lines + 1, self.s_sems.at[0, u]))
+            pl.when(jnp.logical_not(inner))(functools.partial(self.bulk, u, 1, self.s_sems.at[0, u]))
+            self.bulk(u, self.lines, self.s_sems.at[1, u])
             if t in SHARED:
-                self.others(lambda dp: self.y_copy(u, dp).wait_send())
+                self.bulk(u, 2 * self.lines - 1, self.y_sems.at[0, u - SHARED[0]])
         for u in range(UNITS):
-            self.others(lambda dp: self.c_copy(u, dp).wait_send())
+            self.bulk(u, 2 * self.lines - 1, self.c_sems.at[0, u])
 
 
 def greet(dp_count):
@@ -345,11 +345,11 @@
     scale, dp_count, lengths, segments, w_query, w_key, w_value, w_out, w_up, w_down, vectors_in, wide_in,
     hidden, own_hidden, teacher,
     full, table, s_query, s_key, s_value, s_context, spread, probs, gaps, bounds_in, own_bounds, distill,
-    own, own_columns, own_vectors, whole, vectors, weights, z_sems, x_sems, y_sems, c_sems, l_sems, h_sems, o_sems, v_sems, w_sems, bias, counted,
+    own, own_columns, own_vectors, whole, vectors, weights, s_sems, z_sems, x_sems, y_sems, c_sems, l_sems, h_sems, o_sems, v_sems, w_sems, bias, counted,
 ):
     step = pl.program_id(0)
     rows, block = hidden.shape[0], hidden.shape[1]
-    s = Streams(dp_count // 2, own, full, z_sems, x_sems, y_sems, c_sems, l_sems)
+    s = Streams(dp_count // 2, own, full, s_sems, z_sems, x_sems, y_sems, c_sems, l_sems)
     across, beside = (1 - s.yi) * 2 + s.ci, s.yi * 2 + 1 - s.ci
 
     def place(r, seq):
@@ -773,9 +773,9 @@
         for k in range(1, dp_count):
             scatter(mine_b, slices_b, b_sems, k).start()
 
-    @pl.when(step > 1)
-    def _():
-        settle(step - 2)
+    @pl.when(step > 2)
+    def _():
+        settle(step - 3)
 
     @pl.when(step == rows)
     def _():
@@ -818,7 +818,7 @@
              row(first, G_S1), row(first, G_G2), row(first, G_S2), row(second, 3), row(first, G_CCTX), row(first, G_CMID),
              wide[2:3]]
     for ref, part in zip(given, parts):
-        ref[...] = part
+        ref[...] = part[0]
 
 
 def signs_and_scale(latent):
@@ -905,8 +905,8 @@
             scratch_shapes=[
                 pltpu.VMEM((UNITS, size, width), BF16), pltpu.VMEM((size, PAIR), F32), pltpu.VMEM((size, PAIR), BF16),
                 pltpu.VMEM((rows, seq_len, width), BF16), pltpu.VMEM((width, PAIR), BF16), pltpu.VMEM((3, width, width), BF16),
-                sems((2, UNITS, lines * lines)), sems((2, UNITS, lines)), sems((2, UNITS, dp_count)),
-                sems((2, UNITS, dp_count)), sems((UNITS,)), sems((2, 3, rows)), sems((rows,)), sems((2, dp_count)), sems((3,)),
+                sems((2, UNITS)), sems((UNITS, lines)), sems((UNITS, lines)), sems((2, 2 * len(SHARED))),
+                sems((2, UNITS)), sems((UNITS,)), sems((2, 3, rows)), sems((rows,)), sems((2, dp_count)), sems((3,)),
                 pltpu.VMEM((block, seq_len), F32), pltpu.VMEM((block, seq_len), F32),
             ],
             compiler_params=pltpu.CompilerParams(collective_id=0, has_side_effects=True, vmem_limit_bytes=60 * 2**20),
@@ -968,16 +968,16 @@
             return pl.BlockSpec((1,) + shape, lambda i: (jnp.minimum(i, rows - 1),) + (0,) * len(shape))
 
         def then_spec(*shape):
-            return pl.BlockSpec((1,) + shape, lambda i: (jnp.maximum(i - 2, 0),) + (0,) * len(shape))
+            return pl.BlockSpec((1,) + shape, lambda i: (jnp.maximum(i - 3, 0),) + (0,) * len(shape))
 
         own_spec = now_spec(block, width)
         grad_input, early, late = pl.pallas_call(
             functools.partial(last_kernel, scale, dp_count),
-            grid=(rows + 2,),
+            grid=(rows + 3,),
             in_specs=[three, whole(table), now_spec(block, width), now_spec(seq_len, width), now_spec(seq_len, width),
                       now_spec(block, width), now_spec(block, width), now_spec(heads, block, seq_len),
                       now_spec(heads, block, seq_len), pl.BlockSpec((block, width), lambda i: (jnp.minimum(i, rows - 1), 0)),
-                      then_spec(block, width), pl.BlockSpec((block, width), lambda i: (jnp.maximum(i - 2, 0), 0)),
+                      then_spec(block, width), pl.BlockSpec((block, width), lambda i: (jnp.maximum(i - 3, 0), 0)),
                       pl.BlockSpec((1, seq_len, width), lambda i: (jnp.clip(i - 1, 0, rows - 1), 0, 0)),
                       own_spec, whole(sums), whole(distill)],
             out_specs=[then_spec(block, width), pl.BlockSpec((size, PAIR), lambda i: (0, 0)), pl.BlockSpec((8, PAIR), lambda i: (0, 0))],
@@ -998,7 +998,7 @@
         def one_block(shape):
             return pl.BlockSpec(shape, lambda: (0,) * len(shape))
 
-        small_shapes = [(1, w.shape[0]) for w in (b_query, b_value, b_out, b_up, b_down, norm1_gain, norm1_bias, norm2_gain,
+        small_shapes = [w.shape for w in (b_query, b_value, b_out, b_up, b_down, norm1_gain, norm1_bias, norm2_gain,
                                                   norm2_bias, clip_in, clip_ctx, clip_mid, clip_hid)]
         results = pl.pallas_call(
             finish_kernel,
@@ -1013,7 +1013,7 @@
         return (
             (final.reshape(rows, block, width), loss, grad_input.reshape(rows, block, width))
             + tuple(grad if i == 4 else grad.T for i, grad in enumerate(results[:6]))
-            + tuple(part.reshape(-1) for part in results[6:-1])
+            + tuple(results[6:-1])
         )
     else:
         one_spec = pl.BlockSpec((block, width), lambda i: (i, 0))

time: 216 us -> 203 us (0.940)
  Pallas kernels: 205 us -> 194 us
  other arithmetic: 3.12 us -> 0.57 us
    pallas_call x1, Pallas kernels: 100 us -> 93.2 us  [body(): pl.pallas_call(functools.partial(first_kernel, scale, dp_count), grid=(ro...]
    pallas_call x1, Pallas kernels: 57.8 us -> 53.8 us  [body(): pl.pallas_call(functools.partial(last_kernel, scale, dp_count), grid=(row...]
    pallas_call x2 -> x0, other arithmetic: 2.55 us -> none  [body(): pl.pallas_call(finish_kernel, in_specs=[one_block(early.shape), one_block...]
where the time goes in v5:
time: 203 us; the launch traced here: 202 us
  Pallas kernels  194 us (96%)
  local copies, waits for them, and re-layouts  5.68 us (3%)
  between operations  2.49 us (1%)
    pallas_call x1, Pallas kernels, body(): pl.pallas_call(functools.partial(first_kernel, scale, dp_count), grid=(ro...  93.2 us
    pallas_call x1, Pallas kernels, body(): pl.pallas_call(functools.partial(last_kernel, scale, dp_count), grid=(row...  53.8 us
    pallas_call x1, Pallas kernels, body(): pl.pallas_call(functools.partial(chain_kernel, group), grid=(rows // grou...  42.2 us
    pallas_call x1, Pallas kernels, body(): pl.pallas_call(finish_kernel, in_specs=[one_block(early.shape), one_block...  4.52 us

profile of v5, /device:TPU:0, one launch (start us, length us, event | category | flops | bytes accessed | tf_op | source)
XLA Modules:
  0.0 202.5 jit_solution(2226984321390632825)
XLA Ops:
  0.7 2.6 %stack.56.vectors_in = bf16[11,96]{1,0:T(8,128)(2,1)} concatenate(bf16[1,96]{1,0:T(2,128)(2,1)} %bitcast.40, bf16[1,96]{1,0:T(2,128)(2,1)} %bitcast.41, bf16[1,96]{1,0:T(2,128)(2,1)} %bitcast.42, bf16[1,96]{1,0:T(2,128)(2,1)} %bitcast.43, bf16[1,96]{1,0:T(2,128)(2,1)} %bitcast.44, bf16[1,96]{1,0:T(2,128)(2,1)} %bitcast.45, bf16[1,96]{1,0:T(2,128)(2,1)} %bitcast.46, ...), dimensions={0} | concatenate | bytes 4224 | tf_op jit(solution)/shard_map/stack | solution.py:867
  3.3 0.7 stack.58
  4.0 0.7 stack.57
  4.7 0.6 pad_maximum_fusion.wide_in
  5.2 93.2 %shard_map.399 = (bf16[12,768,768]{2,1,0:T(8,128)(2,1)}, f32[32,768]{1,0:T(8,128)}, f32[8,128,768]{2,1,0:T(8,128)}, bf16[8,512,768]{2,1,0:T(8,128)(2,1)}, bf16[8...) custom-call(s32[8]{0:T(128)} %lengths.3, ...), custom_call_target="tpu_custom_call" | custom-call | tf_op jit(solution)/shard_map/pallas_call | solution.py:897
  98.5 42.2 %shard_map.400 = (bf16[1024,768]{1,0:T(8,128)(2,1)}, f32[1024,768]{1,0:T(8,128)}, f32[1024,768]{1,0:T(8,128)}, f32[29,8,768]{2,1,0:T(8,128)}) custom-call(s32[8]{0:T(128)} %lengths.3, bf16[12,768,768]{2,1,0:T(8,128)(2,1)} %get-tuple-element.61.stored.weights, f32[32,768]{1,0:T(8,128)} %get-tuple-element.62.small.table, bf16[1024,768]{1,0:T(8,128)(2,1)} %bitcast.27, ...), custom_call_target="tpu_custom_call" | custom-call | tf_op jit(solution)/shard_map/pallas_call | solution.py:950
  140.6 53.8 %shard_map.401 = (f32[8,128,768]{2,1,0:T(8,128)}, f32[96,128]{1,0:T(8,128)}, f32[8,128]{1,0:T(8,128)}) custom-call(bf16[12,768,768]{2,1,0:T(8,128)(2,1)} %get-tuple-element.61.stored.weights, f32[32,768]{1,0:T(8,128)} %get-tuple-element.62.small.table, f32[8,128,768]{2,1,0:T(8,128)} %get-tuple-element.65.s_query, ...), custom_call_target="tpu_custom_call" | custom-call | tf_op jit(solution)/shard_map/pallas_call | solution.py:974
  194.5 0.0 copy-start
  194.5 4.5 %shard_map.402 = (f32[96,768]{1,0:T(8,128)}, f32[96,768]{1,0:T(8,128)}, f32[96,768]{1,0:T(8,128)}, f32[96,768]{1,0:T(8,128)}, f32[768,384]{1,0:T(8,128)}, /*inde...) custom-call(f32[96,128]{1,0:T(8,128)} %get-tuple-element.77.early, ...), custom_call_target="tpu_custom_call" | custom-call | tf_op jit(solution)/shard_map/pallas_call | solution.py:1003
  199.7 0.0 copy-done
  199.7 1.7 copy.47
Async XLA Ops:
  194.5 5.2 %copy-start = (f32[8,128,768]{2,1,0:T(8,128)S(1)}, f32[8,128,768]{2,1,0:T(8,128)}, u32[]{:S(2)}) copy-start(f32[8,128,768]{2,1,0:T(8,128)} %get-tuple-element.124) | copy-start | bytes 9437188

commit v6 on v5

--- a/solution.py
+++ b/solution.py
@@ -389,9 +389,9 @@
                 s.launch(t + 2)
             if at in (0, 3, 6):
                 s.along_z(t, at // 3 + 1)
-            if at in (1, 4, 7, 10):
+            if at in (2, 5, 8, 11):
                 s.over_x(t, at // 3)
-            if t in SHARED and at == 13:
+            if t in SHARED and at == 16:
                 s.over_y(t)
 
     def points(j):

time: 203 us -> 202 us (level)
  no operation moved by 1% of the time
where the time goes in v6:
time: 202 us
  Pallas kernels  193 us (96%)
  local copies, waits for them, and re-layouts  5.68 us (3%)
  between operations  2.49 us (1%)
    pallas_call x1, Pallas kernels, body(): pl.pallas_call(functools.partial(first_kernel, scale, dp_count), grid=(ro...  92.2 us
    pallas_call x1, Pallas kernels, body(): pl.pallas_call(functools.partial(last_kernel, scale, dp_count), grid=(row...  54.4 us
    pallas_call x1, Pallas kernels, body(): pl.pallas_call(functools.partial(chain_kernel, group), grid=(rows // grou...  42.1 us
    pallas_call x1, Pallas kernels, body(): pl.pallas_call(finish_kernel, in_specs=[one_block(early.shape), one_block...  4.52 us

profile of v6, /device:TPU:0, one launch (start us, length us, event | category | flops | bytes accessed | tf_op | source)
XLA Modules:
  0.0 202.0 jit_solution(17131267495287034644)
XLA Ops:
  0.7 2.6 %stack.56.vectors_in = bf16[11,96]{1,0:T(8,128)(2,1)} concatenate(bf16[1,96]{1,0:T(2,128)(2,1)} %bitcast.40, bf16[1,96]{1,0:T(2,128)(2,1)} %bitcast.41, bf16[1,96]{1,0:T(2,128)(2,1)} %bitcast.42, bf16[1,96]{1,0:T(2,128)(2,1)} %bitcast.43, bf16[1,96]{1,0:T(2,128)(2,1)} %bitcast.44, bf16[1,96]{1,0:T(2,128)(2,1)} %bitcast.45, bf16[1,96]{1,0:T(2,128)(2,1)} %bitcast.46, ...), dimensions={0} | concatenate | bytes 4224 | tf_op jit(solution)/shard_map/stack | solution.py:867
  3.3 0.7 stack.58
  4.0 0.7 stack.57
  4.7 0.6 pad_maximum_fusion.wide_in
  5.2 92.2 %shard_map.399 = (bf16[12,768,768]{2,1,0:T(8,128)(2,1)}, f32[32,768]{1,0:T(8,128)}, f32[8,128,768]{2,1,0:T(8,128)}, bf16[8,512,768]{2,1,0:T(8,128)(2,1)}, bf16[8...) custom-call(s32[8]{0:T(128)} %lengths.3, ...), custom_call_target="tpu_custom_call" | custom-call | tf_op jit(solution)/shard_map/pallas_call | solution.py:897
  97.5 42.1 %shard_map.400 = (bf16[1024,768]{1,0:T(8,128)(2,1)}, f32[1024,768]{1,0:T(8,128)}, f32[1024,768]{1,0:T(8,128)}, f32[29,8,768]{2,1,0:T(8,128)}) custom-call(s32[8]{0:T(128)} %lengths.3, bf16[12,768,768]{2,1,0:T(8,128)(2,1)} %get-tuple-element.61.stored.weights, f32[32,768]{1,0:T(8,128)} %get-tuple-element.62.small.table, bf16[1024,768]{1,0:T(8,128)(2,1)} %bitcast.27, ...), custom_call_target="tpu_custom_call" | custom-call | tf_op jit(solution)/shard_map/pallas_call | solution.py:950
  139.6 54.4 %shard_map.401 = (f32[8,128,768]{2,1,0:T(8,128)}, f32[96,128]{1,0:T(8,128)}, f32[8,128]{1,0:T(8,128)}) custom-call(bf16[12,768,768]{2,1,0:T(8,128)(2,1)} %get-tuple-element.61.stored.weights, f32[32,768]{1,0:T(8,128)} %get-tuple-element.62.small.table, f32[8,128,768]{2,1,0:T(8,128)} %get-tuple-element.65.s_query, ...), custom_call_target="tpu_custom_call" | custom-call | tf_op jit(solution)/shard_map/pallas_call | solution.py:974
  194.0 0.0 copy-start
  194.0 4.5 %shard_map.402 = (f32[96,768]{1,0:T(8,128)}, f32[96,768]{1,0:T(8,128)}, f32[96,768]{1,0:T(8,128)}, f32[96,768]{1,0:T(8,128)}, f32[768,384]{1,0:T(8,128)}, /*inde...) custom-call(f32[96,128]{1,0:T(8,128)} %get-tuple-element.77.early, ...), custom_call_target="tpu_custom_call" | custom-call | tf_op jit(solution)/shard_map/pallas_call | solution.py:1003
  199.2 0.0 copy-done
  199.2 1.7 copy.47
Async XLA Ops:
  194.0 5.2 %copy-start = (f32[8,128,768]{2,1,0:T(8,128)S(1)}, f32[8,128,768]{2,1,0:T(8,128)}, u32[]{:S(2)}) copy-start(f32[8,128,768]{2,1,0:T(8,128)} %get-tuple-element.124) | copy-start | bytes 9437188
